TPU v7x, 256 devices: a whole 4x4x8 slice. The times are simulated.
256 devices in a mesh: pole: 8 (over z), row: 4 (over x), col: 8 (over y, core).
Axes of the slice: x: 4, y: 4, z: 8, core: 2. Of those that a mesh axis runs over, the one named last changes fastest.
Arguments:
- green_blocks: bfloat16 [32, 8, 192, 6144], P('pole', 'col', None, 'row'), parts along dimension 0, may hold values from -0.078125 to 0.078125
- lower_panel: bfloat16 [6144, 256, 128], P(('row', 'col'), 'pole'), parts along dimension 1, may hold values from -1.5 to 1.5
- pattern: int32 [48, 32], replicated, may hold values 0 or 1
- pivot_inverse: float32 [32, 1024, 128], P(('row', 'col'), 'pole'), parts along dimension 1, may hold values from -6 to 6
Outputs:
- green_panel: bfloat16 [49152, 32, 128], P('pole', ('row', 'col')), parts along dimension 0
- green_diag: float32 [32, 1024, 128], P(('row', 'col'), 'pole'), parts along dimension 1
There are 8 independent parts, one for each index of `pole`. A program takes and returns all parts, laid end to end along the dimension named above; an argument that names none is the same for every part. Nothing has to cross between parts.
All inputs are finite; a program needn't handle non-finite values.
Results may differ from a plain program's by a relative error of at most 0.01.
Values may be sent and summed in bfloat16 or wider, within the bound.
No kernel may reach another device: no remote copies, remote signals or barrier semaphores. Data moves between devices by JAX's collectives and lax.ppermute only.
A program may use at most 128 MiB of HBM per device.

v0:
```python
import functools

import jax
import jax.numpy as jnp
from jax import lax
from jax.experimental import pallas as pl
from jax.experimental.pallas import tpu as pltpu
from jax.sharding import PartitionSpec as P

BF16 = jnp.bfloat16
F32 = jnp.float32
SMEM = pl.BlockSpec(memory_space=pltpu.SMEM)
VMEM = pl.BlockSpec(memory_space=pltpu.VMEM)
ANY = pl.BlockSpec(memory_space=pl.ANY)

W = 128
RD = 192
CH = 2 * RD
NR = 4
NY = 4
NC = 8
SPAN = NC * RD
HALF = NR * RD
ORDER = NR * NC * RD


def run_copies(copies):
    for copy in copies:
        copy.start()
    for copy in copies:
        copy.wait()


def call(
    kernel, outs, ins, specs, out_specs, scratch=(), flops=0, bytes_accessed=4 * 2**20, aliases=()
):
    return pl.pallas_call(
        kernel,
        out_shape=[jax.ShapeDtypeStruct(s, d) for s, d in outs],
        in_specs=specs,
        out_specs=out_specs,
        scratch_shapes=list(scratch),
        input_output_aliases=dict(aliases),
        compiler_params=pltpu.CompilerParams(vmem_limit_bytes=24 * 1024 * 1024),
        cost_estimate=pl.CostEstimate(
            flops=flops, bytes_accessed=bytes_accessed, transcendentals=0
        ),
    )(*ins)


def step_of(r, group, core):
    return lax.rem(r + 3 - group, 4) if core == 0 else lax.rem(group + 3 - r, 4)


def along(index, count, core):
    return lax.rem(index + jnp.where(core == 0, count, 4 - count), 4)


def prep_kernel(place, pattern, panel, mine0, theirs0, mine, theirs, turned, sems):
    r, k, position = place[0], place[2], place[3]
    for group in range(NR):
        for part in range(3):
            block = lax.div(position * 3 + part, 2)
            for piece in range(2):
                rows = pl.ds(part * 64 + piece * 32, 32)
                value = jnp.swapaxes(
                    panel[rows, group * 8 : group * 8 + 8, :].astype(F32), 0, 1
                )
                for q in range(NY):
                    for parity in range(2):
                        keep = pattern[group * 8 + q * 2 + parity, block].astype(F32)
                        turned[lax.rem(parity + k, 2), step_of(r, group, parity), q, rows, :] = (
                            value[q * 2 + parity] * keep
                        ).astype(BF16)
    run_copies(
        [
            pltpu.make_async_copy(turned.at[who, part], out, sems.at[i])
            for i, (who, part, out) in enumerate(
                (
                    (1, 0, theirs0),
                    (0, 0, mine0),
                    (1, slice(1, 4), theirs),
                    (0, slice(1, 4), mine),
                )
            )
        ]
    )


def first_chunk_kernel(place, mine, got, after, first, second, sems):
    k = place[2]
    copies = []
    for i, part in enumerate((first, second)):
        for source, half in ((mine, k), (got, 1 - k)):
            copies.append(
                pltpu.make_async_copy(
                    source.at[2 * i : 2 * i + 2], part.at[:, half], sems.at[len(copies)]
                )
            )
    run_copies(copies)


def chunks_kernel(place, mine0, got0, mine, got, after, c0, c1, c2, c3, sems):
    k = place[2]
    copies = []
    for first, rest, half in ((mine0, mine, k), (got0, got, 1 - k)):
        for source, chunk in ((first, c0), (rest.at[0], c1), (rest.at[1], c2), (rest.at[2], c3)):
            copies.append(
                pltpu.make_async_copy(source, chunk.at[:, half], sems.at[len(copies)])
            )
    run_copies(copies)


def load_panel(place, pieces, panel, sems):
    y, k = place[1], place[2]
    parts = len(pieces) // NY
    copies = []
    for i, source in enumerate(pieces):
        hop, part = i // parts, i % parts
        rows = pl.ds(pl.multiple_of(along(y, 4 - hop, k) * CH, CH), CH)
        numbers = slice(part * (NY // parts), (part + 1) * (NY // parts))
        copies.append(pltpu.make_async_copy(source, panel.at[numbers, rows, :], sems.at[i]))
    run_copies(copies)


def product_kernel(count, summed, place, green, *rest):
    pieces, rest = rest[:count], rest[count:]
    acc, (out, panel, sems) = rest[:summed], rest[-3:]
    load_panel(place, pieces, panel, sems)
    for h in range(2):
        both = jnp.concatenate([panel[2 * h], panel[2 * h + 1]], axis=1)
        value = jnp.dot(green[...], both, preferred_element_type=F32)
        for i in range(2):
            part = value[:, i * W : (i + 1) * W]
            if summed:
                part = part + acc[0][2 * h + i].astype(F32)
            out[2 * h + i] = part.astype(BF16)


def product(place, green, pieces, acc, after=()):
    (out,) = call(
        functools.partial(product_kernel, len(pieces), len(acc)),
        [((NY, HALF, W), BF16)],
        (place, green, *pieces, *acc, *after),
        [SMEM, VMEM] + [ANY] * len(pieces) + [VMEM] * len(acc) + [ANY] * len(after),
        [VMEM],
        [pltpu.VMEM((NY, SPAN, W), BF16), pltpu.SemaphoreType.DMA((len(pieces),))],
        flops=2 * HALF * SPAN * 4 * W,
    )
    return out


def last_kernel(half, place, pattern, green, *rest):
    pieces, acc, rest = rest[:4], rest[4], rest[5:]
    if half:
        columns_t, terms, rest = rest[0], rest[1], rest[2:]
    outs, (panel, sems) = rest[:4], rest[4:]
    r, y, k = place[0], place[1], place[2]
    load_panel(place, pieces, panel, sems)
    c = y * 2 + (k if half == 0 else 1 - k)
    for h in range(2):
        order = [lax.rem(y + 2 * h + i, 4) for i in range(2)]
        both = jnp.concatenate([panel[order[0]], panel[order[1]]], axis=1)
        value = jnp.dot(green[...], both, preferred_element_type=F32)
        for i, q in enumerate(order):
            number = r * 8 + q * 2 + k
            out = outs[2 * h + i]
            for j in range(NR):
                for piece in range(3):
                    keep = -pattern[number, lax.div((j * 8 + c) * 3 + piece, 2)].astype(F32)
                    start = j * RD + piece * 64
                    rows = slice(start, start + 64)
                    part = value[rows, i * W : (i + 1) * W] + acc[q, rows, :].astype(F32)
                    out[rows, :] = (part * keep).astype(BF16)
            if half:
                term = jnp.dot(columns_t[1, q], out[0:HALF, :], preferred_element_type=F32)
                out[HALF : HALF + W, :] = (terms[2 * h + i] - term).astype(BF16)


def diag_kernel(place, columns_t, *rest):
    ended, out = rest[:4], rest[4]
    y = place[1]
    for d in range(4):
        q = lax.rem(y + d, 4)
        out[d] = -jnp.dot(columns_t[0, q], ended[d][...], preferred_element_type=F32)


def columns_kernel(place, x0, x1, x2, x3, out, columns, sems):
    r, k = place[0], place[2]
    run_copies(
        [
            pltpu.make_async_copy(source, columns.at[along(r, 1 + s, k)], sems.at[s])
            for s, source in enumerate((x0, x1, x2, x3))
        ]
    )
    for half in range(2):
        parity = k if half == 0 else 1 - k
        for q in range(NY):
            out[half, q] = columns[:, q, parity].reshape(HALF, W).T


def final_kernel(half, place, *rest):
    if half:
        pivot, parts, (_, panel, diag, terms, sems) = rest[0], rest[1:5], rest[5:]
    else:
        parts, (panel, sems) = rest[:4], rest[4:]
    y, k = place[1], place[2]
    copies, last = [], []
    for d in range(4):
        c = lax.rem(y + 4 - d, 4) * 2 + (k if half == 0 else 1 - k)
        for j in range(NR):
            copies.append(
                pltpu.make_async_copy(
                    parts[d].at[j * RD : (j + 1) * RD], panel.at[j, c], sems.at[len(copies)]
                )
            )
        if half:
            last.append(
                pltpu.make_async_copy(
                    parts[d].at[HALF : HALF + W], terms.at[d], sems.at[NR * NY + d]
                )
            )
    for copy in last + copies:
        copy.start()
    for copy in last:
        copy.wait()
    if half:
        total = pivot[...]
        for d in range(4):
            total += terms[d].astype(F32)
        diag[...] = total
    for copy in copies:
        copy.wait()


def local(green_blocks, lower_panel, pattern, pivot_inverse):
    r = lax.axis_index("row")
    col = lax.axis_index("col")
    place = jnp.stack([r, col // 2, col % 2, r * 8 + col]).astype(jnp.int32)
    dma = pltpu.SemaphoreType.DMA

    def sib(v):
        return lax.ppermute(v, "col", [(c, c ^ 1) for c in range(8)])

    def over_y(v, d):
        return lax.ppermute(v, "col", [(c, (c + 2 * d) % 8) for c in range(8)])

    def ring_y(v):
        return lax.ppermute(v, "col", [(c, (c + (6 if c % 2 else 2)) % 8) for c in range(8)])

    def ring_x(v, d=1):
        pairs = [(i, (i + (-8 * d if i % 2 else 8 * d)) % 32) for i in range(32)]
        return lax.ppermute(v, ("row", "col"), pairs)

    pattern = pattern.T
    small, large = ((NY, RD, W), BF16), ((3, NY, RD, W), BF16)
    mine0, theirs0, mine, theirs = call(
        prep_kernel,
        [small, small, large, large],
        (place, pattern, lower_panel),
        [SMEM, SMEM, VMEM],
        [ANY] * 4,
        [pltpu.VMEM((2, NR, NY, RD, W), BF16), dma((4,))],
    )
    got0 = sib(theirs0)
    got = sib(theirs)
    green_own = green_blocks.reshape(HALF, SPAN)
    greens = (green_own, sib(green_own))

    chunk = ((NY, 2, RD, W), BF16)
    first = call(
        first_chunk_kernel,
        [((2, 2, RD, W), BF16)] * 2,
        (place, mine0, got0, greens[1]),
        [SMEM] + [ANY] * 3,
        [ANY] * 2,
        [dma((4,))],
    )
    chunks = call(
        chunks_kernel,
        [chunk] * 4,
        (place, mine0, got0, mine, got, first[0]),
        [SMEM] + [ANY] * 5,
        [ANY] * 4,
        [dma((8,))],
    )
    columns = [ring_x(chunks[s], 3 - s) for s in range(NR - 1)] + [chunks[3]]
    (columns_t,) = call(
        columns_kernel,
        [((2, NY, W, HALF), BF16)],
        (place, *columns),
        [SMEM] + [ANY] * 4,
        [VMEM],
        [pltpu.VMEM((NR, NY, 2, RD, W), BF16), dma((4,))],
    )

    pieces = []
    for parts in (first, *((c,) for c in chunks[1:])):
        held = [p.reshape(-1, CH, W) for p in parts]
        pieces.append(list(held))
        for hop in range(NY - 1):
            held = [ring_y(p) for p in held]
            pieces[-1] += held

    acc = [(), ()]
    for s in range(NR - 1):
        for half in range(2):
            after = () if s else (out,) if half else (columns_t,)
            out = product(place, greens[half], pieces[s], acc[half], after)
            acc[half] = (ring_x(out),)
    parts, terms = [], ()
    for half in range(2):
        outs = call(
            functools.partial(last_kernel, half),
            [((HALF + W * half, W), BF16)] * 4,
            (place, pattern, greens[half], *pieces[3], *acc[half], *terms),
            [SMEM, SMEM, VMEM] + [ANY] * 4 + [VMEM] * (1 + len(terms)),
            [VMEM] * 4,
            [pltpu.VMEM((NY, SPAN, W), BF16), dma((4,))],
            flops=2 * HALF * SPAN * 4 * W,
        )
        parts += [outs[0]] + [over_y(outs[d], d) for d in (1, 2, 3)]
        if half == 0:
            (term,) = call(
                diag_kernel,
                [((4, W, W), F32)],
                (place, columns_t, *outs),
                [SMEM] + [VMEM] * 5,
                [VMEM],
                flops=2 * ORDER * W * W,
            )
            terms = (columns_t, term)
    panel = ((NR, NC, RD, W), BF16)
    (green_panel,) = call(
        functools.partial(final_kernel, 0),
        [panel],
        (place, *parts[:4]),
        [SMEM] + [ANY] * 4,
        [ANY],
        [dma((16,))],
    )
    green_panel, green_diag = call(
        functools.partial(final_kernel, 1),
        [panel, ((W, W), F32)],
        (place, pivot_inverse.reshape(W, W), *parts[4:], green_panel),
        [SMEM, VMEM] + [ANY] * 5,
        [ANY, VMEM],
        [pltpu.VMEM((4, W, W), BF16), dma((20,))],
        aliases=((6, 0),),
    )
    return green_panel.reshape(ORDER, 1, W), green_diag.reshape(1, W, W)


def solution(mesh):
    placed = (
        P("pole", "col", None, "row"),
        P(("row", "col"), "pole", None),
        P(),
        P(("row", "col"), "pole", None),
    )
    return jax.shard_map(
        local,
        mesh=mesh,
        in_specs=placed,
        out_specs=(P("pole", ("row", "col"), None), P(("row", "col"), "pole", None)),
        check_vma=False,
    )
```

profile of v0, /device:TPU:8, one launch (start us, length us, event | category | flops | bytes accessed | tf_op | source)
XLA Modules:
  0.0 129.5 jit_solution(6522935235831528967)
XLA Ops:
  3.0 2.6 %shard_map.59 = (bf16[4,192,128]{2,1,0:T(8,128)(2,1)S(1)}, bf16[4,192,128]{2,1,0:T(8,128)(2,1)S(1)}, bf16[3,4,192,128]{3,2,1,0:T(8,128)(2,1)S(1)}, bf16[3,4,192,128]{3,2,1,0:T(8,128)(2,1)S(1)}) custom-call(s32[4]{0:T(128)S(1)} %pad_add_fusion.place, s32[32,48]{1,0:T(8,128)S(1)} %bitcast.34, bf16[192,32,128]{2,1,0:T(8,128)(2,1)S(1)} %copy-done.1), custom_call_target="tpu_custom_call" | custom-call | bytes 4194304 | tf_op jit(solution)/shard_map/pallas_call | solution.py:37
  10.1 2.8 %collective-permute-start.18 = (bf16[4,2,192,128]{3,2,1,0:T(8,128)(2,1)S(1)}, bf16[4,2,192,128]{3,2,1,0:T(8,128)(2,1)S(1)}, u32[]{:S(2)}, u32[]{:S(2)}) collective-permute-start(bf16[4,2,192,128]{3,2,1,0:T(8,128)(2,1)S(1)} %get-tuple-element.31), channel_id=1, source_target_pairs={{0,24},{1,9},{2,26},{3,11},{4,28},{5,13},{6,30},{7,15},{8,0},{9,17... | collective-permute-start | bytes 1179656 | tf_op jit(solution)/shard_map/ppermute | solution.py:253
  22.3 5.4 %collective-permute-done.18.x0 = bf16[4,2,192,128]{3,2,1,0:T(8,128)(2,1)S(1)} collective-permute-done((bf16[4,2,192,128]{3,2,1,0:T(8,128)(2,1)S(1)}, bf16[4,2,192,128]{3,2,1,0:T(8,128)(2,1)S(1)}, u32[]{:S(2)}, u32[]{:S(2)}) %collective-permute-start.18) | collective-permute-done | bytes 393248 | tf_op jit(solution)/shard_map/ppermute | solution.py:253
  30.2 3.1 %collective-permute-done.15.rest_5_ = bf16[2,384,128]{2,1,0:T(8,128)(2,1)S(1)} collective-permute-done((bf16[2,384,128]{2,1,0:T(8,128)(2,1)S(1)}, bf16[2,384,128]{2,1,0:T(8,128)(2,1)S(1)}, u32[]{:S(2)}, u32[]{:S(2)}) %collective-permute-start.15) | collective-permute-done | bytes 196640 | tf_op jit(solution)/shard_map/ppermute | solution.py:249
  39.0 3.0 %shard_map.63.rest_8_ = bf16[4,768,128]{2,1,0:T(8,128)(2,1)S(1)} custom-call(s32[4]{0:T(128)S(1)} %pad_add_fusion.place, bf16[768,1536]{1,0:T(8,128)(2,1)S(1)} %bitcast.15, bf16[2,384,128]{2,1,0:T(8,128)(2,1)S(1)} %bitcast.23, bf16[2,384,128]{2,1,0:T(8,128)(2,1)S(1)} %bitcast.32, bf16[2,384,128]{2,1,0:T(8,128)(2,1)S(1)} %collective-permute-done.12.rest_2_, ...), custom_call_target="tpu_custom_call" | custom-call | flops 1207959552 | bytes 4194304 | tf_op jit(solution)/shard_map/pallas_call | solution.py:37
  42.1 3.0 %shard_map.64 = bf16[4,768,128]{2,1,0:T(8,128)(2,1)S(1)} custom-call(s32[4]{0:T(128)S(1)} %pad_add_fusion.place, bf16[768,1536]{1,0:T(8,128)(2,1)S(1)} %collective-permute-done.after.green, bf16[2,384,128]{2,1,0:T(8,128)(2,1)S(1)} %bitcast.24, bf16[2,384,128]{2,1,0:T(8,128)(2,1)S(1)} %bitcast.33, bf16[2,384,128]{2,1,0:T(8,128)(2,1)S(1)} %collective-permute-done.12.rest_2_, ...), custom_call_target="tpu_custom_call" | custom-call | flops 1207959552 | bytes 4194304 | tf_op jit(solution)/shard_map/pallas_call | solution.py:37
  47.9 5.5 %collective-permute-done.6.rest_1_ = bf16[4,384,128]{2,1,0:T(8,128)(2,1)S(1)} collective-permute-done((bf16[4,384,128]{2,1,0:T(8,128)(2,1)S(1)}, bf16[4,384,128]{2,1,0:T(8,128)(2,1)S(1)}, u32[]{:S(2)}, u32[]{:S(2)}) %collective-permute-start.6) | collective-permute-done | bytes 393248 | tf_op jit(solution)/shard_map/ppermute | solution.py:249
  54.8 2.8 %collective-permute-done.11.rest_3_ = bf16[4,384,128]{2,1,0:T(8,128)(2,1)S(1)} collective-permute-done((bf16[4,384,128]{2,1,0:T(8,128)(2,1)S(1)}, bf16[4,384,128]{2,1,0:T(8,128)(2,1)S(1)}, u32[]{:S(2)}, u32[]{:S(2)}) %collective-permute-start.11) | collective-permute-done | bytes 393248 | tf_op jit(solution)/shard_map/ppermute | solution.py:249
  57.6 2.2 %shard_map.67 = bf16[4,768,128]{2,1,0:T(8,128)(2,1)S(1)} custom-call(s32[4]{0:T(128)S(1)} %pad_add_fusion.place, bf16[768,1536]{1,0:T(8,128)(2,1)S(1)} %bitcast.16, bf16[4,384,128]{2,1,0:T(8,128)(2,1)S(1)} %bitcast.29, bf16[4,384,128]{2,1,0:T(8,128)(2,1)S(1)} %collective-permute-done.9.rest_1_, bf16[4,384,128]{2,1,0:T(8,128)(2,1)S(1)} %collective-permute-done.10.rest_2_, ...), custom_call_target="tpu_custom_call" | custom-call | flops 1207959552 | bytes 4194304 | tf_op jit(solution)/shard_map/pallas_call | solution.py:37
  59.9 5.5 %collective-permute-start.25 = (bf16[4,768,128]{2,1,0:T(8,128)(2,1)S(1)}, bf16[4,768,128]{2,1,0:T(8,128)(2,1)S(1)}, u32[]{:S(2)}, u32[]{:S(2)}) collective-permute-start(bf16[4,768,128]{2,1,0:T(8,128)(2,1)S(1)} %shard_map.67), channel_id=1, source_target_pairs={{0,8},{1,25},{2,10},{3,27},{4,12},{5,29},{6,14},{7,31},{8,16},{9,1... | collective-permute-start | bytes 2359304 | tf_op jit(solution)/shard_map/ppermute | solution.py:253
  65.4 2.2 %shard_map.65 = bf16[4,768,128]{2,1,0:T(8,128)(2,1)S(1)} custom-call(s32[4]{0:T(128)S(1)} %pad_add_fusion.place, bf16[768,1536]{1,0:T(8,128)(2,1)S(1)} %collective-permute-done.after.green, bf16[4,384,128]{2,1,0:T(8,128)(2,1)S(1)} %bitcast.30, bf16[4,384,128]{2,1,0:T(8,128)(2,1)S(1)} %collective-permute-done.9.rest_1_, ...), custom_call_target="tpu_custom_call" | custom-call | flops 1207959552 | bytes 4194304 | tf_op jit(solution)/shard_map/pallas_call | solution.py:37
  70.0 6.7 %collective-permute-done.3.rest_1_ = bf16[4,384,128]{2,1,0:T(8,128)(2,1)S(1)} collective-permute-done((bf16[4,384,128]{2,1,0:T(8,128)(2,1)S(1)}, bf16[4,384,128]{2,1,0:T(8,128)(2,1)S(1)}, u32[]{:S(2)}, u32[]{:S(2)}) %collective-permute-start.3) | collective-permute-done | bytes 393248 | tf_op jit(solution)/shard_map/ppermute | solution.py:249
  76.8 4.2 %collective-permute-done.8.rest_3_ = bf16[4,384,128]{2,1,0:T(8,128)(2,1)S(1)} collective-permute-done((bf16[4,384,128]{2,1,0:T(8,128)(2,1)S(1)}, bf16[4,384,128]{2,1,0:T(8,128)(2,1)S(1)}, u32[]{:S(2)}, u32[]{:S(2)}) %collective-permute-start.8) | collective-permute-done | bytes 393248 | tf_op jit(solution)/shard_map/ppermute | solution.py:249
  81.0 2.2 %shard_map.68 = bf16[4,768,128]{2,1,0:T(8,128)(2,1)S(1)} custom-call(s32[4]{0:T(128)S(1)} %pad_add_fusion.place, bf16[768,1536]{1,0:T(8,128)(2,1)S(1)} %bitcast.17, bf16[4,384,128]{2,1,0:T(8,128)(2,1)S(1)} %bitcast.26, bf16[4,384,128]{2,1,0:T(8,128)(2,1)S(1)} %collective-permute-done.6.rest_1_, bf16[4,384,128]{2,1,0:T(8,128)(2,1)S(1)} %collective-permute-done.7.rest_2_, ...), custom_call_target="tpu_custom_call" | custom-call | flops 1207959552 | bytes 4194304 | tf_op jit(solution)/shard_map/pallas_call | solution.py:37
  83.4 2.2 %shard_map.66 = bf16[4,768,128]{2,1,0:T(8,128)(2,1)S(1)} custom-call(s32[4]{0:T(128)S(1)} %pad_add_fusion.place, bf16[768,1536]{1,0:T(8,128)(2,1)S(1)} %collective-permute-done.after.green, bf16[4,384,128]{2,1,0:T(8,128)(2,1)S(1)} %bitcast.27, bf16[4,384,128]{2,1,0:T(8,128)(2,1)S(1)} %collective-permute-done.6.rest_1_, ...), custom_call_target="tpu_custom_call" | custom-call | flops 1207959552 | bytes 4194304 | tf_op jit(solution)/shard_map/pallas_call | solution.py:37
  85.7 2.5 %collective-permute-start.23 = (bf16[4,768,128]{2,1,0:T(8,128)(2,1)S(1)}, bf16[4,768,128]{2,1,0:T(8,128)(2,1)S(1)}, u32[]{:S(2)}, u32[]{:S(2)}) collective-permute-start(bf16[4,768,128]{2,1,0:T(8,128)(2,1)S(1)} %shard_map.66), channel_id=1, source_target_pairs={{0,8},{1,25},{2,10},{3,27},{4,12},{5,29},{6,14},{7,31},{8,16},{9,1... | collective-permute-start | bytes 2359304 | tf_op jit(solution)/shard_map/ppermute | solution.py:253
  89.1 10.1 %collective-permute-done.5.rest_3_ = bf16[4,384,128]{2,1,0:T(8,128)(2,1)S(1)} collective-permute-done((bf16[4,384,128]{2,1,0:T(8,128)(2,1)S(1)}, bf16[4,384,128]{2,1,0:T(8,128)(2,1)S(1)}, u32[]{:S(2)}, u32[]{:S(2)}) %collective-permute-start.5) | collective-permute-done | bytes 393248 | tf_op jit(solution)/shard_map/ppermute | solution.py:249
  99.2 2.5 %shard_map.69 = (bf16[768,128]{1,0:T(8,128)(2,1)S(1)}, bf16[768,128]{1,0:T(8,128)(2,1)S(1)}, bf16[768,128]{1,0:T(8,128)(2,1)S(1)}, bf16[768,128]{1,0:T(8,128)(2,1)S(1)}) custom-call(s32[4]{0:T(128)S(1)} %pad_add_fusion.place, s32[32,48]{1,0:T(8,128)S(1)} %bitcast.35, bf16[768,1536]{1,0:T(8,128)(2,1)S(1)} %bitcast.18, bf16[4,384,128]{2,1,0:T(8,128)(2,1)S(1)} %bitcast.20, ...), custom_call_target="tpu_custom_call" | custom-call | flops 1207959552 | bytes 4194304 | tf_op jit(solution)/shard_map/pallas_call | solution.py:37
  102.7 2.2 %collective-permute-done.23.rest_4_ = bf16[4,768,128]{2,1,0:T(8,128)(2,1)S(1)} collective-permute-done((bf16[4,768,128]{2,1,0:T(8,128)(2,1)S(1)}, bf16[4,768,128]{2,1,0:T(8,128)(2,1)S(1)}, u32[]{:S(2)}, u32[]{:S(2)}) %collective-permute-start.23) | collective-permute-done | bytes 786464 | tf_op jit(solution)/shard_map/ppermute | solution.py:253
  105.0 4.3 %shard_map.71 = (bf16[896,128]{1,0:T(8,128)(2,1)S(1)}, bf16[896,128]{1,0:T(8,128)(2,1)S(1)}, bf16[896,128]{1,0:T(8,128)(2,1)S(1)}, bf16[896,128]{1,0:T(8,128)(2,1)S(1)}) custom-call(s32[4]{0:T(128)S(1)} %pad_add_fusion.place, s32[32,48]{1,0:T(8,128)S(1)} %bitcast.36, bf16[768,1536]{1,0:T(8,128)(2,1)S(1)} %collective-permute-done.after.green, ...), custom_call_target="tpu_custom_call" | custom-call | flops 1207959552 | bytes 4194304 | tf_op jit(solution)/shard_map/pallas_call | solution.py:37
  109.4 5.3 %collective-permute-start.28 = (bf16[896,128]{1,0:T(8,128)(2,1)S(1)}, bf16[896,128]{1,0:T(8,128)(2,1)S(1)}, u32[]{:S(2)}, u32[]{:S(2)}) collective-permute-start(bf16[896,128]{1,0:T(8,128)(2,1)S(1)} %get-tuple-element.38), channel_id=1, source_target_pairs={{0,4},{1,5},{2,6},{3,7},{4,0},{5,1},{6,2},{7,3},{8,12},{9,13},{10,... | collective-permute-start | bytes 688136 | tf_op jit(solution)/shard_map/ppermute | solution.py:246
  115.6 3.1 %collective-permute-start.32 = (bf16[768,128]{1,0:T(8,128)(2,1)S(1)}, bf16[768,128]{1,0:T(8,128)(2,1)S(1)}, u32[]{:S(2)}, u32[]{:S(2)}) collective-permute-start(bf16[768,128]{1,0:T(8,128)(2,1)S(1)} %get-tuple-element.35.rest_3_), channel_id=1, source_target_pairs={{0,6},{1,7},{2,0},{3,1},{4,2},{5,3},{6,4},{7,5},{8,14},{9,15},{10,... | collective-permute-start | bytes 589832 | tf_op jit(solution)/shard_map/ppermute | solution.py:246
  118.8 4.6 %collective-permute-done.31.rest_2_ = bf16[768,128]{1,0:T(8,128)(2,1)S(1)} collective-permute-done((bf16[768,128]{1,0:T(8,128)(2,1)S(1)}, bf16[768,128]{1,0:T(8,128)(2,1)S(1)}, u32[]{:S(2)}, u32[]{:S(2)}) %collective-permute-start.31) | collective-permute-done | bytes 196640 | tf_op jit(solution)/shard_map/ppermute | solution.py:246
  126.9 2.4 %shard_map.73 = (bf16[4,8,192,128]{3,2,1,0:T(8,128)(2,1)}, f32[128,128]{1,0:T(8,128)}) custom-call(s32[4]{0:T(128)S(1)} %pad_add_fusion.place, f32[128,128]{1,0:T(8,128)S(1)} %bitcast.37, bf16[896,128]{1,0:T(8,128)(2,1)S(1)} %get-tuple-element.36.rest_1_, bf16[896,128]{1,0:T(8,128)(2,1)S(1)} %collective-permute-done.27.rest_2_, ...), custom_call_target="tpu_custom_call", output_to_operand_aliasing={{0}: (6, {})} | custom-call | bytes 4194304 | tf_op jit(solution)/shard_map/pallas_call | solution.py:37
  (68 shorter events, 37.6 us)
Async XLA Ops:
  10.1 17.5 %collective-permute-start.18 = (bf16[4,2,192,128]{3,2,1,0:T(8,128)(2,1)S(1)}, bf16[4,2,192,128]{3,2,1,0:T(8,128)(2,1)S(1)}, u32[]{:S(2)}, u32[]{:S(2)}) collective-permute-start(bf16[4,2,192,128]{3,2,1,0:T(8,128)(2,1)S(1)} %get-tuple-element.31), channel_id=1, source_target_pairs={{0,24},{1,9},{2,26},{3,11},{4,28},{5,13},{6,30},{7,15},{8,0},{9,17... | collective-permute-start | bytes 1179656 | tf_op jit(solution)/shard_map/ppermute | solution.py:253
  15.8 20.1 %collective-permute-start.19 = (bf16[4,2,192,128]{3,2,1,0:T(8,128)(2,1)S(1)}, bf16[4,2,192,128]{3,2,1,0:T(8,128)(2,1)S(1)}, u32[]{:S(2)}, u32[]{:S(2)}) collective-permute-start(bf16[4,2,192,128]{3,2,1,0:T(8,128)(2,1)S(1)} %get-tuple-element.29), channel_id=1, source_target_pairs={{0,16},{1,17},{2,18},{3,19},{4,20},{5,21},{6,22},{7,23},{8,24},{9,... | collective-permute-start | bytes 1179656 | tf_op jit(solution)/shard_map/ppermute | solution.py:253
  16.6 18.4 %collective-permute-start.9 = (bf16[4,384,128]{2,1,0:T(8,128)(2,1)S(1)}, bf16[4,384,128]{2,1,0:T(8,128)(2,1)S(1)}, u32[]{:S(2)}, u32[]{:S(2)}) collective-permute-start(bf16[4,384,128]{2,1,0:T(8,128)(2,1)S(1)} %bitcast.28), channel_id=1, source_target_pairs={{0,2},{1,7},{2,4},{3,1},{4,6},{5,3},{6,0},{7,5},{8,10},{9,15},{10,... | collective-permute-start | bytes 1179656 | tf_op jit(solution)/shard_map/ppermute | solution.py:249
  18.6 17.3 %collective-permute-start.20 = (bf16[4,2,192,128]{3,2,1,0:T(8,128)(2,1)S(1)}, bf16[4,2,192,128]{3,2,1,0:T(8,128)(2,1)S(1)}, u32[]{:S(2)}, u32[]{:S(2)}) collective-permute-start(bf16[4,2,192,128]{3,2,1,0:T(8,128)(2,1)S(1)} %get-tuple-element.28), channel_id=1, source_target_pairs={{0,8},{1,25},{2,10},{3,27},{4,12},{5,29},{6,14},{7,31},{8,16},{9,1... | collective-permute-start | bytes 1179656 | tf_op jit(solution)/shard_map/ppermute | solution.py:253
  20.7 8.7 %collective-permute-start.14 = (bf16[2,384,128]{2,1,0:T(8,128)(2,1)S(1)}, bf16[2,384,128]{2,1,0:T(8,128)(2,1)S(1)}, u32[]{:S(2)}, u32[]{:S(2)}) collective-permute-start(bf16[2,384,128]{2,1,0:T(8,128)(2,1)S(1)} %collective-permute-done.12.rest_2_), channel_id=1, source_target_pairs={{0,2},{1,7},{2,4},{3,1},{4,6},{5,3},{6,0},{7,5},{8,10},{9,15},{10,... | collective-permute-start | bytes 589832 | tf_op jit(solution)/shard_map/ppermute | solution.py:249
  29.3 8.3 %collective-permute-start.16 = (bf16[2,384,128]{2,1,0:T(8,128)(2,1)S(1)}, bf16[2,384,128]{2,1,0:T(8,128)(2,1)S(1)}, u32[]{:S(2)}, u32[]{:S(2)}) collective-permute-start(bf16[2,384,128]{2,1,0:T(8,128)(2,1)S(1)} %collective-permute-done.14.rest_4_), channel_id=1, source_target_pairs={{0,2},{1,7},{2,4},{3,1},{4,6},{5,3},{6,0},{7,5},{8,10},{9,15},{10,... | collective-permute-start | bytes 589832 | tf_op jit(solution)/shard_map/ppermute | solution.py:249
  35.0 12.0 %collective-permute-start.10 = (bf16[4,384,128]{2,1,0:T(8,128)(2,1)S(1)}, bf16[4,384,128]{2,1,0:T(8,128)(2,1)S(1)}, u32[]{:S(2)}, u32[]{:S(2)}) collective-permute-start(bf16[4,384,128]{2,1,0:T(8,128)(2,1)S(1)} %collective-permute-done.9.rest_1_), channel_id=1, source_target_pairs={{0,2},{1,7},{2,4},{3,1},{4,6},{5,3},{6,0},{7,5},{8,10},{9,15},{10,... | collective-permute-start | bytes 1179656 | tf_op jit(solution)/shard_map/ppermute | solution.py:249
  42.0 15.6 %collective-permute-start.24 = (bf16[4,768,128]{2,1,0:T(8,128)(2,1)S(1)}, bf16[4,768,128]{2,1,0:T(8,128)(2,1)S(1)}, u32[]{:S(2)}, u32[]{:S(2)}) collective-permute-start(bf16[4,768,128]{2,1,0:T(8,128)(2,1)S(1)} %shard_map.63.rest_8_), channel_id=1, source_target_pairs={{0,8},{1,25},{2,10},{3,27},{4,12},{5,29},{6,14},{7,31},{8,16},{9,1... | collective-permute-start | bytes 2359304 | tf_op jit(solution)/shard_map/ppermute | solution.py:253
  45.1 20.3 %collective-permute-start.21 = (bf16[4,768,128]{2,1,0:T(8,128)(2,1)S(1)}, bf16[4,768,128]{2,1,0:T(8,128)(2,1)S(1)}, u32[]{:S(2)}, u32[]{:S(2)}) collective-permute-start(bf16[4,768,128]{2,1,0:T(8,128)(2,1)S(1)} %shard_map.64), channel_id=1, source_target_pairs={{0,8},{1,25},{2,10},{3,27},{4,12},{5,29},{6,14},{7,31},{8,16},{9,1... | collective-permute-start | bytes 2359304 | tf_op jit(solution)/shard_map/ppermute | solution.py:253
  47.0 10.6 %collective-permute-start.11 = (bf16[4,384,128]{2,1,0:T(8,128)(2,1)S(1)}, bf16[4,384,128]{2,1,0:T(8,128)(2,1)S(1)}, u32[]{:S(2)}, u32[]{:S(2)}) collective-permute-start(bf16[4,384,128]{2,1,0:T(8,128)(2,1)S(1)} %collective-permute-done.10.rest_2_), channel_id=1, source_target_pairs={{0,2},{1,7},{2,4},{3,1},{4,6},{5,3},{6,0},{7,5},{8,10},{9,15},{10,... | collective-permute-start | bytes 1179656 | tf_op jit(solution)/shard_map/ppermute | solution.py:249
  53.4 15.3 %collective-permute-start.7 = (bf16[4,384,128]{2,1,0:T(8,128)(2,1)S(1)}, bf16[4,384,128]{2,1,0:T(8,128)(2,1)S(1)}, u32[]{:S(2)}, u32[]{:S(2)}) collective-permute-start(bf16[4,384,128]{2,1,0:T(8,128)(2,1)S(1)} %collective-permute-done.6.rest_1_), channel_id=1, source_target_pairs={{0,2},{1,7},{2,4},{3,1},{4,6},{5,3},{6,0},{7,5},{8,10},{9,15},{10,... | collective-permute-start | bytes 1179656 | tf_op jit(solution)/shard_map/ppermute | solution.py:249
  59.9 21.1 %collective-permute-start.25 = (bf16[4,768,128]{2,1,0:T(8,128)(2,1)S(1)}, bf16[4,768,128]{2,1,0:T(8,128)(2,1)S(1)}, u32[]{:S(2)}, u32[]{:S(2)}) collective-permute-start(bf16[4,768,128]{2,1,0:T(8,128)(2,1)S(1)} %shard_map.67), channel_id=1, source_target_pairs={{0,8},{1,25},{2,10},{3,27},{4,12},{5,29},{6,14},{7,31},{8,16},{9,1... | collective-permute-start | bytes 2359304 | tf_op jit(solution)/shard_map/ppermute | solution.py:253
  67.6 15.8 %collective-permute-start.22 = (bf16[4,768,128]{2,1,0:T(8,128)(2,1)S(1)}, bf16[4,768,128]{2,1,0:T(8,128)(2,1)S(1)}, u32[]{:S(2)}, u32[]{:S(2)}) collective-permute-start(bf16[4,768,128]{2,1,0:T(8,128)(2,1)S(1)} %shard_map.65), channel_id=1, source_target_pairs={{0,8},{1,25},{2,10},{3,27},{4,12},{5,29},{6,14},{7,31},{8,16},{9,1... | collective-permute-start | bytes 2359304 | tf_op jit(solution)/shard_map/ppermute | solution.py:253
  67.8 9.0 %collective-permute-start.3 = (bf16[4,384,128]{2,1,0:T(8,128)(2,1)S(1)}, bf16[4,384,128]{2,1,0:T(8,128)(2,1)S(1)}, u32[]{:S(2)}, u32[]{:S(2)}) collective-permute-start(bf16[4,384,128]{2,1,0:T(8,128)(2,1)S(1)} %bitcast.19), channel_id=1, source_target_pairs={{0,2},{1,7},{2,4},{3,1},{4,6},{5,3},{6,0},{7,5},{8,10},{9,15},{10,... | collective-permute-start | bytes 1179656 | tf_op jit(solution)/shard_map/ppermute | solution.py:249
  68.8 12.2 %collective-permute-start.8 = (bf16[4,384,128]{2,1,0:T(8,128)(2,1)S(1)}, bf16[4,384,128]{2,1,0:T(8,128)(2,1)S(1)}, u32[]{:S(2)}, u32[]{:S(2)}) collective-permute-start(bf16[4,384,128]{2,1,0:T(8,128)(2,1)S(1)} %collective-permute-done.7.rest_2_), channel_id=1, source_target_pairs={{0,2},{1,7},{2,4},{3,1},{4,6},{5,3},{6,0},{7,5},{8,10},{9,15},{10,... | collective-permute-start | bytes 1179656 | tf_op jit(solution)/shard_map/ppermute | solution.py:249
  76.8 11.3 %collective-permute-start.4 = (bf16[4,384,128]{2,1,0:T(8,128)(2,1)S(1)}, bf16[4,384,128]{2,1,0:T(8,128)(2,1)S(1)}, u32[]{:S(2)}, u32[]{:S(2)}) collective-permute-start(bf16[4,384,128]{2,1,0:T(8,128)(2,1)S(1)} %collective-permute-done.3.rest_1_), channel_id=1, source_target_pairs={{0,2},{1,7},{2,4},{3,1},{4,6},{5,3},{6,0},{7,5},{8,10},{9,15},{10,... | collective-permute-start | bytes 1179656 | tf_op jit(solution)/shard_map/ppermute | solution.py:249
  83.3 16.0 %collective-permute-start.26 = (bf16[4,768,128]{2,1,0:T(8,128)(2,1)S(1)}, bf16[4,768,128]{2,1,0:T(8,128)(2,1)S(1)}, u32[]{:S(2)}, u32[]{:S(2)}) collective-permute-start(bf16[4,768,128]{2,1,0:T(8,128)(2,1)S(1)} %shard_map.68), channel_id=1, source_target_pairs={{0,8},{1,25},{2,10},{3,27},{4,12},{5,29},{6,14},{7,31},{8,16},{9,1... | collective-permute-start | bytes 2359304 | tf_op jit(solution)/shard_map/ppermute | solution.py:253
  85.7 19.3 %collective-permute-start.23 = (bf16[4,768,128]{2,1,0:T(8,128)(2,1)S(1)}, bf16[4,768,128]{2,1,0:T(8,128)(2,1)S(1)}, u32[]{:S(2)}, u32[]{:S(2)}) collective-permute-start(bf16[4,768,128]{2,1,0:T(8,128)(2,1)S(1)} %shard_map.66), channel_id=1, source_target_pairs={{0,8},{1,25},{2,10},{3,27},{4,12},{5,29},{6,14},{7,31},{8,16},{9,1... | collective-permute-start | bytes 2359304 | tf_op jit(solution)/shard_map/ppermute | solution.py:253
  88.1 11.1 %collective-permute-start.5 = (bf16[4,384,128]{2,1,0:T(8,128)(2,1)S(1)}, bf16[4,384,128]{2,1,0:T(8,128)(2,1)S(1)}, u32[]{:S(2)}, u32[]{:S(2)}) collective-permute-start(bf16[4,384,128]{2,1,0:T(8,128)(2,1)S(1)} %collective-permute-done.4.rest_2_), channel_id=1, source_target_pairs={{0,2},{1,7},{2,4},{3,1},{4,6},{5,3},{6,0},{7,5},{8,10},{9,15},{10,... | collective-permute-start | bytes 1179656 | tf_op jit(solution)/shard_map/ppermute | solution.py:249
  101.7 13.9 %collective-permute-start.30 = (bf16[768,128]{1,0:T(8,128)(2,1)S(1)}, bf16[768,128]{1,0:T(8,128)(2,1)S(1)}, u32[]{:S(2)}, u32[]{:S(2)}) collective-permute-start(bf16[768,128]{1,0:T(8,128)(2,1)S(1)} %get-tuple-element.33.rest_1_), channel_id=1, source_target_pairs={{0,2},{1,3},{2,4},{3,5},{4,6},{5,7},{6,0},{7,1},{8,10},{9,11},{10,... | collective-permute-start | bytes 589832 | tf_op jit(solution)/shard_map/ppermute | solution.py:246
  109.3 17.6 %collective-permute-start.27 = (bf16[896,128]{1,0:T(8,128)(2,1)S(1)}, bf16[896,128]{1,0:T(8,128)(2,1)S(1)}, u32[]{:S(2)}, u32[]{:S(2)}) collective-permute-start(bf16[896,128]{1,0:T(8,128)(2,1)S(1)} %get-tuple-element.37), channel_id=1, source_target_pairs={{0,2},{1,3},{2,4},{3,5},{4,6},{5,7},{6,0},{7,1},{8,10},{9,11},{10,... | collective-permute-start | bytes 688136 | tf_op jit(solution)/shard_map/ppermute | solution.py:246
  109.4 17.5 %collective-permute-start.28 = (bf16[896,128]{1,0:T(8,128)(2,1)S(1)}, bf16[896,128]{1,0:T(8,128)(2,1)S(1)}, u32[]{:S(2)}, u32[]{:S(2)}) collective-permute-start(bf16[896,128]{1,0:T(8,128)(2,1)S(1)} %get-tuple-element.38), channel_id=1, source_target_pairs={{0,4},{1,5},{2,6},{3,7},{4,0},{5,1},{6,2},{7,3},{8,12},{9,13},{10,... | collective-permute-start | bytes 688136 | tf_op jit(solution)/shard_map/ppermute | solution.py:246
  114.7 12.2 %collective-permute-start.29 = (bf16[896,128]{1,0:T(8,128)(2,1)S(1)}, bf16[896,128]{1,0:T(8,128)(2,1)S(1)}, u32[]{:S(2)}, u32[]{:S(2)}) collective-permute-start(bf16[896,128]{1,0:T(8,128)(2,1)S(1)} %get-tuple-element.39), channel_id=1, source_target_pairs={{0,6},{1,7},{2,0},{3,1},{4,2},{5,3},{6,4},{7,5},{8,14},{9,15},{10,... | collective-permute-start | bytes 688136 | tf_op jit(solution)/shard_map/ppermute | solution.py:246
  115.6 9.7 %collective-permute-start.32 = (bf16[768,128]{1,0:T(8,128)(2,1)S(1)}, bf16[768,128]{1,0:T(8,128)(2,1)S(1)}, u32[]{:S(2)}, u32[]{:S(2)}) collective-permute-start(bf16[768,128]{1,0:T(8,128)(2,1)S(1)} %get-tuple-element.35.rest_3_), channel_id=1, source_target_pairs={{0,6},{1,7},{2,0},{3,1},{4,2},{5,3},{6,4},{7,5},{8,14},{9,15},{10,... | collective-permute-start | bytes 589832 | tf_op jit(solution)/shard_map/ppermute | solution.py:246
  (14 other events, 91.2 us)
where the time goes:
time: 131 us; the launch traced here: 129 us
  waiting for transfers between devices  53.7 us (41%)
  starting transfers between devices  39.4 us (30%)
  Pallas kernels  33 us (25%)
  local copies, waits for them, and re-layouts  2.14 us (2%)
    ppermute x15, waiting for transfers between devices, ring_y(): lax.ppermute(v, 'col', [(c, (c + (6 if c % 2 else 2)) % 8) for c in range...  37.7 us
    pallas_call x15, Pallas kernels, call(): pl.pallas_call(kernel, out_shape=[jax.ShapeDtypeStruct(s, d) for s, d in...  33 us
    ppermute x15, starting transfers between devices, ring_y(): lax.ppermute(v, 'col', [(c, (c + (6 if c % 2 else 2)) % 8) for c in range...  17 us
    ppermute x9, starting transfers between devices, ring_x(): return lax.ppermute(v, ('row', 'col'), pairs)  12.1 us
    ppermute x6, starting transfers between devices, over_y(): return lax.ppermute(v, 'col', [(c, (c + 2 * d) % 8) for c in range(8)])  9.55 us
    ppermute x9, waiting for transfers between devices, ring_x(): return lax.ppermute(v, ('row', 'col'), pairs)  7.6 us
    ppermute x6, waiting for transfers between devices, over_y(): return lax.ppermute(v, 'col', [(c, (c + 2 * d) % 8) for c in range(8)])  6.58 us
  transfers between devices with their start and end apart: 33, of which 14 were waited for; matrix products, arithmetic and copies ran while one was open for 0% of the time, Pallas kernels for 23%

commit v1 on v0

--- a/solution.py
+++ b/solution.py
@@ -22,6 +22,7 @@
 SPAN = NC * RD
 HALF = NR * RD
 ORDER = NR * NC * RD
+UP = 1
 
 
 def run_copies(copies):
@@ -32,7 +33,7 @@
 
 
 def call(
-    kernel, outs, ins, specs, out_specs, scratch=(), flops=0, bytes_accessed=4 * 2**20, aliases=()
+    kernel, outs, ins, specs, out_specs, scratch=(), flops=0, bytes_accessed=1024, aliases=()
 ):
     return pl.pallas_call(
         kernel,
@@ -49,11 +50,11 @@
 
 
 def step_of(r, group, core):
-    return lax.rem(r + 3 - group, 4) if core == 0 else lax.rem(group + 3 - r, 4)
+    return lax.rem(r + 3 - group, 4) if core == UP else lax.rem(group + 3 - r, 4)
 
 
 def along(index, count, core):
-    return lax.rem(index + jnp.where(core == 0, count, 4 - count), 4)
+    return lax.rem(index + jnp.where(core == UP, count, 4 - count), 4)
 
 
 def prep_kernel(place, pattern, panel, mine0, theirs0, mine, theirs, turned, sems):
@@ -87,44 +88,42 @@
     )
 
 
-def first_chunk_kernel(place, mine, got, after, first, second, sems):
+def first_chunk_kernel(place, mine, got, after, chunk, sems):
+    k = place[2]
+    run_copies(
+        [
+            pltpu.make_async_copy(source, chunk.at[:, half], sems.at[i])
+            for i, (source, half) in enumerate(((mine, k), (got, 1 - k)))
+        ]
+    )
+
+
+def chunks_kernel(place, mine, got, after, c1, c2, c3, sems):
     k = place[2]
     copies = []
-    for i, part in enumerate((first, second)):
-        for source, half in ((mine, k), (got, 1 - k)):
+    for source, half in ((mine, k), (got, 1 - k)):
+        for i, chunk in enumerate((c1, c2, c3)):
             copies.append(
-                pltpu.make_async_copy(
-                    source.at[2 * i : 2 * i + 2], part.at[:, half], sems.at[len(copies)]
-                )
+                pltpu.make_async_copy(source.at[i], chunk.at[:, half], sems.at[len(copies)])
             )
     run_copies(copies)
 
 
-def chunks_kernel(place, mine0, got0, mine, got, after, c0, c1, c2, c3, sems):
-    k = place[2]
-    copies = []
-    for first, rest, half in ((mine0, mine, k), (got0, got, 1 - k)):
-        for source, chunk in ((first, c0), (rest.at[0], c1), (rest.at[1], c2), (rest.at[2], c3)):
-            copies.append(
-                pltpu.make_async_copy(source, chunk.at[:, half], sems.at[len(copies)])
-            )
-    run_copies(copies)
+def after_kernel(value, first, second, out, sems):
+    run_copies([pltpu.make_async_copy(value, out, sems.at[0])])
 
 
 def load_panel(place, pieces, panel, sems):
     y, k = place[1], place[2]
-    parts = len(pieces) // NY
     copies = []
-    for i, source in enumerate(pieces):
-        hop, part = i // parts, i % parts
+    for hop, source in enumerate(pieces):
         rows = pl.ds(pl.multiple_of(along(y, 4 - hop, k) * CH, CH), CH)
-        numbers = slice(part * (NY // parts), (part + 1) * (NY // parts))
-        copies.append(pltpu.make_async_copy(source, panel.at[numbers, rows, :], sems.at[i]))
+        copies.append(pltpu.make_async_copy(source, panel.at[:, rows, :], sems.at[hop]))
     run_copies(copies)
 
 
-def product_kernel(count, summed, place, green, *rest):
-    pieces, rest = rest[:count], rest[count:]
+def product_kernel(summed, place, green, *rest):
+    pieces, rest = rest[:4], rest[4:]
     acc, (out, panel, sems) = rest[:summed], rest[-3:]
     load_panel(place, pieces, panel, sems)
     for h in range(2):
@@ -139,13 +138,12 @@
 
 def product(place, green, pieces, acc, after=()):
     (out,) = call(
-        functools.partial(product_kernel, len(pieces), len(acc)),
+        functools.partial(product_kernel, len(acc)),
         [((NY, HALF, W), BF16)],
         (place, green, *pieces, *acc, *after),
-        [SMEM, VMEM] + [ANY] * len(pieces) + [VMEM] * len(acc) + [ANY] * len(after),
+        [SMEM, VMEM] + [ANY] * 4 + [VMEM] * len(acc) + [ANY] * len(after),
         [VMEM],
-        [pltpu.VMEM((NY, SPAN, W), BF16), pltpu.SemaphoreType.DMA((len(pieces),))],
-        flops=2 * HALF * SPAN * 4 * W,
+        [pltpu.VMEM((NY, SPAN, W), BF16), pltpu.SemaphoreType.DMA((4,))],
     )
     return out
 
@@ -153,9 +151,12 @@
 def last_kernel(half, place, pattern, green, *rest):
     pieces, acc, rest = rest[:4], rest[4], rest[5:]
     if half:
-        columns_t, terms, rest = rest[0], rest[1], rest[2:]
-    outs, (panel, sems) = rest[:4], rest[4:]
+        columns_t, terms, opposite, rest = rest[0], rest[1], rest[2], rest[5:]
+    outs, (panel, sems, *own) = rest[:4], rest[4:]
     r, y, k = place[0], place[1], place[2]
+    if half:
+        first = pltpu.make_async_copy(opposite, outs[2].at[HALF + W :], own[0].at[0])
+        first.start()
     load_panel(place, pieces, panel, sems)
     c = y * 2 + (k if half == 0 else 1 - k)
     for h in range(2):
@@ -175,6 +176,8 @@
             if half:
                 term = jnp.dot(columns_t[1, q], out[0:HALF, :], preferred_element_type=F32)
                 out[HALF : HALF + W, :] = (terms[2 * h + i] - term).astype(BF16)
+    if half:
+        first.wait()
 
 
 def diag_kernel(place, columns_t, *rest):
@@ -199,36 +202,36 @@
             out[half, q] = columns[:, q, parity].reshape(HALF, W).T
 
 
-def final_kernel(half, place, *rest):
-    if half:
-        pivot, parts, (_, panel, diag, terms, sems) = rest[0], rest[1:5], rest[5:]
-    else:
-        parts, (panel, sems) = rest[:4], rest[4:]
+def final_kernel(place, pivot, *rest):
+    parts, (panel, diag, terms, sems) = rest[:7], rest[7:]
     y, k = place[1], place[2]
+    sources = [
+        (parts[0], 0, 0, 0),
+        (parts[1], 0, 0, 1),
+        (parts[2], 0, 0, 3),
+        (parts[5], HALF + W, 0, 2),
+        (parts[3], 0, 1, 0),
+        (parts[4], 0, 1, 1),
+        (parts[5], 0, 1, 2),
+        (parts[6], 0, 1, 3),
+    ]
     copies, last = [], []
-    for d in range(4):
+    for source, start, half, d in sources:
         c = lax.rem(y + 4 - d, 4) * 2 + (k if half == 0 else 1 - k)
         for j in range(NR):
-            copies.append(
-                pltpu.make_async_copy(
-                    parts[d].at[j * RD : (j + 1) * RD], panel.at[j, c], sems.at[len(copies)]
-                )
-            )
+            rows = source.at[start + j * RD : start + (j + 1) * RD]
+            copies.append(pltpu.make_async_copy(rows, panel.at[j, c], sems.at[len(copies)]))
         if half:
-            last.append(
-                pltpu.make_async_copy(
-                    parts[d].at[HALF : HALF + W], terms.at[d], sems.at[NR * NY + d]
-                )
-            )
+            rows = source.at[HALF : HALF + W]
+            last.append(pltpu.make_async_copy(rows, terms.at[d], sems.at[NR * NC + d]))
     for copy in last + copies:
         copy.start()
     for copy in last:
         copy.wait()
-    if half:
-        total = pivot[...]
-        for d in range(4):
-            total += terms[d].astype(F32)
-        diag[...] = total
+    total = pivot[...]
+    for d in range(4):
+        total += terms[d].astype(F32)
+    diag[...] = total
     for copy in copies:
         copy.wait()
 
@@ -245,11 +248,12 @@
     def over_y(v, d):
         return lax.ppermute(v, "col", [(c, (c + 2 * d) % 8) for c in range(8)])
 
-    def ring_y(v):
-        return lax.ppermute(v, "col", [(c, (c + (6 if c % 2 else 2)) % 8) for c in range(8)])
+    def ring_y(v, d=1):
+        pairs = [(c, (c + (2 * d if c % 2 == UP else -2 * d)) % 8) for c in range(8)]
+        return lax.ppermute(v, "col", pairs)
 
     def ring_x(v, d=1):
-        pairs = [(i, (i + (-8 * d if i % 2 else 8 * d)) % 32) for i in range(32)]
+        pairs = [(i, (i + (8 * d if i % 2 == UP else -8 * d)) % 32) for i in range(32)]
         return lax.ppermute(v, ("row", "col"), pairs)
 
     pattern = pattern.T
@@ -268,23 +272,34 @@
     greens = (green_own, sib(green_own))
 
     chunk = ((NY, 2, RD, W), BF16)
-    first = call(
+    (chunk0,) = call(
         first_chunk_kernel,
-        [((2, 2, RD, W), BF16)] * 2,
+        [chunk],
         (place, mine0, got0, greens[1]),
         [SMEM] + [ANY] * 3,
-        [ANY] * 2,
-        [dma((4,))],
-    )
-    chunks = call(
-        chunks_kernel,
-        [chunk] * 4,
-        (place, mine0, got0, mine, got, first[0]),
-        [SMEM] + [ANY] * 5,
-        [ANY] * 4,
-        [dma((8,))],
-    )
-    columns = [ring_x(chunks[s], 3 - s) for s in range(NR - 1)] + [chunks[3]]
+        [ANY],
+        [dma((2,))],
+    )
+    chunks = (chunk0,) + tuple(
+        call(
+            chunks_kernel,
+            [chunk] * 3,
+            (place, mine, got, chunk0),
+            [SMEM] + [ANY] * 3,
+            [ANY] * 3,
+            [dma((6,))],
+        )
+    )
+    columns = [ring_x(chunks[0], 3), None, ring_x(chunks[2], 1), chunks[3]]
+    (sent,) = call(
+        after_kernel,
+        [chunk],
+        (chunks[1], columns[0], columns[2]),
+        [ANY] * 3,
+        [ANY],
+        [dma((1,))],
+    )
+    columns[1] = ring_x(sent, 2)
     (columns_t,) = call(
         columns_kernel,
         [((2, NY, W, HALF), BF16)],
@@ -295,31 +310,54 @@
     )
 
     pieces = []
-    for parts in (first, *((c,) for c in chunks[1:])):
-        held = [p.reshape(-1, CH, W) for p in parts]
-        pieces.append(list(held))
-        for hop in range(NY - 1):
-            held = [ring_y(p) for p in held]
-            pieces[-1] += held
-
+    for s in range(NR):
+        sent = own = chunks[s].reshape(NY, CH, W)
+        if s:
+            (sent,) = call(
+                after_kernel,
+                [((NY, CH, W), BF16)],
+                (own, *near),
+                [ANY] * 3,
+                [ANY],
+                [dma((1,))],
+            )
+        near = (ring_y(sent), ring_y(sent, -1))
+        pieces.append((own, near[0], ring_y(near[0]), near[1]))
+
+    before = {
+        (0, 0): (columns[0], columns[2]),
+        (0, 1): (pieces[1][1], pieces[1][3], columns[1]),
+        (1, 0): (columns_t,),
+        (1, 1): (pieces[2][1], pieces[2][3]),
+        (2, 0): (),
+        (2, 1): (pieces[3][1], pieces[3][3]),
+    }
     acc = [(), ()]
     for s in range(NR - 1):
         for half in range(2):
-            after = () if s else (out,) if half else (columns_t,)
+            after = before[s, half]
+            if s == 0 and half:
+                after += (out,)
             out = product(place, greens[half], pieces[s], acc[half], after)
             acc[half] = (ring_x(out),)
-    parts, terms = [], ()
+    parts, terms, last_after = [], (), ()
     for half in range(2):
+        rows = [HALF + W * half] * 4
+        rows[2] += HALF * half
         outs = call(
             functools.partial(last_kernel, half),
-            [((HALF + W * half, W), BF16)] * 4,
-            (place, pattern, greens[half], *pieces[3], *acc[half], *terms),
-            [SMEM, SMEM, VMEM] + [ANY] * 4 + [VMEM] * (1 + len(terms)),
+            [((n, W), BF16) for n in rows],
+            (place, pattern, greens[half], *pieces[3], *acc[half], *terms, *last_after),
+            [SMEM, SMEM, VMEM]
+            + [ANY] * 4
+            + [VMEM] * (1 + len(terms))
+            + [ANY] * len(last_after),
             [VMEM] * 4,
-            [pltpu.VMEM((NY, SPAN, W), BF16), dma((4,))],
-            flops=2 * HALF * SPAN * 4 * W,
+            [pltpu.VMEM((NY, SPAN, W), BF16), dma((4,))] + [dma((1,))] * half,
         )
-        parts += [outs[0]] + [over_y(outs[d], d) for d in (1, 2, 3)]
+        parts.append(outs[0])
+        for d in (1, 2, 3) if half else (1, 3):
+            parts.append(over_y(outs[d], d))
         if half == 0:
             (term,) = call(
                 diag_kernel,
@@ -327,26 +365,16 @@
                 (place, columns_t, *outs),
                 [SMEM] + [VMEM] * 5,
                 [VMEM],
-                flops=2 * ORDER * W * W,
             )
             terms = (columns_t, term)
-    panel = ((NR, NC, RD, W), BF16)
-    (green_panel,) = call(
-        functools.partial(final_kernel, 0),
-        [panel],
-        (place, *parts[:4]),
-        [SMEM] + [ANY] * 4,
-        [ANY],
-        [dma((16,))],
-    )
+            last_after = (outs[2], parts[1], parts[2])
     green_panel, green_diag = call(
-        functools.partial(final_kernel, 1),
-        [panel, ((W, W), F32)],
-        (place, pivot_inverse.reshape(W, W), *parts[4:], green_panel),
-        [SMEM, VMEM] + [ANY] * 5,
+        final_kernel,
+        [((NR, NC, RD, W), BF16), ((W, W), F32)],
+        (place, pivot_inverse.reshape(W, W), *parts),
+        [SMEM, VMEM] + [ANY] * 7,
         [ANY, VMEM],
-        [pltpu.VMEM((4, W, W), BF16), dma((20,))],
-        aliases=((6, 0),),
+        [pltpu.VMEM((4, W, W), BF16), dma((36,))],
     )
     return green_panel.reshape(ORDER, 1, W), green_diag.reshape(1, W, W)
 

time: 131 us -> 124 us (0.947)
  waiting for transfers between devices: 53.7 us -> 40.8 us
  starting transfers between devices: 39.4 us -> 48.4 us
  Pallas kernels: 33 us -> 31 us
    ppermute x15 -> x12, waiting for transfers between devices: 37.7 us -> 22.5 us  [ring_y(): return lax.ppermute(v, 'col', pairs)]
    ppermute x9, starting transfers between devices: 12.1 us -> 22.1 us  [ring_x(): return lax.ppermute(v, ('row', 'col'), pairs)]
    ppermute x6 -> x5, waiting for transfers between devices: 6.58 us -> 14.8 us  [over_y(): return lax.ppermute(v, 'col', [(c, (c + 2 * d) % 8) for c in range(8)])]
    ppermute x9, waiting for transfers between devices: 7.6 us -> 1.75 us  [ring_x(): return lax.ppermute(v, ('row', 'col'), pairs)]
    pallas_call x15 -> x18, Pallas kernels: 33 us -> 31 us  [call(): pl.pallas_call(kernel, out_shape=[jax.ShapeDtypeStruct(s, d) for s, d in...]
    ppermute x6 -> x5, starting transfers between devices: 9.55 us -> 8.42 us  [over_y(): return lax.ppermute(v, 'col', [(c, (c + 2 * d) % 8) for c in range(8)])]
    ppermute x15 -> x12, starting transfers between devices: 17 us -> 17.1 us  [ring_y(): return lax.ppermute(v, 'col', pairs)]
  transfers between devices with their start and end apart: 33 -> 29, of which waited for: 14 -> 11; matrix products, arithmetic and copies ran while one was open for 0% -> 0% of each run, Pallas kernels for 23% -> 19%
where the time goes in v1:
time: 124 us; the launch traced here: 123 us
  starting transfers between devices  48.4 us (39%)
  waiting for transfers between devices  40.8 us (33%)
  Pallas kernels  31 us (25%)
  local copies, waits for them, and re-layouts  2.14 us (2%)
    pallas_call x18, Pallas kernels, call(): pl.pallas_call(kernel, out_shape=[jax.ShapeDtypeStruct(s, d) for s, d in...  31 us
    ppermute x12, waiting for transfers between devices, ring_y(): return lax.ppermute(v, 'col', pairs)  22.5 us
    ppermute x9, starting transfers between devices, ring_x(): return lax.ppermute(v, ('row', 'col'), pairs)  22.1 us
    ppermute x12, starting transfers between devices, ring_y(): return lax.ppermute(v, 'col', pairs)  17.1 us
    ppermute x5, waiting for transfers between devices, over_y(): return lax.ppermute(v, 'col', [(c, (c + 2 * d) % 8) for c in range(8)])  14.8 us
    ppermute x5, starting transfers between devices, over_y(): return lax.ppermute(v, 'col', [(c, (c + 2 * d) % 8) for c in range(8)])  8.42 us
  transfers between devices with their start and end apart: 29, of which 11 were waited for; matrix products, arithmetic and copies ran while one was open for 0% of the time, Pallas kernels for 19%

profile of v1, /device:TPU:8, one launch (start us, length us, event | category | flops | bytes accessed | tf_op | source)
XLA Modules:
  0.0 123.5 jit_solution(4968458906139277005)
XLA Ops:
  3.0 2.6 %shard_map.59 = (bf16[4,192,128]{2,1,0:T(8,128)(2,1)S(1)}, bf16[4,192,128]{2,1,0:T(8,128)(2,1)S(1)}, bf16[3,4,192,128]{3,2,1,0:T(8,128)(2,1)S(1)}, bf16[3,4,192,128]{3,2,1,0:T(8,128)(2,1)S(1)}) custom-call(s32[4]{0:T(128)S(1)} %pad_add_fusion.place, s32[32,48]{1,0:T(8,128)S(1)} %bitcast.31, bf16[192,32,128]{2,1,0:T(8,128)(2,1)S(1)} %copy-done.1), custom_call_target="tpu_custom_call" | custom-call | bytes 1024 | tf_op jit(solution)/shard_map/pallas_call | solution.py:38
  8.8 2.3 %collective-permute-start.3 = (bf16[4,384,128]{2,1,0:T(8,128)(2,1)S(1)}, bf16[4,384,128]{2,1,0:T(8,128)(2,1)S(1)}, u32[]{:S(2)}, u32[]{:S(2)}) collective-permute-start(bf16[4,384,128]{2,1,0:T(8,128)(2,1)S(1)} %bitcast.24), channel_id=1, source_target_pairs={{0,6},{1,3},{2,0},{3,5},{4,2},{5,7},{6,4},{7,1},{8,14},{9,11},{10,... | collective-permute-start | bytes 1179656 | tf_op jit(solution)/shard_map/ppermute | solution.py:253
  12.0 2.7 %collective-permute-start.16 = (bf16[4,2,192,128]{3,2,1,0:T(8,128)(2,1)S(1)}, bf16[4,2,192,128]{3,2,1,0:T(8,128)(2,1)S(1)}, u32[]{:S(2)}, u32[]{:S(2)}) collective-permute-start(bf16[4,2,192,128]{3,2,1,0:T(8,128)(2,1)S(1)} %get-tuple-element.24), channel_id=1, source_target_pairs={{0,24},{1,9},{2,26},{3,11},{4,28},{5,13},{6,30},{7,15},{8,0},{9,17... | collective-permute-start | bytes 1179656 | tf_op jit(solution)/shard_map/ppermute | solution.py:257
  14.7 5.5 %collective-permute-done.3.first.rest_1_ = bf16[4,384,128]{2,1,0:T(8,128)(2,1)S(1)} collective-permute-done((bf16[4,384,128]{2,1,0:T(8,128)(2,1)S(1)}, bf16[4,384,128]{2,1,0:T(8,128)(2,1)S(1)}, u32[]{:S(2)}, u32[]{:S(2)}) %collective-permute-start.3) | collective-permute-done | bytes 393248 | tf_op jit(solution)/shard_map/ppermute | solution.py:253
  20.2 2.3 %collective-permute-start.14 = (bf16[4,384,128]{2,1,0:T(8,128)(2,1)S(1)}, bf16[4,384,128]{2,1,0:T(8,128)(2,1)S(1)}, u32[]{:S(2)}, u32[]{:S(2)}) collective-permute-start(bf16[4,384,128]{2,1,0:T(8,128)(2,1)S(1)} %collective-permute-done.3.first.rest_1_), channel_id=1, source_target_pairs={{0,6},{1,3},{2,0},{3,5},{4,2},{5,7},{6,4},{7,1},{8,14},{9,11},{10,... | collective-permute-start | bytes 1179656 | tf_op jit(solution)/shard_map/ppermute | solution.py:253
  25.0 3.7 %collective-permute-start.18 = (bf16[4,2,192,128]{3,2,1,0:T(8,128)(2,1)S(1)}, bf16[4,2,192,128]{3,2,1,0:T(8,128)(2,1)S(1)}, u32[]{:S(2)}, u32[]{:S(2)}) collective-permute-start(bf16[4,2,192,128]{3,2,1,0:T(8,128)(2,1)S(1)} %shard_map.66), channel_id=1, source_target_pairs={{0,16},{1,17},{2,18},{3,19},{4,20},{5,21},{6,22},{7,23},{8,24},{9,... | collective-permute-start | bytes 1179656 | tf_op jit(solution)/shard_map/ppermute | solution.py:257
  28.7 3.4 %collective-permute-done.14.rest_2_ = bf16[4,384,128]{2,1,0:T(8,128)(2,1)S(1)} collective-permute-done((bf16[4,384,128]{2,1,0:T(8,128)(2,1)S(1)}, bf16[4,384,128]{2,1,0:T(8,128)(2,1)S(1)}, u32[]{:S(2)}, u32[]{:S(2)}) %collective-permute-start.14) | collective-permute-done | bytes 393248 | tf_op jit(solution)/shard_map/ppermute | solution.py:253
  34.3 2.8 %collective-permute-start.17 = (bf16[4,768,128]{2,1,0:T(8,128)(2,1)S(1)}, bf16[4,768,128]{2,1,0:T(8,128)(2,1)S(1)}, u32[]{:S(2)}, u32[]{:S(2)}) collective-permute-start(bf16[4,768,128]{2,1,0:T(8,128)(2,1)S(1)} %shard_map.65.rest_7_), channel_id=1, source_target_pairs={{0,24},{1,9},{2,26},{3,11},{4,28},{5,13},{6,30},{7,15},{8,0},{9,17... | collective-permute-start | bytes 2359304 | tf_op jit(solution)/shard_map/ppermute | solution.py:257
  48.8 3.5 %collective-permute-done.13.rest_2_ = bf16[4,384,128]{2,1,0:T(8,128)(2,1)S(1)} collective-permute-done((bf16[4,384,128]{2,1,0:T(8,128)(2,1)S(1)}, bf16[4,384,128]{2,1,0:T(8,128)(2,1)S(1)}, u32[]{:S(2)}, u32[]{:S(2)}) %collective-permute-start.13) | collective-permute-done | bytes 393248 | tf_op jit(solution)/shard_map/ppermute | solution.py:253
  52.4 2.2 %shard_map.68 = bf16[4,768,128]{2,1,0:T(8,128)(2,1)S(1)} custom-call(s32[4]{0:T(128)S(1)} %pad_add_fusion.place, bf16[768,1536]{1,0:T(8,128)(2,1)S(1)} %bitcast.15, bf16[4,384,128]{2,1,0:T(8,128)(2,1)S(1)} %bitcast.19, bf16[4,384,128]{2,1,0:T(8,128)(2,1)S(1)} %collective-permute-done.5.first.rest_1_.rest_4_, ...), custom_call_target="tpu_custom_call" | custom-call | bytes 1024 | tf_op jit(solution)/shard_map/pallas_call | solution.py:38
  54.6 2.7 %collective-permute-start.19 = (bf16[4,768,128]{2,1,0:T(8,128)(2,1)S(1)}, bf16[4,768,128]{2,1,0:T(8,128)(2,1)S(1)}, u32[]{:S(2)}, u32[]{:S(2)}) collective-permute-start(bf16[4,768,128]{2,1,0:T(8,128)(2,1)S(1)} %shard_map.68), channel_id=1, source_target_pairs={{0,24},{1,9},{2,26},{3,11},{4,28},{5,13},{6,30},{7,15},{8,0},{9,17... | collective-permute-start | bytes 2359304 | tf_op jit(solution)/shard_map/ppermute | solution.py:257
  63.8 2.8 %collective-permute-start.9 = (bf16[4,384,128]{2,1,0:T(8,128)(2,1)S(1)}, bf16[4,384,128]{2,1,0:T(8,128)(2,1)S(1)}, u32[]{:S(2)}, u32[]{:S(2)}) collective-permute-start(bf16[4,384,128]{2,1,0:T(8,128)(2,1)S(1)} %shard_map.64), channel_id=1, source_target_pairs={{0,6},{1,3},{2,0},{3,5},{4,2},{5,7},{6,4},{7,1},{8,14},{9,11},{10,... | collective-permute-start | bytes 1179656 | tf_op jit(solution)/shard_map/ppermute | solution.py:253
  66.6 3.3 %collective-permute-done.12.rest_2_ = bf16[4,384,128]{2,1,0:T(8,128)(2,1)S(1)} collective-permute-done((bf16[4,384,128]{2,1,0:T(8,128)(2,1)S(1)}, bf16[4,384,128]{2,1,0:T(8,128)(2,1)S(1)}, u32[]{:S(2)}, u32[]{:S(2)}) %collective-permute-start.12) | collective-permute-done | bytes 393248 | tf_op jit(solution)/shard_map/ppermute | solution.py:253
  69.9 2.2 %shard_map.69 = bf16[4,768,128]{2,1,0:T(8,128)(2,1)S(1)} custom-call(s32[4]{0:T(128)S(1)} %pad_add_fusion.place, bf16[768,1536]{1,0:T(8,128)(2,1)S(1)} %bitcast.16, bf16[4,384,128]{2,1,0:T(8,128)(2,1)S(1)} %bitcast.29, bf16[4,384,128]{2,1,0:T(8,128)(2,1)S(1)} %collective-permute-done.7.first.rest_1_.rest_5_, ...), custom_call_target="tpu_custom_call" | custom-call | bytes 1024 | tf_op jit(solution)/shard_map/pallas_call | solution.py:38
  72.1 2.9 %collective-permute-start.20 = (bf16[4,768,128]{2,1,0:T(8,128)(2,1)S(1)}, bf16[4,768,128]{2,1,0:T(8,128)(2,1)S(1)}, u32[]{:S(2)}, u32[]{:S(2)}) collective-permute-start(bf16[4,768,128]{2,1,0:T(8,128)(2,1)S(1)} %shard_map.69), channel_id=1, source_target_pairs={{0,24},{1,9},{2,26},{3,11},{4,28},{5,13},{6,30},{7,15},{8,0},{9,17... | collective-permute-start | bytes 2359304 | tf_op jit(solution)/shard_map/ppermute | solution.py:257
  77.4 3.8 %collective-permute-start.25 = (bf16[4,768,128]{2,1,0:T(8,128)(2,1)S(1)}, bf16[4,768,128]{2,1,0:T(8,128)(2,1)S(1)}, u32[]{:S(2)}, u32[]{:S(2)}) collective-permute-start(bf16[4,768,128]{2,1,0:T(8,128)(2,1)S(1)} %shard_map.73), channel_id=1, source_target_pairs={{0,24},{1,9},{2,26},{3,11},{4,28},{5,13},{6,30},{7,15},{8,0},{9,17... | collective-permute-start | bytes 2359304 | tf_op jit(solution)/shard_map/ppermute | solution.py:257
  82.5 6.8 %collective-permute-done.10.rest_2_ = bf16[4,384,128]{2,1,0:T(8,128)(2,1)S(1)} collective-permute-done((bf16[4,384,128]{2,1,0:T(8,128)(2,1)S(1)}, bf16[4,384,128]{2,1,0:T(8,128)(2,1)S(1)}, u32[]{:S(2)}, u32[]{:S(2)}) %collective-permute-start.10) | collective-permute-done | bytes 393248 | tf_op jit(solution)/shard_map/ppermute | solution.py:253
  89.3 2.5 %shard_map.70 = (bf16[768,128]{1,0:T(8,128)(2,1)S(1)}, bf16[768,128]{1,0:T(8,128)(2,1)S(1)}, bf16[768,128]{1,0:T(8,128)(2,1)S(1)}, bf16[768,128]{1,0:T(8,128)(2,1)S(1)}) custom-call(s32[4]{0:T(128)S(1)} %pad_add_fusion.place, s32[32,48]{1,0:T(8,128)S(1)} %bitcast.32, bf16[768,1536]{1,0:T(8,128)(2,1)S(1)} %bitcast.17, bf16[4,384,128]{2,1,0:T(8,128)(2,1)S(1)} %bitcast.22, ...), custom_call_target="tpu_custom_call" | custom-call | bytes 1024 | tf_op jit(solution)/shard_map/pallas_call | solution.py:38
  95.5 2.6 %collective-permute-done.21.rest_8_.rest_1_ = bf16[768,128]{1,0:T(8,128)(2,1)S(1)} collective-permute-done((bf16[768,128]{1,0:T(8,128)(2,1)S(1)}, bf16[768,128]{1,0:T(8,128)(2,1)S(1)}, u32[]{:S(2)}, u32[]{:S(2)}) %collective-permute-start.21) | collective-permute-done | bytes 196640 | tf_op jit(solution)/shard_map/ppermute | solution.py:249
  98.1 3.5 %collective-permute-done.22.rest_9_.rest_2_ = bf16[768,128]{1,0:T(8,128)(2,1)S(1)} collective-permute-done((bf16[768,128]{1,0:T(8,128)(2,1)S(1)}, bf16[768,128]{1,0:T(8,128)(2,1)S(1)}, u32[]{:S(2)}, u32[]{:S(2)}) %collective-permute-start.22) | collective-permute-done | bytes 196640 | tf_op jit(solution)/shard_map/ppermute | solution.py:249
  101.7 4.6 %shard_map.75 = (bf16[896,128]{1,0:T(8,128)(2,1)S(1)}, bf16[896,128]{1,0:T(8,128)(2,1)S(1)}, bf16[1664,128]{1,0:T(8,128)(2,1)S(1)}, bf16[896,128]{1,0:T(8,128)(2,1)S(1)}) custom-call(s32[4]{0:T(128)S(1)} %pad_add_fusion.place, s32[32,48]{1,0:T(8,128)S(1)} %bitcast.33, bf16[768,1536]{1,0:T(8,128)(2,1)S(1)} %collective-permute-done.2.after.green, ...), custom_call_target="tpu_custom_call" | custom-call | bytes 1024 | tf_op jit(solution)/shard_map/pallas_call | solution.py:38
  106.2 2.7 %collective-permute-start.27 = (bf16[1664,128]{1,0:T(8,128)(2,1)S(1)}, bf16[1664,128]{1,0:T(8,128)(2,1)S(1)}, u32[]{:S(2)}, u32[]{:S(2)}) collective-permute-start(bf16[1664,128]{1,0:T(8,128)(2,1)S(1)} %get-tuple-element.32), channel_id=1, source_target_pairs={{0,4},{1,5},{2,6},{3,7},{4,0},{5,1},{6,2},{7,3},{8,12},{9,13},{10,... | collective-permute-start | bytes 1277960 | tf_op jit(solution)/shard_map/ppermute | solution.py:249
  111.9 8.6 %collective-permute-done.26.rest_4_ = bf16[896,128]{1,0:T(8,128)(2,1)S(1)} collective-permute-done((bf16[896,128]{1,0:T(8,128)(2,1)S(1)}, bf16[896,128]{1,0:T(8,128)(2,1)S(1)}, u32[]{:S(2)}, u32[]{:S(2)}) %collective-permute-start.26) | collective-permute-done | bytes 229408 | tf_op jit(solution)/shard_map/ppermute | solution.py:249
  120.5 2.8 %shard_map.76 = (bf16[4,8,192,128]{3,2,1,0:T(8,128)(2,1)}, f32[128,128]{1,0:T(8,128)}) custom-call(s32[4]{0:T(128)S(1)} %pad_add_fusion.place, f32[128,128]{1,0:T(8,128)S(1)} %bitcast.34, bf16[768,128]{1,0:T(8,128)(2,1)S(1)} %get-tuple-element.26.rest_0_, bf16[768,128]{1,0:T(8,128)(2,1)S(1)} %collective-permute-done.21.rest_8_.rest_1_, ...), custom_call_target="tpu_custom_call" | custom-call | bytes 1024 | tf_op jit(solution)/shard_map/pallas_call | solution.py:38
  (63 shorter events, 39.7 us)
Async XLA Ops:
  8.8 11.4 %collective-permute-start.3 = (bf16[4,384,128]{2,1,0:T(8,128)(2,1)S(1)}, bf16[4,384,128]{2,1,0:T(8,128)(2,1)S(1)}, u32[]{:S(2)}, u32[]{:S(2)}) collective-permute-start(bf16[4,384,128]{2,1,0:T(8,128)(2,1)S(1)} %bitcast.24), channel_id=1, source_target_pairs={{0,6},{1,3},{2,0},{3,5},{4,2},{5,7},{6,4},{7,1},{8,14},{9,11},{10,... | collective-permute-start | bytes 1179656 | tf_op jit(solution)/shard_map/ppermute | solution.py:253
  11.0 11.5 %collective-permute-start.4 = (bf16[4,384,128]{2,1,0:T(8,128)(2,1)S(1)}, bf16[4,384,128]{2,1,0:T(8,128)(2,1)S(1)}, u32[]{:S(2)}, u32[]{:S(2)}) collective-permute-start(bf16[4,384,128]{2,1,0:T(8,128)(2,1)S(1)} %bitcast.25), channel_id=1, source_target_pairs={{0,2},{1,7},{2,4},{3,1},{4,6},{5,3},{6,0},{7,5},{8,10},{9,15},{10,... | collective-permute-start | bytes 1179656 | tf_op jit(solution)/shard_map/ppermute | solution.py:253
  12.0 12.8 %collective-permute-start.16 = (bf16[4,2,192,128]{3,2,1,0:T(8,128)(2,1)S(1)}, bf16[4,2,192,128]{3,2,1,0:T(8,128)(2,1)S(1)}, u32[]{:S(2)}, u32[]{:S(2)}) collective-permute-start(bf16[4,2,192,128]{3,2,1,0:T(8,128)(2,1)S(1)} %get-tuple-element.24), channel_id=1, source_target_pairs={{0,24},{1,9},{2,26},{3,11},{4,28},{5,13},{6,30},{7,15},{8,0},{9,17... | collective-permute-start | bytes 1179656 | tf_op jit(solution)/shard_map/ppermute | solution.py:257
  14.7 10.1 %collective-permute-start.15 = (bf16[4,2,192,128]{3,2,1,0:T(8,128)(2,1)S(1)}, bf16[4,2,192,128]{3,2,1,0:T(8,128)(2,1)S(1)}, u32[]{:S(2)}, u32[]{:S(2)}) collective-permute-start(bf16[4,2,192,128]{3,2,1,0:T(8,128)(2,1)S(1)} %shard_map.60.after), channel_id=1, source_target_pairs={{0,8},{1,25},{2,10},{3,27},{4,12},{5,29},{6,14},{7,31},{8,16},{9,1... | collective-permute-start | bytes 1179656 | tf_op jit(solution)/shard_map/ppermute | solution.py:257
  20.2 11.9 %collective-permute-start.14 = (bf16[4,384,128]{2,1,0:T(8,128)(2,1)S(1)}, bf16[4,384,128]{2,1,0:T(8,128)(2,1)S(1)}, u32[]{:S(2)}, u32[]{:S(2)}) collective-permute-start(bf16[4,384,128]{2,1,0:T(8,128)(2,1)S(1)} %collective-permute-done.3.first.rest_1_), channel_id=1, source_target_pairs={{0,6},{1,3},{2,0},{3,5},{4,2},{5,7},{6,4},{7,1},{8,14},{9,11},{10,... | collective-permute-start | bytes 1179656 | tf_op jit(solution)/shard_map/ppermute | solution.py:253
  22.7 14.4 %collective-permute-start.6 = (bf16[4,384,128]{2,1,0:T(8,128)(2,1)S(1)}, bf16[4,384,128]{2,1,0:T(8,128)(2,1)S(1)}, u32[]{:S(2)}, u32[]{:S(2)}) collective-permute-start(bf16[4,384,128]{2,1,0:T(8,128)(2,1)S(1)} %shard_map.62), channel_id=1, source_target_pairs={{0,2},{1,7},{2,4},{3,1},{4,6},{5,3},{6,0},{7,5},{8,10},{9,15},{10,... | collective-permute-start | bytes 1179656 | tf_op jit(solution)/shard_map/ppermute | solution.py:253
  22.8 14.4 %collective-permute-start.5 = (bf16[4,384,128]{2,1,0:T(8,128)(2,1)S(1)}, bf16[4,384,128]{2,1,0:T(8,128)(2,1)S(1)}, u32[]{:S(2)}, u32[]{:S(2)}) collective-permute-start(bf16[4,384,128]{2,1,0:T(8,128)(2,1)S(1)} %shard_map.62), channel_id=1, source_target_pairs={{0,6},{1,3},{2,0},{3,5},{4,2},{5,7},{6,4},{7,1},{8,14},{9,11},{10,... | collective-permute-start | bytes 1179656 | tf_op jit(solution)/shard_map/ppermute | solution.py:253
  25.0 13.7 %collective-permute-start.18 = (bf16[4,2,192,128]{3,2,1,0:T(8,128)(2,1)S(1)}, bf16[4,2,192,128]{3,2,1,0:T(8,128)(2,1)S(1)}, u32[]{:S(2)}, u32[]{:S(2)}) collective-permute-start(bf16[4,2,192,128]{3,2,1,0:T(8,128)(2,1)S(1)} %shard_map.66), channel_id=1, source_target_pairs={{0,16},{1,17},{2,18},{3,19},{4,20},{5,21},{6,22},{7,23},{8,24},{9,... | collective-permute-start | bytes 1179656 | tf_op jit(solution)/shard_map/ppermute | solution.py:257
  34.3 18.1 %collective-permute-start.17 = (bf16[4,768,128]{2,1,0:T(8,128)(2,1)S(1)}, bf16[4,768,128]{2,1,0:T(8,128)(2,1)S(1)}, u32[]{:S(2)}, u32[]{:S(2)}) collective-permute-start(bf16[4,768,128]{2,1,0:T(8,128)(2,1)S(1)} %shard_map.65.rest_7_), channel_id=1, source_target_pairs={{0,24},{1,9},{2,26},{3,11},{4,28},{5,13},{6,30},{7,15},{8,0},{9,17... | collective-permute-start | bytes 2359304 | tf_op jit(solution)/shard_map/ppermute | solution.py:257
  41.0 16.3 %collective-permute-start.23 = (bf16[4,768,128]{2,1,0:T(8,128)(2,1)S(1)}, bf16[4,768,128]{2,1,0:T(8,128)(2,1)S(1)}, u32[]{:S(2)}, u32[]{:S(2)}) collective-permute-start(bf16[4,768,128]{2,1,0:T(8,128)(2,1)S(1)} %shard_map.71), channel_id=1, source_target_pairs={{0,24},{1,9},{2,26},{3,11},{4,28},{5,13},{6,30},{7,15},{8,0},{9,17... | collective-permute-start | bytes 2359304 | tf_op jit(solution)/shard_map/ppermute | solution.py:257
  42.5 9.8 %collective-permute-start.13 = (bf16[4,384,128]{2,1,0:T(8,128)(2,1)S(1)}, bf16[4,384,128]{2,1,0:T(8,128)(2,1)S(1)}, u32[]{:S(2)}, u32[]{:S(2)}) collective-permute-start(bf16[4,384,128]{2,1,0:T(8,128)(2,1)S(1)} %collective-permute-done.5.first.rest_1_.rest_4_), channel_id=1, source_target_pairs={{0,6},{1,3},{2,0},{3,5},{4,2},{5,7},{6,4},{7,1},{8,14},{9,11},{10,... | collective-permute-start | bytes 1179656 | tf_op jit(solution)/shard_map/ppermute | solution.py:253
  44.7 12.6 %collective-permute-start.8 = (bf16[4,384,128]{2,1,0:T(8,128)(2,1)S(1)}, bf16[4,384,128]{2,1,0:T(8,128)(2,1)S(1)}, u32[]{:S(2)}, u32[]{:S(2)}) collective-permute-start(bf16[4,384,128]{2,1,0:T(8,128)(2,1)S(1)} %shard_map.63), channel_id=1, source_target_pairs={{0,2},{1,7},{2,4},{3,1},{4,6},{5,3},{6,0},{7,5},{8,10},{9,15},{10,... | collective-permute-start | bytes 1179656 | tf_op jit(solution)/shard_map/ppermute | solution.py:253
  44.8 12.4 %collective-permute-start.7 = (bf16[4,384,128]{2,1,0:T(8,128)(2,1)S(1)}, bf16[4,384,128]{2,1,0:T(8,128)(2,1)S(1)}, u32[]{:S(2)}, u32[]{:S(2)}) collective-permute-start(bf16[4,384,128]{2,1,0:T(8,128)(2,1)S(1)} %shard_map.63), channel_id=1, source_target_pairs={{0,6},{1,3},{2,0},{3,5},{4,2},{5,7},{6,4},{7,1},{8,14},{9,11},{10,... | collective-permute-start | bytes 1179656 | tf_op jit(solution)/shard_map/ppermute | solution.py:253
  54.6 15.3 %collective-permute-start.19 = (bf16[4,768,128]{2,1,0:T(8,128)(2,1)S(1)}, bf16[4,768,128]{2,1,0:T(8,128)(2,1)S(1)}, u32[]{:S(2)}, u32[]{:S(2)}) collective-permute-start(bf16[4,768,128]{2,1,0:T(8,128)(2,1)S(1)} %shard_map.68), channel_id=1, source_target_pairs={{0,24},{1,9},{2,26},{3,11},{4,28},{5,13},{6,30},{7,15},{8,0},{9,17... | collective-permute-start | bytes 2359304 | tf_op jit(solution)/shard_map/ppermute | solution.py:257
  59.5 15.7 %collective-permute-start.24 = (bf16[4,768,128]{2,1,0:T(8,128)(2,1)S(1)}, bf16[4,768,128]{2,1,0:T(8,128)(2,1)S(1)}, u32[]{:S(2)}, u32[]{:S(2)}) collective-permute-start(bf16[4,768,128]{2,1,0:T(8,128)(2,1)S(1)} %shard_map.72), channel_id=1, source_target_pairs={{0,24},{1,9},{2,26},{3,11},{4,28},{5,13},{6,30},{7,15},{8,0},{9,17... | collective-permute-start | bytes 2359304 | tf_op jit(solution)/shard_map/ppermute | solution.py:257
  61.5 8.4 %collective-permute-start.12 = (bf16[4,384,128]{2,1,0:T(8,128)(2,1)S(1)}, bf16[4,384,128]{2,1,0:T(8,128)(2,1)S(1)}, u32[]{:S(2)}, u32[]{:S(2)}) collective-permute-start(bf16[4,384,128]{2,1,0:T(8,128)(2,1)S(1)} %collective-permute-done.7.first.rest_1_.rest_5_), channel_id=1, source_target_pairs={{0,6},{1,3},{2,0},{3,5},{4,2},{5,7},{6,4},{7,1},{8,14},{9,11},{10,... | collective-permute-start | bytes 1179656 | tf_op jit(solution)/shard_map/ppermute | solution.py:253
  63.0 12.1 %collective-permute-start.11 = (bf16[4,384,128]{2,1,0:T(8,128)(2,1)S(1)}, bf16[4,384,128]{2,1,0:T(8,128)(2,1)S(1)}, u32[]{:S(2)}, u32[]{:S(2)}) collective-permute-start(bf16[4,384,128]{2,1,0:T(8,128)(2,1)S(1)} %shard_map.64), channel_id=1, source_target_pairs={{0,2},{1,7},{2,4},{3,1},{4,6},{5,3},{6,0},{7,5},{8,10},{9,15},{10,... | collective-permute-start | bytes 1179656 | tf_op jit(solution)/shard_map/ppermute | solution.py:253
  63.8 11.3 %collective-permute-start.9 = (bf16[4,384,128]{2,1,0:T(8,128)(2,1)S(1)}, bf16[4,384,128]{2,1,0:T(8,128)(2,1)S(1)}, u32[]{:S(2)}, u32[]{:S(2)}) collective-permute-start(bf16[4,384,128]{2,1,0:T(8,128)(2,1)S(1)} %shard_map.64), channel_id=1, source_target_pairs={{0,6},{1,3},{2,0},{3,5},{4,2},{5,7},{6,4},{7,1},{8,14},{9,11},{10,... | collective-permute-start | bytes 1179656 | tf_op jit(solution)/shard_map/ppermute | solution.py:253
  72.1 17.2 %collective-permute-start.20 = (bf16[4,768,128]{2,1,0:T(8,128)(2,1)S(1)}, bf16[4,768,128]{2,1,0:T(8,128)(2,1)S(1)}, u32[]{:S(2)}, u32[]{:S(2)}) collective-permute-start(bf16[4,768,128]{2,1,0:T(8,128)(2,1)S(1)} %shard_map.69), channel_id=1, source_target_pairs={{0,24},{1,9},{2,26},{3,11},{4,28},{5,13},{6,30},{7,15},{8,0},{9,17... | collective-permute-start | bytes 2359304 | tf_op jit(solution)/shard_map/ppermute | solution.py:257
  77.4 18.1 %collective-permute-start.25 = (bf16[4,768,128]{2,1,0:T(8,128)(2,1)S(1)}, bf16[4,768,128]{2,1,0:T(8,128)(2,1)S(1)}, u32[]{:S(2)}, u32[]{:S(2)}) collective-permute-start(bf16[4,768,128]{2,1,0:T(8,128)(2,1)S(1)} %shard_map.73), channel_id=1, source_target_pairs={{0,24},{1,9},{2,26},{3,11},{4,28},{5,13},{6,30},{7,15},{8,0},{9,17... | collective-permute-start | bytes 2359304 | tf_op jit(solution)/shard_map/ppermute | solution.py:257
  81.2 8.1 %collective-permute-start.10 = (bf16[4,384,128]{2,1,0:T(8,128)(2,1)S(1)}, bf16[4,384,128]{2,1,0:T(8,128)(2,1)S(1)}, u32[]{:S(2)}, u32[]{:S(2)}) collective-permute-start(bf16[4,384,128]{2,1,0:T(8,128)(2,1)S(1)} %collective-permute-done.9.rest_1_.rest_5_), channel_id=1, source_target_pairs={{0,6},{1,3},{2,0},{3,5},{4,2},{5,7},{6,4},{7,1},{8,14},{9,11},{10,... | collective-permute-start | bytes 1179656 | tf_op jit(solution)/shard_map/ppermute | solution.py:253
  106.2 14.3 %collective-permute-start.27 = (bf16[1664,128]{1,0:T(8,128)(2,1)S(1)}, bf16[1664,128]{1,0:T(8,128)(2,1)S(1)}, u32[]{:S(2)}, u32[]{:S(2)}) collective-permute-start(bf16[1664,128]{1,0:T(8,128)(2,1)S(1)} %get-tuple-element.32), channel_id=1, source_target_pairs={{0,4},{1,5},{2,6},{3,7},{4,0},{5,1},{6,2},{7,3},{8,12},{9,13},{10,... | collective-permute-start | bytes 1277960 | tf_op jit(solution)/shard_map/ppermute | solution.py:249
  108.9 11.6 %collective-permute-start.26 = (bf16[896,128]{1,0:T(8,128)(2,1)S(1)}, bf16[896,128]{1,0:T(8,128)(2,1)S(1)}, u32[]{:S(2)}, u32[]{:S(2)}) collective-permute-start(bf16[896,128]{1,0:T(8,128)(2,1)S(1)} %get-tuple-element.31), channel_id=1, source_target_pairs={{0,2},{1,3},{2,4},{3,5},{4,6},{5,7},{6,0},{7,1},{8,10},{9,11},{10,... | collective-permute-start | bytes 688136 | tf_op jit(solution)/shard_map/ppermute | solution.py:249
  109.9 10.6 %collective-permute-start.28 = (bf16[896,128]{1,0:T(8,128)(2,1)S(1)}, bf16[896,128]{1,0:T(8,128)(2,1)S(1)}, u32[]{:S(2)}, u32[]{:S(2)}) collective-permute-start(bf16[896,128]{1,0:T(8,128)(2,1)S(1)} %get-tuple-element.33), channel_id=1, source_target_pairs={{0,6},{1,7},{2,0},{3,1},{4,2},{5,3},{6,4},{7,5},{8,14},{9,15},{10,... | collective-permute-start | bytes 688136 | tf_op jit(solution)/shard_map/ppermute | solution.py:249
  (10 other events, 83.0 us)

commit v2 on v1

--- a/solution.py
+++ b/solution.py
@@ -109,26 +109,39 @@
     run_copies(copies)
 
 
-def after_kernel(value, first, second, out, sems):
+def after_kernel(value, *rest):
+    out, sems = rest[-2:]
     run_copies([pltpu.make_async_copy(value, out, sems.at[0])])
 
 
-def load_panel(place, pieces, panel, sems):
+def turn_kernel(place, own, sib, own_out, sib_out, sems):
     y, k = place[1], place[2]
     copies = []
-    for hop, source in enumerate(pieces):
-        rows = pl.ds(pl.multiple_of(along(y, 4 - hop, k) * CH, CH), CH)
-        copies.append(pltpu.make_async_copy(source, panel.at[:, rows, :], sems.at[hop]))
+    for source, target in ((own, own_out), (sib, sib_out)):
+        for hop in range(NY):
+            columns = pl.ds(pl.multiple_of(along(y, 4 - hop, k) * CH, CH), CH)
+            copies.append(
+                pltpu.make_async_copy(
+                    source.at[:, columns],
+                    target.at[:, hop * CH : (hop + 1) * CH],
+                    sems.at[len(copies)],
+                )
+            )
     run_copies(copies)
 
 
-def product_kernel(summed, place, green, *rest):
+def multiply(green, pieces, first, second):
+    both = jnp.concatenate(
+        [jnp.concatenate([p[first], p[second]], axis=1) for p in pieces], axis=0
+    )
+    return jnp.dot(green[...], both, preferred_element_type=F32)
+
+
+def product_kernel(summed, green, *rest):
     pieces, rest = rest[:4], rest[4:]
-    acc, (out, panel, sems) = rest[:summed], rest[-3:]
-    load_panel(place, pieces, panel, sems)
+    acc, out = rest[:summed], rest[-1]
     for h in range(2):
-        both = jnp.concatenate([panel[2 * h], panel[2 * h + 1]], axis=1)
-        value = jnp.dot(green[...], both, preferred_element_type=F32)
+        value = multiply(green, pieces, 2 * h, 2 * h + 1)
         for i in range(2):
             part = value[:, i * W : (i + 1) * W]
             if summed:
@@ -136,14 +149,13 @@
             out[2 * h + i] = part.astype(BF16)
 
 
-def product(place, green, pieces, acc, after=()):
+def product(green, pieces, acc, after=()):
     (out,) = call(
         functools.partial(product_kernel, len(acc)),
         [((NY, HALF, W), BF16)],
-        (place, green, *pieces, *acc, *after),
-        [SMEM, VMEM] + [ANY] * 4 + [VMEM] * len(acc) + [ANY] * len(after),
+        (green, *pieces, *acc, *after),
+        [VMEM] * (5 + len(acc)) + [ANY] * len(after),
         [VMEM],
-        [pltpu.VMEM((NY, SPAN, W), BF16), pltpu.SemaphoreType.DMA((4,))],
     )
     return out
 
@@ -152,17 +164,15 @@
     pieces, acc, rest = rest[:4], rest[4], rest[5:]
     if half:
         columns_t, terms, opposite, rest = rest[0], rest[1], rest[2], rest[5:]
-    outs, (panel, sems, *own) = rest[:4], rest[4:]
+    outs, own = rest[:4], rest[4:]
     r, y, k = place[0], place[1], place[2]
     if half:
         first = pltpu.make_async_copy(opposite, outs[2].at[HALF + W :], own[0].at[0])
         first.start()
-    load_panel(place, pieces, panel, sems)
     c = y * 2 + (k if half == 0 else 1 - k)
     for h in range(2):
         order = [lax.rem(y + 2 * h + i, 4) for i in range(2)]
-        both = jnp.concatenate([panel[order[0]], panel[order[1]]], axis=1)
-        value = jnp.dot(green[...], both, preferred_element_type=F32)
+        value = multiply(green, pieces, *order)
         for i, q in enumerate(order):
             number = r * 8 + q * 2 + k
             out = outs[2 * h + i]
@@ -173,9 +183,15 @@
                     rows = slice(start, start + 64)
                     part = value[rows, i * W : (i + 1) * W] + acc[q, rows, :].astype(F32)
                     out[rows, :] = (part * keep).astype(BF16)
-            if half:
-                term = jnp.dot(columns_t[1, q], out[0:HALF, :], preferred_element_type=F32)
-                out[HALF : HALF + W, :] = (terms[2 * h + i] - term).astype(BF16)
+        if half:
+            left = jnp.concatenate([columns_t[1, q] for q in order], axis=0)
+            right = jnp.concatenate([outs[2 * h + i][0:HALF, :] for i in range(2)], axis=1)
+            term = jnp.dot(left, right, preferred_element_type=F32)
+            for i in range(2):
+                block = slice(i * W, (i + 1) * W)
+                outs[2 * h + i][HALF : HALF + W, :] = (
+                    terms[2 * h + i] - term[block, block]
+                ).astype(BF16)
     if half:
         first.wait()
 
@@ -203,7 +219,7 @@
 
 
 def final_kernel(place, pivot, *rest):
-    parts, (panel, diag, terms, sems) = rest[:7], rest[7:]
+    parts, (panel, diag, sems) = rest[:7], rest[7:]
     y, k = place[1], place[2]
     sources = [
         (parts[0], 0, 0, 0),
@@ -215,22 +231,17 @@
         (parts[5], 0, 1, 2),
         (parts[6], 0, 1, 3),
     ]
-    copies, last = [], []
+    copies = []
     for source, start, half, d in sources:
         c = lax.rem(y + 4 - d, 4) * 2 + (k if half == 0 else 1 - k)
         for j in range(NR):
             rows = source.at[start + j * RD : start + (j + 1) * RD]
             copies.append(pltpu.make_async_copy(rows, panel.at[j, c], sems.at[len(copies)]))
-        if half:
-            rows = source.at[HALF : HALF + W]
-            last.append(pltpu.make_async_copy(rows, terms.at[d], sems.at[NR * NC + d]))
-    for copy in last + copies:
+    for copy in copies:
         copy.start()
-    for copy in last:
-        copy.wait()
     total = pivot[...]
-    for d in range(4):
-        total += terms[d].astype(F32)
+    for source in parts[3:]:
+        total += source[HALF : HALF + W, :].astype(F32)
     diag[...] = total
     for copy in copies:
         copy.wait()
@@ -291,11 +302,19 @@
         )
     )
     columns = [ring_x(chunks[0], 3), None, ring_x(chunks[2], 1), chunks[3]]
+    turned = call(
+        turn_kernel,
+        [((HALF, SPAN), BF16)] * 2,
+        (place, *greens),
+        [SMEM, ANY, ANY],
+        [ANY] * 2,
+        [dma((8,))],
+    )
     (sent,) = call(
         after_kernel,
         [chunk],
-        (chunks[1], columns[0], columns[2]),
-        [ANY] * 3,
+        (chunks[1], columns[0], columns[2], *turned),
+        [ANY] * 5,
         [ANY],
         [dma((1,))],
     )
@@ -338,7 +357,7 @@
             after = before[s, half]
             if s == 0 and half:
                 after += (out,)
-            out = product(place, greens[half], pieces[s], acc[half], after)
+            out = product(turned[half], pieces[s], acc[half], after)
             acc[half] = (ring_x(out),)
     parts, terms, last_after = [], (), ()
     for half in range(2):
@@ -347,13 +366,12 @@
         outs = call(
             functools.partial(last_kernel, half),
             [((n, W), BF16) for n in rows],
-            (place, pattern, greens[half], *pieces[3], *acc[half], *terms, *last_after),
+            (place, pattern, turned[half], *pieces[3], *acc[half], *terms, *last_after),
             [SMEM, SMEM, VMEM]
-            + [ANY] * 4
-            + [VMEM] * (1 + len(terms))
+            + [VMEM] * (5 + len(terms))
             + [ANY] * len(last_after),
             [VMEM] * 4,
-            [pltpu.VMEM((NY, SPAN, W), BF16), dma((4,))] + [dma((1,))] * half,
+            [dma((1,))] * half,
         )
         parts.append(outs[0])
         for d in (1, 2, 3) if half else (1, 3):
@@ -372,9 +390,9 @@
         final_kernel,
         [((NR, NC, RD, W), BF16), ((W, W), F32)],
         (place, pivot_inverse.reshape(W, W), *parts),
-        [SMEM, VMEM] + [ANY] * 7,
+        [SMEM, VMEM] + [ANY] * 3 + [VMEM] * 4,
         [ANY, VMEM],
-        [pltpu.VMEM((4, W, W), BF16), dma((36,))],
+        [dma((32,))],
     )
     return green_panel.reshape(ORDER, 1, W), green_diag.reshape(1, W, W)
 

time: 124 us -> 118 us (0.952)
  Pallas kernels: 31 us -> 26.2 us
  waiting for transfers between devices: 40.8 us -> 37.1 us
  starting transfers between devices: 48.4 us -> 49.9 us
    pallas_call x18 -> x19, Pallas kernels: 31 us -> 26.2 us  [call(): pl.pallas_call(kernel, out_shape=[jax.ShapeDtypeStruct(s, d) for s, d in...]
    ppermute x5, waiting for transfers between devices: 14.8 us -> 11.7 us  [over_y(): return lax.ppermute(v, 'col', [(c, (c + 2 * d) % 8) for c in range(8)])]
    ppermute x12, waiting for transfers between devices: 22.5 us -> 19.8 us  [ring_y(): return lax.ppermute(v, 'col', pairs)]
    ppermute x12, starting transfers between devices: 17.1 us -> 19.3 us  [ring_y(): return lax.ppermute(v, 'col', pairs)]
    ppermute x9, waiting for transfers between devices: 1.75 us -> 3.73 us  [ring_x(): return lax.ppermute(v, ('row', 'col'), pairs)]
  transfers between devices with their start and end apart: 29 -> 29, of which waited for: 11 -> 12; matrix products, arithmetic and copies ran while one was open for 0% -> 0% of each run, Pallas kernels for 19% -> 17%
where the time goes in v2:
time: 118 us; the launch traced here: 116 us
  starting transfers between devices  49.9 us (42%)
  waiting for transfers between devices  37.1 us (31%)
  Pallas kernels  26.2 us (22%)
  local copies, waits for them, and re-layouts  2.14 us (2%)
    pallas_call x19, Pallas kernels, call(): pl.pallas_call(kernel, out_shape=[jax.ShapeDtypeStruct(s, d) for s, d in...  26.2 us
    ppermute x9, starting transfers between devices, ring_x(): return lax.ppermute(v, ('row', 'col'), pairs)  21.7 us
    ppermute x12, waiting for transfers between devices, ring_y(): return lax.ppermute(v, 'col', pairs)  19.8 us
    ppermute x12, starting transfers between devices, ring_y(): return lax.ppermute(v, 'col', pairs)  19.3 us
    ppermute x5, waiting for transfers between devices, over_y(): return lax.ppermute(v, 'col', [(c, (c + 2 * d) % 8) for c in range(8)])  11.7 us
    ppermute x5, starting transfers between devices, over_y(): return lax.ppermute(v, 'col', [(c, (c + 2 * d) % 8) for c in range(8)])  8.2 us
    ppermute x9, waiting for transfers between devices, ring_x(): return lax.ppermute(v, ('row', 'col'), pairs)  3.73 us
  transfers between devices with their start and end apart: 29, of which 12 were waited for; matrix products, arithmetic and copies ran while one was open for 0% of the time, Pallas kernels for 17%

profile of v2, /device:TPU:8, one launch (start us, length us, event | category | flops | bytes accessed | tf_op | source)
XLA Modules:
  0.0 116.4 jit_solution(17045919671348764556)
XLA Ops:
  3.0 2.6 %shard_map.60 = (bf16[4,192,128]{2,1,0:T(8,128)(2,1)S(1)}, bf16[4,192,128]{2,1,0:T(8,128)(2,1)S(1)}, bf16[3,4,192,128]{3,2,1,0:T(8,128)(2,1)S(1)}, bf16[3,4,192,128]{3,2,1,0:T(8,128)(2,1)S(1)}) custom-call(s32[4]{0:T(128)S(1)} %pad_add_fusion.place, s32[32,48]{1,0:T(8,128)S(1)} %bitcast.28, bf16[192,32,128]{2,1,0:T(8,128)(2,1)S(1)} %copy-done.1), custom_call_target="tpu_custom_call" | custom-call | bytes 1024 | tf_op jit(solution)/shard_map/pallas_call | solution.py:38
  8.8 2.3 %collective-permute-start.3 = (bf16[4,384,128]{2,1,0:T(8,128)(2,1)S(1)}, bf16[4,384,128]{2,1,0:T(8,128)(2,1)S(1)}, u32[]{:S(2)}, u32[]{:S(2)}) collective-permute-start(bf16[4,384,128]{2,1,0:T(8,128)(2,1)S(1)} %bitcast.19), channel_id=1, source_target_pairs={{0,6},{1,3},{2,0},{3,5},{4,2},{5,7},{6,4},{7,1},{8,14},{9,11},{10,... | collective-permute-start | bytes 1179656 | tf_op jit(solution)/shard_map/ppermute | solution.py:264
  12.0 2.7 %collective-permute-start.16 = (bf16[4,2,192,128]{3,2,1,0:T(8,128)(2,1)S(1)}, bf16[4,2,192,128]{3,2,1,0:T(8,128)(2,1)S(1)}, u32[]{:S(2)}, u32[]{:S(2)}) collective-permute-start(bf16[4,2,192,128]{3,2,1,0:T(8,128)(2,1)S(1)} %get-tuple-element.27), channel_id=1, source_target_pairs={{0,24},{1,9},{2,26},{3,11},{4,28},{5,13},{6,30},{7,15},{8,0},{9,17... | collective-permute-start | bytes 1179656 | tf_op jit(solution)/shard_map/ppermute | solution.py:268
  14.7 5.5 %collective-permute-done.3.rest_0_.rest_1_ = bf16[4,384,128]{2,1,0:T(8,128)(2,1)S(1)} collective-permute-done((bf16[4,384,128]{2,1,0:T(8,128)(2,1)S(1)}, bf16[4,384,128]{2,1,0:T(8,128)(2,1)S(1)}, u32[]{:S(2)}, u32[]{:S(2)}) %collective-permute-start.3) | collective-permute-done | bytes 393248 | tf_op jit(solution)/shard_map/ppermute | solution.py:264
  20.2 2.3 %collective-permute-start.14 = (bf16[4,384,128]{2,1,0:T(8,128)(2,1)S(1)}, bf16[4,384,128]{2,1,0:T(8,128)(2,1)S(1)}, u32[]{:S(2)}, u32[]{:S(2)}) collective-permute-start(bf16[4,384,128]{2,1,0:T(8,128)(2,1)S(1)} %collective-permute-done.3.rest_0_.rest_1_), channel_id=1, source_target_pairs={{0,6},{1,3},{2,0},{3,5},{4,2},{5,7},{6,4},{7,1},{8,14},{9,11},{10,... | collective-permute-start | bytes 1179656 | tf_op jit(solution)/shard_map/ppermute | solution.py:264
  26.2 3.7 %collective-permute-start.18 = (bf16[4,2,192,128]{3,2,1,0:T(8,128)(2,1)S(1)}, bf16[4,2,192,128]{3,2,1,0:T(8,128)(2,1)S(1)}, u32[]{:S(2)}, u32[]{:S(2)}) collective-permute-start(bf16[4,2,192,128]{3,2,1,0:T(8,128)(2,1)S(1)} %shard_map.67), channel_id=1, source_target_pairs={{0,16},{1,17},{2,18},{3,19},{4,20},{5,21},{6,22},{7,23},{8,24},{9,... | collective-permute-start | bytes 1179656 | tf_op jit(solution)/shard_map/ppermute | solution.py:268
  33.2 2.3 %collective-permute-start.17 = (bf16[4,768,128]{2,1,0:T(8,128)(2,1)S(1)}, bf16[4,768,128]{2,1,0:T(8,128)(2,1)S(1)}, u32[]{:S(2)}, u32[]{:S(2)}) collective-permute-start(bf16[4,768,128]{2,1,0:T(8,128)(2,1)S(1)} %shard_map.66.rest_7_), channel_id=1, source_target_pairs={{0,24},{1,9},{2,26},{3,11},{4,28},{5,13},{6,30},{7,15},{8,0},{9,17... | collective-permute-start | bytes 2359304 | tf_op jit(solution)/shard_map/ppermute | solution.py:268
  36.4 3.5 %collective-permute-done.18.x1.rest_6_ = bf16[4,2,192,128]{3,2,1,0:T(8,128)(2,1)S(1)} collective-permute-done((bf16[4,2,192,128]{3,2,1,0:T(8,128)(2,1)S(1)}, bf16[4,2,192,128]{3,2,1,0:T(8,128)(2,1)S(1)}, u32[]{:S(2)}, u32[]{:S(2)}) %collective-permute-start.18) | collective-permute-done | bytes 393248 | tf_op jit(solution)/shard_map/ppermute | solution.py:268
  41.7 3.1 %collective-permute-start.13 = (bf16[4,384,128]{2,1,0:T(8,128)(2,1)S(1)}, bf16[4,384,128]{2,1,0:T(8,128)(2,1)S(1)}, u32[]{:S(2)}, u32[]{:S(2)}) collective-permute-start(bf16[4,384,128]{2,1,0:T(8,128)(2,1)S(1)} %collective-permute-done.5.rest_0_.rest_1_.rest_4_), channel_id=1, source_target_pairs={{0,6},{1,3},{2,0},{3,5},{4,2},{5,7},{6,4},{7,1},{8,14},{9,11},{10,... | collective-permute-start | bytes 1179656 | tf_op jit(solution)/shard_map/ppermute | solution.py:264
  52.5 3.1 %collective-permute-start.19 = (bf16[4,768,128]{2,1,0:T(8,128)(2,1)S(1)}, bf16[4,768,128]{2,1,0:T(8,128)(2,1)S(1)}, u32[]{:S(2)}, u32[]{:S(2)}) collective-permute-start(bf16[4,768,128]{2,1,0:T(8,128)(2,1)S(1)} %shard_map.69), channel_id=1, source_target_pairs={{0,24},{1,9},{2,26},{3,11},{4,28},{5,13},{6,30},{7,15},{8,0},{9,17... | collective-permute-start | bytes 2359304 | tf_op jit(solution)/shard_map/ppermute | solution.py:268
  56.9 2.8 %collective-permute-start.24 = (bf16[4,768,128]{2,1,0:T(8,128)(2,1)S(1)}, bf16[4,768,128]{2,1,0:T(8,128)(2,1)S(1)}, u32[]{:S(2)}, u32[]{:S(2)}) collective-permute-start(bf16[4,768,128]{2,1,0:T(8,128)(2,1)S(1)} %shard_map.73), channel_id=1, source_target_pairs={{0,24},{1,9},{2,26},{3,11},{4,28},{5,13},{6,30},{7,15},{8,0},{9,17... | collective-permute-start | bytes 2359304 | tf_op jit(solution)/shard_map/ppermute | solution.py:268
  59.7 2.5 %collective-permute-start.12 = (bf16[4,384,128]{2,1,0:T(8,128)(2,1)S(1)}, bf16[4,384,128]{2,1,0:T(8,128)(2,1)S(1)}, u32[]{:S(2)}, u32[]{:S(2)}) collective-permute-start(bf16[4,384,128]{2,1,0:T(8,128)(2,1)S(1)} %collective-permute-done.7.rest_0_.rest_1_.rest_5_), channel_id=1, source_target_pairs={{0,6},{1,3},{2,0},{3,5},{4,2},{5,7},{6,4},{7,1},{8,14},{9,11},{10,... | collective-permute-start | bytes 1179656 | tf_op jit(solution)/shard_map/ppermute | solution.py:264
  62.5 2.4 %collective-permute-start.9 = (bf16[4,384,128]{2,1,0:T(8,128)(2,1)S(1)}, bf16[4,384,128]{2,1,0:T(8,128)(2,1)S(1)}, u32[]{:S(2)}, u32[]{:S(2)}) collective-permute-start(bf16[4,384,128]{2,1,0:T(8,128)(2,1)S(1)} %shard_map.65), channel_id=1, source_target_pairs={{0,6},{1,3},{2,0},{3,5},{4,2},{5,7},{6,4},{7,1},{8,14},{9,11},{10,... | collective-permute-start | bytes 1179656 | tf_op jit(solution)/shard_map/ppermute | solution.py:264
  64.9 4.0 %collective-permute-done.12.rest_2_ = bf16[4,384,128]{2,1,0:T(8,128)(2,1)S(1)} collective-permute-done((bf16[4,384,128]{2,1,0:T(8,128)(2,1)S(1)}, bf16[4,384,128]{2,1,0:T(8,128)(2,1)S(1)}, u32[]{:S(2)}, u32[]{:S(2)}) %collective-permute-start.12) | collective-permute-done | bytes 393248 | tf_op jit(solution)/shard_map/ppermute | solution.py:264
  70.3 2.9 %collective-permute-start.20 = (bf16[4,768,128]{2,1,0:T(8,128)(2,1)S(1)}, bf16[4,768,128]{2,1,0:T(8,128)(2,1)S(1)}, u32[]{:S(2)}, u32[]{:S(2)}) collective-permute-start(bf16[4,768,128]{2,1,0:T(8,128)(2,1)S(1)} %shard_map.70), channel_id=1, source_target_pairs={{0,24},{1,9},{2,26},{3,11},{4,28},{5,13},{6,30},{7,15},{8,0},{9,17... | collective-permute-start | bytes 2359304 | tf_op jit(solution)/shard_map/ppermute | solution.py:268
  74.9 3.8 %collective-permute-start.25 = (bf16[4,768,128]{2,1,0:T(8,128)(2,1)S(1)}, bf16[4,768,128]{2,1,0:T(8,128)(2,1)S(1)}, u32[]{:S(2)}, u32[]{:S(2)}) collective-permute-start(bf16[4,768,128]{2,1,0:T(8,128)(2,1)S(1)} %shard_map.74), channel_id=1, source_target_pairs={{0,24},{1,9},{2,26},{3,11},{4,28},{5,13},{6,30},{7,15},{8,0},{9,17... | collective-permute-start | bytes 2359304 | tf_op jit(solution)/shard_map/ppermute | solution.py:268
  78.6 2.5 %collective-permute-start.10 = (bf16[4,384,128]{2,1,0:T(8,128)(2,1)S(1)}, bf16[4,384,128]{2,1,0:T(8,128)(2,1)S(1)}, u32[]{:S(2)}, u32[]{:S(2)}) collective-permute-start(bf16[4,384,128]{2,1,0:T(8,128)(2,1)S(1)} %collective-permute-done.9.rest_1_.rest_5_), channel_id=1, source_target_pairs={{0,6},{1,3},{2,0},{3,5},{4,2},{5,7},{6,4},{7,1},{8,14},{9,11},{10,... | collective-permute-start | bytes 1179656 | tf_op jit(solution)/shard_map/ppermute | solution.py:264
  81.1 5.3 %collective-permute-done.10.rest_2_ = bf16[4,384,128]{2,1,0:T(8,128)(2,1)S(1)} collective-permute-done((bf16[4,384,128]{2,1,0:T(8,128)(2,1)S(1)}, bf16[4,384,128]{2,1,0:T(8,128)(2,1)S(1)}, u32[]{:S(2)}, u32[]{:S(2)}) %collective-permute-start.10) | collective-permute-done | bytes 393248 | tf_op jit(solution)/shard_map/ppermute | solution.py:264
  86.4 2.2 %shard_map.71 = (bf16[768,128]{1,0:T(8,128)(2,1)S(1)}, bf16[768,128]{1,0:T(8,128)(2,1)S(1)}, bf16[768,128]{1,0:T(8,128)(2,1)S(1)}, bf16[768,128]{1,0:T(8,128)(2,1)S(1)}) custom-call(s32[4]{0:T(128)S(1)} %pad_add_fusion.place, s32[32,48]{1,0:T(8,128)S(1)} %bitcast.29, bf16[768,1536]{1,0:T(8,128)(2,1)S(1)} %get-tuple-element.21.green.rest_2_, ...), custom_call_target="tpu_custom_call" | custom-call | bytes 1024 | tf_op jit(solution)/shard_map/pallas_call | solution.py:38
  92.2 2.6 %collective-permute-done.21.rest_8_.rest_1_ = bf16[768,128]{1,0:T(8,128)(2,1)S(1)} collective-permute-done((bf16[768,128]{1,0:T(8,128)(2,1)S(1)}, bf16[768,128]{1,0:T(8,128)(2,1)S(1)}, u32[]{:S(2)}, u32[]{:S(2)}) %collective-permute-start.21) | collective-permute-done | bytes 196640 | tf_op jit(solution)/shard_map/ppermute | solution.py:260
  96.7 4.2 %shard_map.76 = (bf16[896,128]{1,0:T(8,128)(2,1)S(1)}, bf16[896,128]{1,0:T(8,128)(2,1)S(1)}, bf16[1664,128]{1,0:T(8,128)(2,1)S(1)}, bf16[896,128]{1,0:T(8,128)(2,1)S(1)}) custom-call(s32[4]{0:T(128)S(1)} %pad_add_fusion.place, s32[32,48]{1,0:T(8,128)S(1)} %bitcast.30, bf16[768,1536]{1,0:T(8,128)(2,1)S(1)} %get-tuple-element.29.rest_3_.green, ...), custom_call_target="tpu_custom_call" | custom-call | bytes 1024 | tf_op jit(solution)/shard_map/pallas_call | solution.py:38
  100.9 3.5 %collective-permute-start.27 = (bf16[1664,128]{1,0:T(8,128)(2,1)S(1)}, bf16[1664,128]{1,0:T(8,128)(2,1)S(1)}, u32[]{:S(2)}, u32[]{:S(2)}) collective-permute-start(bf16[1664,128]{1,0:T(8,128)(2,1)S(1)} %get-tuple-element.36), channel_id=1, source_target_pairs={{0,4},{1,5},{2,6},{3,7},{4,0},{5,1},{6,2},{7,3},{8,12},{9,13},{10,... | collective-permute-start | bytes 1277960 | tf_op jit(solution)/shard_map/ppermute | solution.py:260
  106.4 7.2 %collective-permute-done.26.rest_4_ = bf16[896,128]{1,0:T(8,128)(2,1)S(1)} collective-permute-done((bf16[896,128]{1,0:T(8,128)(2,1)S(1)}, bf16[896,128]{1,0:T(8,128)(2,1)S(1)}, u32[]{:S(2)}, u32[]{:S(2)}) %collective-permute-start.26) | collective-permute-done | bytes 229408 | tf_op jit(solution)/shard_map/ppermute | solution.py:260
  113.7 2.6 %shard_map.77 = (bf16[4,8,192,128]{3,2,1,0:T(8,128)(2,1)}, f32[128,128]{1,0:T(8,128)}) custom-call(s32[4]{0:T(128)S(1)} %pad_add_fusion.place, f32[128,128]{1,0:T(8,128)S(1)} %bitcast.31, bf16[768,128]{1,0:T(8,128)(2,1)S(1)} %get-tuple-element.30.rest_0_, bf16[768,128]{1,0:T(8,128)(2,1)S(1)} %collective-permute-done.21.rest_8_.rest_1_, ...), custom_call_target="tpu_custom_call" | custom-call | bytes 1024 | tf_op jit(solution)/shard_map/pallas_call | solution.py:38
  (64 shorter events, 35.9 us)
Async XLA Ops:
  8.8 11.4 %collective-permute-start.3 = (bf16[4,384,128]{2,1,0:T(8,128)(2,1)S(1)}, bf16[4,384,128]{2,1,0:T(8,128)(2,1)S(1)}, u32[]{:S(2)}, u32[]{:S(2)}) collective-permute-start(bf16[4,384,128]{2,1,0:T(8,128)(2,1)S(1)} %bitcast.19), channel_id=1, source_target_pairs={{0,6},{1,3},{2,0},{3,5},{4,2},{5,7},{6,4},{7,1},{8,14},{9,11},{10,... | collective-permute-start | bytes 1179656 | tf_op jit(solution)/shard_map/ppermute | solution.py:264
  11.0 12.6 %collective-permute-start.4 = (bf16[4,384,128]{2,1,0:T(8,128)(2,1)S(1)}, bf16[4,384,128]{2,1,0:T(8,128)(2,1)S(1)}, u32[]{:S(2)}, u32[]{:S(2)}) collective-permute-start(bf16[4,384,128]{2,1,0:T(8,128)(2,1)S(1)} %bitcast.20), channel_id=1, source_target_pairs={{0,2},{1,7},{2,4},{3,1},{4,6},{5,3},{6,0},{7,5},{8,10},{9,15},{10,... | collective-permute-start | bytes 1179656 | tf_op jit(solution)/shard_map/ppermute | solution.py:264
  12.0 13.9 %collective-permute-start.16 = (bf16[4,2,192,128]{3,2,1,0:T(8,128)(2,1)S(1)}, bf16[4,2,192,128]{3,2,1,0:T(8,128)(2,1)S(1)}, u32[]{:S(2)}, u32[]{:S(2)}) collective-permute-start(bf16[4,2,192,128]{3,2,1,0:T(8,128)(2,1)S(1)} %get-tuple-element.27), channel_id=1, source_target_pairs={{0,24},{1,9},{2,26},{3,11},{4,28},{5,13},{6,30},{7,15},{8,0},{9,17... | collective-permute-start | bytes 1179656 | tf_op jit(solution)/shard_map/ppermute | solution.py:268
  14.7 11.3 %collective-permute-start.15 = (bf16[4,2,192,128]{3,2,1,0:T(8,128)(2,1)S(1)}, bf16[4,2,192,128]{3,2,1,0:T(8,128)(2,1)S(1)}, u32[]{:S(2)}, u32[]{:S(2)}) collective-permute-start(bf16[4,2,192,128]{3,2,1,0:T(8,128)(2,1)S(1)} %shard_map.61.after), channel_id=1, source_target_pairs={{0,8},{1,25},{2,10},{3,27},{4,12},{5,29},{6,14},{7,31},{8,16},{9,1... | collective-permute-start | bytes 1179656 | tf_op jit(solution)/shard_map/ppermute | solution.py:268
  20.2 11.6 %collective-permute-start.14 = (bf16[4,384,128]{2,1,0:T(8,128)(2,1)S(1)}, bf16[4,384,128]{2,1,0:T(8,128)(2,1)S(1)}, u32[]{:S(2)}, u32[]{:S(2)}) collective-permute-start(bf16[4,384,128]{2,1,0:T(8,128)(2,1)S(1)} %collective-permute-done.3.rest_0_.rest_1_), channel_id=1, source_target_pairs={{0,6},{1,3},{2,0},{3,5},{4,2},{5,7},{6,4},{7,1},{8,14},{9,11},{10,... | collective-permute-start | bytes 1179656 | tf_op jit(solution)/shard_map/ppermute | solution.py:264
  23.9 11.6 %collective-permute-start.6 = (bf16[4,384,128]{2,1,0:T(8,128)(2,1)S(1)}, bf16[4,384,128]{2,1,0:T(8,128)(2,1)S(1)}, u32[]{:S(2)}, u32[]{:S(2)}) collective-permute-start(bf16[4,384,128]{2,1,0:T(8,128)(2,1)S(1)} %shard_map.63), channel_id=1, source_target_pairs={{0,2},{1,7},{2,4},{3,1},{4,6},{5,3},{6,0},{7,5},{8,10},{9,15},{10,... | collective-permute-start | bytes 1179656 | tf_op jit(solution)/shard_map/ppermute | solution.py:264
  24.0 12.4 %collective-permute-start.5 = (bf16[4,384,128]{2,1,0:T(8,128)(2,1)S(1)}, bf16[4,384,128]{2,1,0:T(8,128)(2,1)S(1)}, u32[]{:S(2)}, u32[]{:S(2)}) collective-permute-start(bf16[4,384,128]{2,1,0:T(8,128)(2,1)S(1)} %shard_map.63), channel_id=1, source_target_pairs={{0,6},{1,3},{2,0},{3,5},{4,2},{5,7},{6,4},{7,1},{8,14},{9,11},{10,... | collective-permute-start | bytes 1179656 | tf_op jit(solution)/shard_map/ppermute | solution.py:264
  26.2 13.7 %collective-permute-start.18 = (bf16[4,2,192,128]{3,2,1,0:T(8,128)(2,1)S(1)}, bf16[4,2,192,128]{3,2,1,0:T(8,128)(2,1)S(1)}, u32[]{:S(2)}, u32[]{:S(2)}) collective-permute-start(bf16[4,2,192,128]{3,2,1,0:T(8,128)(2,1)S(1)} %shard_map.67), channel_id=1, source_target_pairs={{0,16},{1,17},{2,18},{3,19},{4,20},{5,21},{6,22},{7,23},{8,24},{9,... | collective-permute-start | bytes 1179656 | tf_op jit(solution)/shard_map/ppermute | solution.py:268
  33.2 17.9 %collective-permute-start.17 = (bf16[4,768,128]{2,1,0:T(8,128)(2,1)S(1)}, bf16[4,768,128]{2,1,0:T(8,128)(2,1)S(1)}, u32[]{:S(2)}, u32[]{:S(2)}) collective-permute-start(bf16[4,768,128]{2,1,0:T(8,128)(2,1)S(1)} %shard_map.66.rest_7_), channel_id=1, source_target_pairs={{0,24},{1,9},{2,26},{3,11},{4,28},{5,13},{6,30},{7,15},{8,0},{9,17... | collective-permute-start | bytes 2359304 | tf_op jit(solution)/shard_map/ppermute | solution.py:268
  41.3 14.3 %collective-permute-start.23 = (bf16[4,768,128]{2,1,0:T(8,128)(2,1)S(1)}, bf16[4,768,128]{2,1,0:T(8,128)(2,1)S(1)}, u32[]{:S(2)}, u32[]{:S(2)}) collective-permute-start(bf16[4,768,128]{2,1,0:T(8,128)(2,1)S(1)} %shard_map.72), channel_id=1, source_target_pairs={{0,24},{1,9},{2,26},{3,11},{4,28},{5,13},{6,30},{7,15},{8,0},{9,17... | collective-permute-start | bytes 2359304 | tf_op jit(solution)/shard_map/ppermute | solution.py:268
  41.7 9.4 %collective-permute-start.13 = (bf16[4,384,128]{2,1,0:T(8,128)(2,1)S(1)}, bf16[4,384,128]{2,1,0:T(8,128)(2,1)S(1)}, u32[]{:S(2)}, u32[]{:S(2)}) collective-permute-start(bf16[4,384,128]{2,1,0:T(8,128)(2,1)S(1)} %collective-permute-done.5.rest_0_.rest_1_.rest_4_), channel_id=1, source_target_pairs={{0,6},{1,3},{2,0},{3,5},{4,2},{5,7},{6,4},{7,1},{8,14},{9,11},{10,... | collective-permute-start | bytes 1179656 | tf_op jit(solution)/shard_map/ppermute | solution.py:264
  45.0 10.6 %collective-permute-start.8 = (bf16[4,384,128]{2,1,0:T(8,128)(2,1)S(1)}, bf16[4,384,128]{2,1,0:T(8,128)(2,1)S(1)}, u32[]{:S(2)}, u32[]{:S(2)}) collective-permute-start(bf16[4,384,128]{2,1,0:T(8,128)(2,1)S(1)} %shard_map.64), channel_id=1, source_target_pairs={{0,2},{1,7},{2,4},{3,1},{4,6},{5,3},{6,0},{7,5},{8,10},{9,15},{10,... | collective-permute-start | bytes 1179656 | tf_op jit(solution)/shard_map/ppermute | solution.py:264
  45.0 10.5 %collective-permute-start.7 = (bf16[4,384,128]{2,1,0:T(8,128)(2,1)S(1)}, bf16[4,384,128]{2,1,0:T(8,128)(2,1)S(1)}, u32[]{:S(2)}, u32[]{:S(2)}) collective-permute-start(bf16[4,384,128]{2,1,0:T(8,128)(2,1)S(1)} %shard_map.64), channel_id=1, source_target_pairs={{0,6},{1,3},{2,0},{3,5},{4,2},{5,7},{6,4},{7,1},{8,14},{9,11},{10,... | collective-permute-start | bytes 1179656 | tf_op jit(solution)/shard_map/ppermute | solution.py:264
  52.5 16.4 %collective-permute-start.19 = (bf16[4,768,128]{2,1,0:T(8,128)(2,1)S(1)}, bf16[4,768,128]{2,1,0:T(8,128)(2,1)S(1)}, u32[]{:S(2)}, u32[]{:S(2)}) collective-permute-start(bf16[4,768,128]{2,1,0:T(8,128)(2,1)S(1)} %shard_map.69), channel_id=1, source_target_pairs={{0,24},{1,9},{2,26},{3,11},{4,28},{5,13},{6,30},{7,15},{8,0},{9,17... | collective-permute-start | bytes 2359304 | tf_op jit(solution)/shard_map/ppermute | solution.py:268
  56.9 16.5 %collective-permute-start.24 = (bf16[4,768,128]{2,1,0:T(8,128)(2,1)S(1)}, bf16[4,768,128]{2,1,0:T(8,128)(2,1)S(1)}, u32[]{:S(2)}, u32[]{:S(2)}) collective-permute-start(bf16[4,768,128]{2,1,0:T(8,128)(2,1)S(1)} %shard_map.73), channel_id=1, source_target_pairs={{0,24},{1,9},{2,26},{3,11},{4,28},{5,13},{6,30},{7,15},{8,0},{9,17... | collective-permute-start | bytes 2359304 | tf_op jit(solution)/shard_map/ppermute | solution.py:268
  59.7 9.2 %collective-permute-start.12 = (bf16[4,384,128]{2,1,0:T(8,128)(2,1)S(1)}, bf16[4,384,128]{2,1,0:T(8,128)(2,1)S(1)}, u32[]{:S(2)}, u32[]{:S(2)}) collective-permute-start(bf16[4,384,128]{2,1,0:T(8,128)(2,1)S(1)} %collective-permute-done.7.rest_0_.rest_1_.rest_5_), channel_id=1, source_target_pairs={{0,6},{1,3},{2,0},{3,5},{4,2},{5,7},{6,4},{7,1},{8,14},{9,11},{10,... | collective-permute-start | bytes 1179656 | tf_op jit(solution)/shard_map/ppermute | solution.py:264
  62.4 10.8 %collective-permute-start.11 = (bf16[4,384,128]{2,1,0:T(8,128)(2,1)S(1)}, bf16[4,384,128]{2,1,0:T(8,128)(2,1)S(1)}, u32[]{:S(2)}, u32[]{:S(2)}) collective-permute-start(bf16[4,384,128]{2,1,0:T(8,128)(2,1)S(1)} %shard_map.65), channel_id=1, source_target_pairs={{0,2},{1,7},{2,4},{3,1},{4,6},{5,3},{6,0},{7,5},{8,10},{9,15},{10,... | collective-permute-start | bytes 1179656 | tf_op jit(solution)/shard_map/ppermute | solution.py:264
  62.5 10.7 %collective-permute-start.9 = (bf16[4,384,128]{2,1,0:T(8,128)(2,1)S(1)}, bf16[4,384,128]{2,1,0:T(8,128)(2,1)S(1)}, u32[]{:S(2)}, u32[]{:S(2)}) collective-permute-start(bf16[4,384,128]{2,1,0:T(8,128)(2,1)S(1)} %shard_map.65), channel_id=1, source_target_pairs={{0,6},{1,3},{2,0},{3,5},{4,2},{5,7},{6,4},{7,1},{8,14},{9,11},{10,... | collective-permute-start | bytes 1179656 | tf_op jit(solution)/shard_map/ppermute | solution.py:264
  70.3 16.1 %collective-permute-start.20 = (bf16[4,768,128]{2,1,0:T(8,128)(2,1)S(1)}, bf16[4,768,128]{2,1,0:T(8,128)(2,1)S(1)}, u32[]{:S(2)}, u32[]{:S(2)}) collective-permute-start(bf16[4,768,128]{2,1,0:T(8,128)(2,1)S(1)} %shard_map.70), channel_id=1, source_target_pairs={{0,24},{1,9},{2,26},{3,11},{4,28},{5,13},{6,30},{7,15},{8,0},{9,17... | collective-permute-start | bytes 2359304 | tf_op jit(solution)/shard_map/ppermute | solution.py:268
  74.9 17.3 %collective-permute-start.25 = (bf16[4,768,128]{2,1,0:T(8,128)(2,1)S(1)}, bf16[4,768,128]{2,1,0:T(8,128)(2,1)S(1)}, u32[]{:S(2)}, u32[]{:S(2)}) collective-permute-start(bf16[4,768,128]{2,1,0:T(8,128)(2,1)S(1)} %shard_map.74), channel_id=1, source_target_pairs={{0,24},{1,9},{2,26},{3,11},{4,28},{5,13},{6,30},{7,15},{8,0},{9,17... | collective-permute-start | bytes 2359304 | tf_op jit(solution)/shard_map/ppermute | solution.py:268
  78.6 7.8 %collective-permute-start.10 = (bf16[4,384,128]{2,1,0:T(8,128)(2,1)S(1)}, bf16[4,384,128]{2,1,0:T(8,128)(2,1)S(1)}, u32[]{:S(2)}, u32[]{:S(2)}) collective-permute-start(bf16[4,384,128]{2,1,0:T(8,128)(2,1)S(1)} %collective-permute-done.9.rest_1_.rest_5_), channel_id=1, source_target_pairs={{0,6},{1,3},{2,0},{3,5},{4,2},{5,7},{6,4},{7,1},{8,14},{9,11},{10,... | collective-permute-start | bytes 1179656 | tf_op jit(solution)/shard_map/ppermute | solution.py:264
  100.9 12.8 %collective-permute-start.27 = (bf16[1664,128]{1,0:T(8,128)(2,1)S(1)}, bf16[1664,128]{1,0:T(8,128)(2,1)S(1)}, u32[]{:S(2)}, u32[]{:S(2)}) collective-permute-start(bf16[1664,128]{1,0:T(8,128)(2,1)S(1)} %get-tuple-element.36), channel_id=1, source_target_pairs={{0,4},{1,5},{2,6},{3,7},{4,0},{5,1},{6,2},{7,3},{8,12},{9,13},{10,... | collective-permute-start | bytes 1277960 | tf_op jit(solution)/shard_map/ppermute | solution.py:260
  104.4 9.3 %collective-permute-start.26 = (bf16[896,128]{1,0:T(8,128)(2,1)S(1)}, bf16[896,128]{1,0:T(8,128)(2,1)S(1)}, u32[]{:S(2)}, u32[]{:S(2)}) collective-permute-start(bf16[896,128]{1,0:T(8,128)(2,1)S(1)} %get-tuple-element.35), channel_id=1, source_target_pairs={{0,2},{1,3},{2,4},{3,5},{4,6},{5,7},{6,0},{7,1},{8,10},{9,11},{10,... | collective-permute-start | bytes 688136 | tf_op jit(solution)/shard_map/ppermute | solution.py:260
  104.4 9.3 %collective-permute-start.28 = (bf16[896,128]{1,0:T(8,128)(2,1)S(1)}, bf16[896,128]{1,0:T(8,128)(2,1)S(1)}, u32[]{:S(2)}, u32[]{:S(2)}) collective-permute-start(bf16[896,128]{1,0:T(8,128)(2,1)S(1)} %get-tuple-element.37), channel_id=1, source_target_pairs={{0,6},{1,7},{2,0},{3,1},{4,2},{5,3},{6,4},{7,5},{8,14},{9,15},{10,... | collective-permute-start | bytes 688136 | tf_op jit(solution)/shard_map/ppermute | solution.py:260
  (10 other events, 81.7 us)

commit v3 on v2

--- a/solution.py
+++ b/solution.py
@@ -183,7 +183,9 @@
                     rows = slice(start, start + 64)
                     part = value[rows, i * W : (i + 1) * W] + acc[q, rows, :].astype(F32)
                     out[rows, :] = (part * keep).astype(BF16)
-        if half:
+    if half:
+        for h in range(2):
+            order = [lax.rem(y + 2 * h + i, 4) for i in range(2)]
             left = jnp.concatenate([columns_t[1, q] for q in order], axis=0)
             right = jnp.concatenate([outs[2 * h + i][0:HALF, :] for i in range(2)], axis=1)
             term = jnp.dot(left, right, preferred_element_type=F32)
@@ -192,7 +194,6 @@
                 outs[2 * h + i][HALF : HALF + W, :] = (
                     terms[2 * h + i] - term[block, block]
                 ).astype(BF16)
-    if half:
         first.wait()
 
 

time: 118 us -> 116 us (0.983)
  Pallas kernels: 26.2 us -> 24.7 us
    pallas_call x19, Pallas kernels: 26.2 us -> 24.7 us  [call(): pl.pallas_call(kernel, out_shape=[jax.ShapeDtypeStruct(s, d) for s, d in...]
where the time goes in v3:
time: 116 us; the launch traced here: 115 us
  starting transfers between devices  49.9 us (43%)
  waiting for transfers between devices  37.1 us (32%)
  Pallas kernels  24.7 us (21%)
  local copies, waits for them, and re-layouts  2.14 us (2%)
    pallas_call x19, Pallas kernels, call(): pl.pallas_call(kernel, out_shape=[jax.ShapeDtypeStruct(s, d) for s, d in...  24.7 us
    ppermute x9, starting transfers between devices, ring_x(): return lax.ppermute(v, ('row', 'col'), pairs)  21.7 us
    ppermute x12, waiting for transfers between devices, ring_y(): return lax.ppermute(v, 'col', pairs)  19.8 us
    ppermute x12, starting transfers between devices, ring_y(): return lax.ppermute(v, 'col', pairs)  19.3 us
    ppermute x5, waiting for transfers between devices, over_y(): return lax.ppermute(v, 'col', [(c, (c + 2 * d) % 8) for c in range(8)])  11.8 us
    ppermute x5, starting transfers between devices, over_y(): return lax.ppermute(v, 'col', [(c, (c + 2 * d) % 8) for c in range(8)])  8.2 us
    ppermute x9, waiting for transfers between devices, ring_x(): return lax.ppermute(v, ('row', 'col'), pairs)  3.73 us
  transfers between devices with their start and end apart: 29, of which 12 were waited for; matrix products, arithmetic and copies ran while one was open for 0% of the time, Pallas kernels for 17%

profile of v3, /device:TPU:8, one launch (start us, length us, event | category | flops | bytes accessed | tf_op | source)
XLA Modules:
  0.0 115.0 jit_solution(12433047944853263161)
XLA Ops:
  3.0 2.6 %shard_map.60 = (bf16[4,192,128]{2,1,0:T(8,128)(2,1)S(1)}, bf16[4,192,128]{2,1,0:T(8,128)(2,1)S(1)}, bf16[3,4,192,128]{3,2,1,0:T(8,128)(2,1)S(1)}, bf16[3,4,192,128]{3,2,1,0:T(8,128)(2,1)S(1)}) custom-call(s32[4]{0:T(128)S(1)} %pad_add_fusion.place, s32[32,48]{1,0:T(8,128)S(1)} %bitcast.28, bf16[192,32,128]{2,1,0:T(8,128)(2,1)S(1)} %copy-done.1), custom_call_target="tpu_custom_call" | custom-call | bytes 1024 | tf_op jit(solution)/shard_map/pallas_call | solution.py:38
  8.8 2.3 %collective-permute-start.3 = (bf16[4,384,128]{2,1,0:T(8,128)(2,1)S(1)}, bf16[4,384,128]{2,1,0:T(8,128)(2,1)S(1)}, u32[]{:S(2)}, u32[]{:S(2)}) collective-permute-start(bf16[4,384,128]{2,1,0:T(8,128)(2,1)S(1)} %bitcast.19), channel_id=1, source_target_pairs={{0,6},{1,3},{2,0},{3,5},{4,2},{5,7},{6,4},{7,1},{8,14},{9,11},{10,... | collective-permute-start | bytes 1179656 | tf_op jit(solution)/shard_map/ppermute | solution.py:265
  12.0 2.7 %collective-permute-start.16 = (bf16[4,2,192,128]{3,2,1,0:T(8,128)(2,1)S(1)}, bf16[4,2,192,128]{3,2,1,0:T(8,128)(2,1)S(1)}, u32[]{:S(2)}, u32[]{:S(2)}) collective-permute-start(bf16[4,2,192,128]{3,2,1,0:T(8,128)(2,1)S(1)} %get-tuple-element.27), channel_id=1, source_target_pairs={{0,24},{1,9},{2,26},{3,11},{4,28},{5,13},{6,30},{7,15},{8,0},{9,17... | collective-permute-start | bytes 1179656 | tf_op jit(solution)/shard_map/ppermute | solution.py:269
  14.7 5.5 %collective-permute-done.3.rest_0_.rest_1_ = bf16[4,384,128]{2,1,0:T(8,128)(2,1)S(1)} collective-permute-done((bf16[4,384,128]{2,1,0:T(8,128)(2,1)S(1)}, bf16[4,384,128]{2,1,0:T(8,128)(2,1)S(1)}, u32[]{:S(2)}, u32[]{:S(2)}) %collective-permute-start.3) | collective-permute-done | bytes 393248 | tf_op jit(solution)/shard_map/ppermute | solution.py:265
  20.2 2.3 %collective-permute-start.14 = (bf16[4,384,128]{2,1,0:T(8,128)(2,1)S(1)}, bf16[4,384,128]{2,1,0:T(8,128)(2,1)S(1)}, u32[]{:S(2)}, u32[]{:S(2)}) collective-permute-start(bf16[4,384,128]{2,1,0:T(8,128)(2,1)S(1)} %collective-permute-done.3.rest_0_.rest_1_), channel_id=1, source_target_pairs={{0,6},{1,3},{2,0},{3,5},{4,2},{5,7},{6,4},{7,1},{8,14},{9,11},{10,... | collective-permute-start | bytes 1179656 | tf_op jit(solution)/shard_map/ppermute | solution.py:265
  26.2 3.7 %collective-permute-start.18 = (bf16[4,2,192,128]{3,2,1,0:T(8,128)(2,1)S(1)}, bf16[4,2,192,128]{3,2,1,0:T(8,128)(2,1)S(1)}, u32[]{:S(2)}, u32[]{:S(2)}) collective-permute-start(bf16[4,2,192,128]{3,2,1,0:T(8,128)(2,1)S(1)} %shard_map.67), channel_id=1, source_target_pairs={{0,16},{1,17},{2,18},{3,19},{4,20},{5,21},{6,22},{7,23},{8,24},{9,... | collective-permute-start | bytes 1179656 | tf_op jit(solution)/shard_map/ppermute | solution.py:269
  33.2 2.3 %collective-permute-start.17 = (bf16[4,768,128]{2,1,0:T(8,128)(2,1)S(1)}, bf16[4,768,128]{2,1,0:T(8,128)(2,1)S(1)}, u32[]{:S(2)}, u32[]{:S(2)}) collective-permute-start(bf16[4,768,128]{2,1,0:T(8,128)(2,1)S(1)} %shard_map.66.rest_7_), channel_id=1, source_target_pairs={{0,24},{1,9},{2,26},{3,11},{4,28},{5,13},{6,30},{7,15},{8,0},{9,17... | collective-permute-start | bytes 2359304 | tf_op jit(solution)/shard_map/ppermute | solution.py:269
  36.4 3.5 %collective-permute-done.18.x1.rest_6_ = bf16[4,2,192,128]{3,2,1,0:T(8,128)(2,1)S(1)} collective-permute-done((bf16[4,2,192,128]{3,2,1,0:T(8,128)(2,1)S(1)}, bf16[4,2,192,128]{3,2,1,0:T(8,128)(2,1)S(1)}, u32[]{:S(2)}, u32[]{:S(2)}) %collective-permute-start.18) | collective-permute-done | bytes 393248 | tf_op jit(solution)/shard_map/ppermute | solution.py:269
  41.7 3.1 %collective-permute-start.13 = (bf16[4,384,128]{2,1,0:T(8,128)(2,1)S(1)}, bf16[4,384,128]{2,1,0:T(8,128)(2,1)S(1)}, u32[]{:S(2)}, u32[]{:S(2)}) collective-permute-start(bf16[4,384,128]{2,1,0:T(8,128)(2,1)S(1)} %collective-permute-done.5.rest_0_.rest_1_.rest_4_), channel_id=1, source_target_pairs={{0,6},{1,3},{2,0},{3,5},{4,2},{5,7},{6,4},{7,1},{8,14},{9,11},{10,... | collective-permute-start | bytes 1179656 | tf_op jit(solution)/shard_map/ppermute | solution.py:265
  52.5 3.1 %collective-permute-start.19 = (bf16[4,768,128]{2,1,0:T(8,128)(2,1)S(1)}, bf16[4,768,128]{2,1,0:T(8,128)(2,1)S(1)}, u32[]{:S(2)}, u32[]{:S(2)}) collective-permute-start(bf16[4,768,128]{2,1,0:T(8,128)(2,1)S(1)} %shard_map.69), channel_id=1, source_target_pairs={{0,24},{1,9},{2,26},{3,11},{4,28},{5,13},{6,30},{7,15},{8,0},{9,17... | collective-permute-start | bytes 2359304 | tf_op jit(solution)/shard_map/ppermute | solution.py:269
  56.9 2.8 %collective-permute-start.24 = (bf16[4,768,128]{2,1,0:T(8,128)(2,1)S(1)}, bf16[4,768,128]{2,1,0:T(8,128)(2,1)S(1)}, u32[]{:S(2)}, u32[]{:S(2)}) collective-permute-start(bf16[4,768,128]{2,1,0:T(8,128)(2,1)S(1)} %shard_map.73), channel_id=1, source_target_pairs={{0,24},{1,9},{2,26},{3,11},{4,28},{5,13},{6,30},{7,15},{8,0},{9,17... | collective-permute-start | bytes 2359304 | tf_op jit(solution)/shard_map/ppermute | solution.py:269
  59.7 2.5 %collective-permute-start.12 = (bf16[4,384,128]{2,1,0:T(8,128)(2,1)S(1)}, bf16[4,384,128]{2,1,0:T(8,128)(2,1)S(1)}, u32[]{:S(2)}, u32[]{:S(2)}) collective-permute-start(bf16[4,384,128]{2,1,0:T(8,128)(2,1)S(1)} %collective-permute-done.7.rest_0_.rest_1_.rest_5_), channel_id=1, source_target_pairs={{0,6},{1,3},{2,0},{3,5},{4,2},{5,7},{6,4},{7,1},{8,14},{9,11},{10,... | collective-permute-start | bytes 1179656 | tf_op jit(solution)/shard_map/ppermute | solution.py:265
  62.5 2.4 %collective-permute-start.9 = (bf16[4,384,128]{2,1,0:T(8,128)(2,1)S(1)}, bf16[4,384,128]{2,1,0:T(8,128)(2,1)S(1)}, u32[]{:S(2)}, u32[]{:S(2)}) collective-permute-start(bf16[4,384,128]{2,1,0:T(8,128)(2,1)S(1)} %shard_map.65), channel_id=1, source_target_pairs={{0,6},{1,3},{2,0},{3,5},{4,2},{5,7},{6,4},{7,1},{8,14},{9,11},{10,... | collective-permute-start | bytes 1179656 | tf_op jit(solution)/shard_map/ppermute | solution.py:265
  64.9 4.0 %collective-permute-done.12.rest_2_ = bf16[4,384,128]{2,1,0:T(8,128)(2,1)S(1)} collective-permute-done((bf16[4,384,128]{2,1,0:T(8,128)(2,1)S(1)}, bf16[4,384,128]{2,1,0:T(8,128)(2,1)S(1)}, u32[]{:S(2)}, u32[]{:S(2)}) %collective-permute-start.12) | collective-permute-done | bytes 393248 | tf_op jit(solution)/shard_map/ppermute | solution.py:265
  70.3 2.9 %collective-permute-start.20 = (bf16[4,768,128]{2,1,0:T(8,128)(2,1)S(1)}, bf16[4,768,128]{2,1,0:T(8,128)(2,1)S(1)}, u32[]{:S(2)}, u32[]{:S(2)}) collective-permute-start(bf16[4,768,128]{2,1,0:T(8,128)(2,1)S(1)} %shard_map.70), channel_id=1, source_target_pairs={{0,24},{1,9},{2,26},{3,11},{4,28},{5,13},{6,30},{7,15},{8,0},{9,17... | collective-permute-start | bytes 2359304 | tf_op jit(solution)/shard_map/ppermute | solution.py:269
  74.9 3.8 %collective-permute-start.25 = (bf16[4,768,128]{2,1,0:T(8,128)(2,1)S(1)}, bf16[4,768,128]{2,1,0:T(8,128)(2,1)S(1)}, u32[]{:S(2)}, u32[]{:S(2)}) collective-permute-start(bf16[4,768,128]{2,1,0:T(8,128)(2,1)S(1)} %shard_map.74), channel_id=1, source_target_pairs={{0,24},{1,9},{2,26},{3,11},{4,28},{5,13},{6,30},{7,15},{8,0},{9,17... | collective-permute-start | bytes 2359304 | tf_op jit(solution)/shard_map/ppermute | solution.py:269
  78.6 2.5 %collective-permute-start.10 = (bf16[4,384,128]{2,1,0:T(8,128)(2,1)S(1)}, bf16[4,384,128]{2,1,0:T(8,128)(2,1)S(1)}, u32[]{:S(2)}, u32[]{:S(2)}) collective-permute-start(bf16[4,384,128]{2,1,0:T(8,128)(2,1)S(1)} %collective-permute-done.9.rest_1_.rest_5_), channel_id=1, source_target_pairs={{0,6},{1,3},{2,0},{3,5},{4,2},{5,7},{6,4},{7,1},{8,14},{9,11},{10,... | collective-permute-start | bytes 1179656 | tf_op jit(solution)/shard_map/ppermute | solution.py:265
  81.1 5.3 %collective-permute-done.10.rest_2_ = bf16[4,384,128]{2,1,0:T(8,128)(2,1)S(1)} collective-permute-done((bf16[4,384,128]{2,1,0:T(8,128)(2,1)S(1)}, bf16[4,384,128]{2,1,0:T(8,128)(2,1)S(1)}, u32[]{:S(2)}, u32[]{:S(2)}) %collective-permute-start.10) | collective-permute-done | bytes 393248 | tf_op jit(solution)/shard_map/ppermute | solution.py:265
  86.4 2.2 %shard_map.71 = (bf16[768,128]{1,0:T(8,128)(2,1)S(1)}, bf16[768,128]{1,0:T(8,128)(2,1)S(1)}, bf16[768,128]{1,0:T(8,128)(2,1)S(1)}, bf16[768,128]{1,0:T(8,128)(2,1)S(1)}) custom-call(s32[4]{0:T(128)S(1)} %pad_add_fusion.place, s32[32,48]{1,0:T(8,128)S(1)} %bitcast.29, bf16[768,1536]{1,0:T(8,128)(2,1)S(1)} %get-tuple-element.21.green.rest_2_, ...), custom_call_target="tpu_custom_call" | custom-call | bytes 1024 | tf_op jit(solution)/shard_map/pallas_call | solution.py:38
  92.2 2.6 %collective-permute-done.21.rest_8_.rest_1_ = bf16[768,128]{1,0:T(8,128)(2,1)S(1)} collective-permute-done((bf16[768,128]{1,0:T(8,128)(2,1)S(1)}, bf16[768,128]{1,0:T(8,128)(2,1)S(1)}, u32[]{:S(2)}, u32[]{:S(2)}) %collective-permute-start.21) | collective-permute-done | bytes 196640 | tf_op jit(solution)/shard_map/ppermute | solution.py:261
  96.7 2.7 %shard_map.76 = (bf16[896,128]{1,0:T(8,128)(2,1)S(1)}, bf16[896,128]{1,0:T(8,128)(2,1)S(1)}, bf16[1664,128]{1,0:T(8,128)(2,1)S(1)}, bf16[896,128]{1,0:T(8,128)(2,1)S(1)}) custom-call(s32[4]{0:T(128)S(1)} %pad_add_fusion.place, s32[32,48]{1,0:T(8,128)S(1)} %bitcast.30, bf16[768,1536]{1,0:T(8,128)(2,1)S(1)} %get-tuple-element.29.rest_3_.green, ...), custom_call_target="tpu_custom_call" | custom-call | bytes 1024 | tf_op jit(solution)/shard_map/pallas_call | solution.py:38
  99.4 3.5 %collective-permute-start.27 = (bf16[1664,128]{1,0:T(8,128)(2,1)S(1)}, bf16[1664,128]{1,0:T(8,128)(2,1)S(1)}, u32[]{:S(2)}, u32[]{:S(2)}) collective-permute-start(bf16[1664,128]{1,0:T(8,128)(2,1)S(1)} %get-tuple-element.36), channel_id=1, source_target_pairs={{0,4},{1,5},{2,6},{3,7},{4,0},{5,1},{6,2},{7,3},{8,12},{9,13},{10,... | collective-permute-start | bytes 1277960 | tf_op jit(solution)/shard_map/ppermute | solution.py:261
  105.0 7.3 %collective-permute-done.26.rest_4_ = bf16[896,128]{1,0:T(8,128)(2,1)S(1)} collective-permute-done((bf16[896,128]{1,0:T(8,128)(2,1)S(1)}, bf16[896,128]{1,0:T(8,128)(2,1)S(1)}, u32[]{:S(2)}, u32[]{:S(2)}) %collective-permute-start.26) | collective-permute-done | bytes 229408 | tf_op jit(solution)/shard_map/ppermute | solution.py:261
  112.3 2.6 %shard_map.77 = (bf16[4,8,192,128]{3,2,1,0:T(8,128)(2,1)}, f32[128,128]{1,0:T(8,128)}) custom-call(s32[4]{0:T(128)S(1)} %pad_add_fusion.place, f32[128,128]{1,0:T(8,128)S(1)} %bitcast.31, bf16[768,128]{1,0:T(8,128)(2,1)S(1)} %get-tuple-element.30.rest_0_, bf16[768,128]{1,0:T(8,128)(2,1)S(1)} %collective-permute-done.21.rest_8_.rest_1_, ...), custom_call_target="tpu_custom_call" | custom-call | bytes 1024 | tf_op jit(solution)/shard_map/pallas_call | solution.py:38
  (64 shorter events, 35.9 us)
Async XLA Ops:
  8.8 11.4 %collective-permute-start.3 = (bf16[4,384,128]{2,1,0:T(8,128)(2,1)S(1)}, bf16[4,384,128]{2,1,0:T(8,128)(2,1)S(1)}, u32[]{:S(2)}, u32[]{:S(2)}) collective-permute-start(bf16[4,384,128]{2,1,0:T(8,128)(2,1)S(1)} %bitcast.19), channel_id=1, source_target_pairs={{0,6},{1,3},{2,0},{3,5},{4,2},{5,7},{6,4},{7,1},{8,14},{9,11},{10,... | collective-permute-start | bytes 1179656 | tf_op jit(solution)/shard_map/ppermute | solution.py:265
  11.0 12.6 %collective-permute-start.4 = (bf16[4,384,128]{2,1,0:T(8,128)(2,1)S(1)}, bf16[4,384,128]{2,1,0:T(8,128)(2,1)S(1)}, u32[]{:S(2)}, u32[]{:S(2)}) collective-permute-start(bf16[4,384,128]{2,1,0:T(8,128)(2,1)S(1)} %bitcast.20), channel_id=1, source_target_pairs={{0,2},{1,7},{2,4},{3,1},{4,6},{5,3},{6,0},{7,5},{8,10},{9,15},{10,... | collective-permute-start | bytes 1179656 | tf_op jit(solution)/shard_map/ppermute | solution.py:265
  12.0 13.9 %collective-permute-start.16 = (bf16[4,2,192,128]{3,2,1,0:T(8,128)(2,1)S(1)}, bf16[4,2,192,128]{3,2,1,0:T(8,128)(2,1)S(1)}, u32[]{:S(2)}, u32[]{:S(2)}) collective-permute-start(bf16[4,2,192,128]{3,2,1,0:T(8,128)(2,1)S(1)} %get-tuple-element.27), channel_id=1, source_target_pairs={{0,24},{1,9},{2,26},{3,11},{4,28},{5,13},{6,30},{7,15},{8,0},{9,17... | collective-permute-start | bytes 1179656 | tf_op jit(solution)/shard_map/ppermute | solution.py:269
  14.7 11.3 %collective-permute-start.15 = (bf16[4,2,192,128]{3,2,1,0:T(8,128)(2,1)S(1)}, bf16[4,2,192,128]{3,2,1,0:T(8,128)(2,1)S(1)}, u32[]{:S(2)}, u32[]{:S(2)}) collective-permute-start(bf16[4,2,192,128]{3,2,1,0:T(8,128)(2,1)S(1)} %shard_map.61.after), channel_id=1, source_target_pairs={{0,8},{1,25},{2,10},{3,27},{4,12},{5,29},{6,14},{7,31},{8,16},{9,1... | collective-permute-start | bytes 1179656 | tf_op jit(solution)/shard_map/ppermute | solution.py:269
  20.2 11.6 %collective-permute-start.14 = (bf16[4,384,128]{2,1,0:T(8,128)(2,1)S(1)}, bf16[4,384,128]{2,1,0:T(8,128)(2,1)S(1)}, u32[]{:S(2)}, u32[]{:S(2)}) collective-permute-start(bf16[4,384,128]{2,1,0:T(8,128)(2,1)S(1)} %collective-permute-done.3.rest_0_.rest_1_), channel_id=1, source_target_pairs={{0,6},{1,3},{2,0},{3,5},{4,2},{5,7},{6,4},{7,1},{8,14},{9,11},{10,... | collective-permute-start | bytes 1179656 | tf_op jit(solution)/shard_map/ppermute | solution.py:265
  23.9 11.6 %collective-permute-start.6 = (bf16[4,384,128]{2,1,0:T(8,128)(2,1)S(1)}, bf16[4,384,128]{2,1,0:T(8,128)(2,1)S(1)}, u32[]{:S(2)}, u32[]{:S(2)}) collective-permute-start(bf16[4,384,128]{2,1,0:T(8,128)(2,1)S(1)} %shard_map.63), channel_id=1, source_target_pairs={{0,2},{1,7},{2,4},{3,1},{4,6},{5,3},{6,0},{7,5},{8,10},{9,15},{10,... | collective-permute-start | bytes 1179656 | tf_op jit(solution)/shard_map/ppermute | solution.py:265
  24.0 12.4 %collective-permute-start.5 = (bf16[4,384,128]{2,1,0:T(8,128)(2,1)S(1)}, bf16[4,384,128]{2,1,0:T(8,128)(2,1)S(1)}, u32[]{:S(2)}, u32[]{:S(2)}) collective-permute-start(bf16[4,384,128]{2,1,0:T(8,128)(2,1)S(1)} %shard_map.63), channel_id=1, source_target_pairs={{0,6},{1,3},{2,0},{3,5},{4,2},{5,7},{6,4},{7,1},{8,14},{9,11},{10,... | collective-permute-start | bytes 1179656 | tf_op jit(solution)/shard_map/ppermute | solution.py:265
  26.2 13.7 %collective-permute-start.18 = (bf16[4,2,192,128]{3,2,1,0:T(8,128)(2,1)S(1)}, bf16[4,2,192,128]{3,2,1,0:T(8,128)(2,1)S(1)}, u32[]{:S(2)}, u32[]{:S(2)}) collective-permute-start(bf16[4,2,192,128]{3,2,1,0:T(8,128)(2,1)S(1)} %shard_map.67), channel_id=1, source_target_pairs={{0,16},{1,17},{2,18},{3,19},{4,20},{5,21},{6,22},{7,23},{8,24},{9,... | collective-permute-start | bytes 1179656 | tf_op jit(solution)/shard_map/ppermute | solution.py:269
  33.2 17.9 %collective-permute-start.17 = (bf16[4,768,128]{2,1,0:T(8,128)(2,1)S(1)}, bf16[4,768,128]{2,1,0:T(8,128)(2,1)S(1)}, u32[]{:S(2)}, u32[]{:S(2)}) collective-permute-start(bf16[4,768,128]{2,1,0:T(8,128)(2,1)S(1)} %shard_map.66.rest_7_), channel_id=1, source_target_pairs={{0,24},{1,9},{2,26},{3,11},{4,28},{5,13},{6,30},{7,15},{8,0},{9,17... | collective-permute-start | bytes 2359304 | tf_op jit(solution)/shard_map/ppermute | solution.py:269
  41.3 14.3 %collective-permute-start.23 = (bf16[4,768,128]{2,1,0:T(8,128)(2,1)S(1)}, bf16[4,768,128]{2,1,0:T(8,128)(2,1)S(1)}, u32[]{:S(2)}, u32[]{:S(2)}) collective-permute-start(bf16[4,768,128]{2,1,0:T(8,128)(2,1)S(1)} %shard_map.72), channel_id=1, source_target_pairs={{0,24},{1,9},{2,26},{3,11},{4,28},{5,13},{6,30},{7,15},{8,0},{9,17... | collective-permute-start | bytes 2359304 | tf_op jit(solution)/shard_map/ppermute | solution.py:269
  41.7 9.4 %collective-permute-start.13 = (bf16[4,384,128]{2,1,0:T(8,128)(2,1)S(1)}, bf16[4,384,128]{2,1,0:T(8,128)(2,1)S(1)}, u32[]{:S(2)}, u32[]{:S(2)}) collective-permute-start(bf16[4,384,128]{2,1,0:T(8,128)(2,1)S(1)} %collective-permute-done.5.rest_0_.rest_1_.rest_4_), channel_id=1, source_target_pairs={{0,6},{1,3},{2,0},{3,5},{4,2},{5,7},{6,4},{7,1},{8,14},{9,11},{10,... | collective-permute-start | bytes 1179656 | tf_op jit(solution)/shard_map/ppermute | solution.py:265
  45.0 10.6 %collective-permute-start.8 = (bf16[4,384,128]{2,1,0:T(8,128)(2,1)S(1)}, bf16[4,384,128]{2,1,0:T(8,128)(2,1)S(1)}, u32[]{:S(2)}, u32[]{:S(2)}) collective-permute-start(bf16[4,384,128]{2,1,0:T(8,128)(2,1)S(1)} %shard_map.64), channel_id=1, source_target_pairs={{0,2},{1,7},{2,4},{3,1},{4,6},{5,3},{6,0},{7,5},{8,10},{9,15},{10,... | collective-permute-start | bytes 1179656 | tf_op jit(solution)/shard_map/ppermute | solution.py:265
  45.0 10.5 %collective-permute-start.7 = (bf16[4,384,128]{2,1,0:T(8,128)(2,1)S(1)}, bf16[4,384,128]{2,1,0:T(8,128)(2,1)S(1)}, u32[]{:S(2)}, u32[]{:S(2)}) collective-permute-start(bf16[4,384,128]{2,1,0:T(8,128)(2,1)S(1)} %shard_map.64), channel_id=1, source_target_pairs={{0,6},{1,3},{2,0},{3,5},{4,2},{5,7},{6,4},{7,1},{8,14},{9,11},{10,... | collective-permute-start | bytes 1179656 | tf_op jit(solution)/shard_map/ppermute | solution.py:265
  52.5 16.4 %collective-permute-start.19 = (bf16[4,768,128]{2,1,0:T(8,128)(2,1)S(1)}, bf16[4,768,128]{2,1,0:T(8,128)(2,1)S(1)}, u32[]{:S(2)}, u32[]{:S(2)}) collective-permute-start(bf16[4,768,128]{2,1,0:T(8,128)(2,1)S(1)} %shard_map.69), channel_id=1, source_target_pairs={{0,24},{1,9},{2,26},{3,11},{4,28},{5,13},{6,30},{7,15},{8,0},{9,17... | collective-permute-start | bytes 2359304 | tf_op jit(solution)/shard_map/ppermute | solution.py:269
  56.9 16.5 %collective-permute-start.24 = (bf16[4,768,128]{2,1,0:T(8,128)(2,1)S(1)}, bf16[4,768,128]{2,1,0:T(8,128)(2,1)S(1)}, u32[]{:S(2)}, u32[]{:S(2)}) collective-permute-start(bf16[4,768,128]{2,1,0:T(8,128)(2,1)S(1)} %shard_map.73), channel_id=1, source_target_pairs={{0,24},{1,9},{2,26},{3,11},{4,28},{5,13},{6,30},{7,15},{8,0},{9,17... | collective-permute-start | bytes 2359304 | tf_op jit(solution)/shard_map/ppermute | solution.py:269
  59.7 9.2 %collective-permute-start.12 = (bf16[4,384,128]{2,1,0:T(8,128)(2,1)S(1)}, bf16[4,384,128]{2,1,0:T(8,128)(2,1)S(1)}, u32[]{:S(2)}, u32[]{:S(2)}) collective-permute-start(bf16[4,384,128]{2,1,0:T(8,128)(2,1)S(1)} %collective-permute-done.7.rest_0_.rest_1_.rest_5_), channel_id=1, source_target_pairs={{0,6},{1,3},{2,0},{3,5},{4,2},{5,7},{6,4},{7,1},{8,14},{9,11},{10,... | collective-permute-start | bytes 1179656 | tf_op jit(solution)/shard_map/ppermute | solution.py:265
  62.4 10.8 %collective-permute-start.11 = (bf16[4,384,128]{2,1,0:T(8,128)(2,1)S(1)}, bf16[4,384,128]{2,1,0:T(8,128)(2,1)S(1)}, u32[]{:S(2)}, u32[]{:S(2)}) collective-permute-start(bf16[4,384,128]{2,1,0:T(8,128)(2,1)S(1)} %shard_map.65), channel_id=1, source_target_pairs={{0,2},{1,7},{2,4},{3,1},{4,6},{5,3},{6,0},{7,5},{8,10},{9,15},{10,... | collective-permute-start | bytes 1179656 | tf_op jit(solution)/shard_map/ppermute | solution.py:265
  62.5 10.7 %collective-permute-start.9 = (bf16[4,384,128]{2,1,0:T(8,128)(2,1)S(1)}, bf16[4,384,128]{2,1,0:T(8,128)(2,1)S(1)}, u32[]{:S(2)}, u32[]{:S(2)}) collective-permute-start(bf16[4,384,128]{2,1,0:T(8,128)(2,1)S(1)} %shard_map.65), channel_id=1, source_target_pairs={{0,6},{1,3},{2,0},{3,5},{4,2},{5,7},{6,4},{7,1},{8,14},{9,11},{10,... | collective-permute-start | bytes 1179656 | tf_op jit(solution)/shard_map/ppermute | solution.py:265
  70.3 16.1 %collective-permute-start.20 = (bf16[4,768,128]{2,1,0:T(8,128)(2,1)S(1)}, bf16[4,768,128]{2,1,0:T(8,128)(2,1)S(1)}, u32[]{:S(2)}, u32[]{:S(2)}) collective-permute-start(bf16[4,768,128]{2,1,0:T(8,128)(2,1)S(1)} %shard_map.70), channel_id=1, source_target_pairs={{0,24},{1,9},{2,26},{3,11},{4,28},{5,13},{6,30},{7,15},{8,0},{9,17... | collective-permute-start | bytes 2359304 | tf_op jit(solution)/shard_map/ppermute | solution.py:269
  74.9 17.3 %collective-permute-start.25 = (bf16[4,768,128]{2,1,0:T(8,128)(2,1)S(1)}, bf16[4,768,128]{2,1,0:T(8,128)(2,1)S(1)}, u32[]{:S(2)}, u32[]{:S(2)}) collective-permute-start(bf16[4,768,128]{2,1,0:T(8,128)(2,1)S(1)} %shard_map.74), channel_id=1, source_target_pairs={{0,24},{1,9},{2,26},{3,11},{4,28},{5,13},{6,30},{7,15},{8,0},{9,17... | collective-permute-start | bytes 2359304 | tf_op jit(solution)/shard_map/ppermute | solution.py:269
  78.6 7.8 %collective-permute-start.10 = (bf16[4,384,128]{2,1,0:T(8,128)(2,1)S(1)}, bf16[4,384,128]{2,1,0:T(8,128)(2,1)S(1)}, u32[]{:S(2)}, u32[]{:S(2)}) collective-permute-start(bf16[4,384,128]{2,1,0:T(8,128)(2,1)S(1)} %collective-permute-done.9.rest_1_.rest_5_), channel_id=1, source_target_pairs={{0,6},{1,3},{2,0},{3,5},{4,2},{5,7},{6,4},{7,1},{8,14},{9,11},{10,... | collective-permute-start | bytes 1179656 | tf_op jit(solution)/shard_map/ppermute | solution.py:265
  99.4 12.8 %collective-permute-start.27 = (bf16[1664,128]{1,0:T(8,128)(2,1)S(1)}, bf16[1664,128]{1,0:T(8,128)(2,1)S(1)}, u32[]{:S(2)}, u32[]{:S(2)}) collective-permute-start(bf16[1664,128]{1,0:T(8,128)(2,1)S(1)} %get-tuple-element.36), channel_id=1, source_target_pairs={{0,4},{1,5},{2,6},{3,7},{4,0},{5,1},{6,2},{7,3},{8,12},{9,13},{10,... | collective-permute-start | bytes 1277960 | tf_op jit(solution)/shard_map/ppermute | solution.py:261
  103.0 9.3 %collective-permute-start.26 = (bf16[896,128]{1,0:T(8,128)(2,1)S(1)}, bf16[896,128]{1,0:T(8,128)(2,1)S(1)}, u32[]{:S(2)}, u32[]{:S(2)}) collective-permute-start(bf16[896,128]{1,0:T(8,128)(2,1)S(1)} %get-tuple-element.35), channel_id=1, source_target_pairs={{0,2},{1,3},{2,4},{3,5},{4,6},{5,7},{6,0},{7,1},{8,10},{9,11},{10,... | collective-permute-start | bytes 688136 | tf_op jit(solution)/shard_map/ppermute | solution.py:261
  103.0 9.3 %collective-permute-start.28 = (bf16[896,128]{1,0:T(8,128)(2,1)S(1)}, bf16[896,128]{1,0:T(8,128)(2,1)S(1)}, u32[]{:S(2)}, u32[]{:S(2)}) collective-permute-start(bf16[896,128]{1,0:T(8,128)(2,1)S(1)} %get-tuple-element.37), channel_id=1, source_target_pairs={{0,6},{1,7},{2,0},{3,1},{4,2},{5,3},{6,4},{7,5},{8,14},{9,15},{10,... | collective-permute-start | bytes 688136 | tf_op jit(solution)/shard_map/ppermute | solution.py:261
  (10 other events, 80.3 us)

commit v4 on v3

--- a/solution.py
+++ b/solution.py
@@ -220,7 +220,7 @@
 
 
 def final_kernel(place, pivot, *rest):
-    parts, (panel, diag, sems) = rest[:7], rest[7:]
+    parts, (panel, diag, block, sems) = rest[:7], rest[7:]
     y, k = place[1], place[2]
     sources = [
         (parts[0], 0, 0, 0),
@@ -243,7 +243,9 @@
     total = pivot[...]
     for source in parts[3:]:
         total += source[HALF : HALF + W, :].astype(F32)
-    diag[...] = total
+    block[...] = total
+    copies.append(pltpu.make_async_copy(block, diag, sems.at[len(copies)]))
+    copies[-1].start()
     for copy in copies:
         copy.wait()
 
@@ -392,8 +394,8 @@
         [((NR, NC, RD, W), BF16), ((W, W), F32)],
         (place, pivot_inverse.reshape(W, W), *parts),
         [SMEM, VMEM] + [ANY] * 3 + [VMEM] * 4,
-        [ANY, VMEM],
-        [dma((32,))],
+        [ANY, ANY],
+        [pltpu.VMEM((W, W), F32), dma((33,))],
     )
     return green_panel.reshape(ORDER, 1, W), green_diag.reshape(1, W, W)
 

time: 116 us -> 116 us (level)
  no operation moved by 1% of the time
where the time goes in v4:
time: 116 us; the launch traced here: 114 us
  starting transfers between devices  49.9 us (43%)
  waiting for transfers between devices  37.1 us (32%)
  Pallas kernels  24.1 us (21%)
  local copies, waits for them, and re-layouts  2.14 us (2%)
    pallas_call x19, Pallas kernels, call(): pl.pallas_call(kernel, out_shape=[jax.ShapeDtypeStruct(s, d) for s, d in...  24.1 us
    ppermute x9, starting transfers between devices, ring_x(): return lax.ppermute(v, ('row', 'col'), pairs)  21.7 us
    ppermute x12, waiting for transfers between devices, ring_y(): return lax.ppermute(v, 'col', pairs)  19.8 us
    ppermute x12, starting transfers between devices, ring_y(): return lax.ppermute(v, 'col', pairs)  19.3 us
    ppermute x5, waiting for transfers between devices, over_y(): return lax.ppermute(v, 'col', [(c, (c + 2 * d) % 8) for c in range(8)])  11.8 us
    ppermute x5, starting transfers between devices, over_y(): return lax.ppermute(v, 'col', [(c, (c + 2 * d) % 8) for c in range(8)])  8.2 us
    ppermute x9, waiting for transfers between devices, ring_x(): return lax.ppermute(v, ('row', 'col'), pairs)  3.73 us
  transfers between devices with their start and end apart: 29, of which 12 were waited for; matrix products, arithmetic and copies ran while one was open for 0% of the time, Pallas kernels for 17%

profile of v4, /device:TPU:8, one launch (start us, length us, event | category | flops | bytes accessed | tf_op | source)
XLA Modules:
  0.0 114.4 jit_solution(17552005873166839687)
XLA Ops:
  3.0 2.6 %shard_map.60 = (bf16[4,192,128]{2,1,0:T(8,128)(2,1)S(1)}, bf16[4,192,128]{2,1,0:T(8,128)(2,1)S(1)}, bf16[3,4,192,128]{3,2,1,0:T(8,128)(2,1)S(1)}, bf16[3,4,192,128]{3,2,1,0:T(8,128)(2,1)S(1)}) custom-call(s32[4]{0:T(128)S(1)} %pad_add_fusion.place, s32[32,48]{1,0:T(8,128)S(1)} %bitcast.28, bf16[192,32,128]{2,1,0:T(8,128)(2,1)S(1)} %copy-done.1), custom_call_target="tpu_custom_call" | custom-call | bytes 1024 | tf_op jit(solution)/shard_map/pallas_call | solution.py:38
  8.8 2.3 %collective-permute-start.3 = (bf16[4,384,128]{2,1,0:T(8,128)(2,1)S(1)}, bf16[4,384,128]{2,1,0:T(8,128)(2,1)S(1)}, u32[]{:S(2)}, u32[]{:S(2)}) collective-permute-start(bf16[4,384,128]{2,1,0:T(8,128)(2,1)S(1)} %bitcast.19), channel_id=1, source_target_pairs={{0,6},{1,3},{2,0},{3,5},{4,2},{5,7},{6,4},{7,1},{8,14},{9,11},{10,... | collective-permute-start | bytes 1179656 | tf_op jit(solution)/shard_map/ppermute | solution.py:267
  12.0 2.7 %collective-permute-start.16 = (bf16[4,2,192,128]{3,2,1,0:T(8,128)(2,1)S(1)}, bf16[4,2,192,128]{3,2,1,0:T(8,128)(2,1)S(1)}, u32[]{:S(2)}, u32[]{:S(2)}) collective-permute-start(bf16[4,2,192,128]{3,2,1,0:T(8,128)(2,1)S(1)} %get-tuple-element.27), channel_id=1, source_target_pairs={{0,24},{1,9},{2,26},{3,11},{4,28},{5,13},{6,30},{7,15},{8,0},{9,17... | collective-permute-start | bytes 1179656 | tf_op jit(solution)/shard_map/ppermute | solution.py:271
  14.7 5.5 %collective-permute-done.3.rest_0_.rest_1_ = bf16[4,384,128]{2,1,0:T(8,128)(2,1)S(1)} collective-permute-done((bf16[4,384,128]{2,1,0:T(8,128)(2,1)S(1)}, bf16[4,384,128]{2,1,0:T(8,128)(2,1)S(1)}, u32[]{:S(2)}, u32[]{:S(2)}) %collective-permute-start.3) | collective-permute-done | bytes 393248 | tf_op jit(solution)/shard_map/ppermute | solution.py:267
  20.2 2.3 %collective-permute-start.14 = (bf16[4,384,128]{2,1,0:T(8,128)(2,1)S(1)}, bf16[4,384,128]{2,1,0:T(8,128)(2,1)S(1)}, u32[]{:S(2)}, u32[]{:S(2)}) collective-permute-start(bf16[4,384,128]{2,1,0:T(8,128)(2,1)S(1)} %collective-permute-done.3.rest_0_.rest_1_), channel_id=1, source_target_pairs={{0,6},{1,3},{2,0},{3,5},{4,2},{5,7},{6,4},{7,1},{8,14},{9,11},{10,... | collective-permute-start | bytes 1179656 | tf_op jit(solution)/shard_map/ppermute | solution.py:267
  26.2 3.7 %collective-permute-start.18 = (bf16[4,2,192,128]{3,2,1,0:T(8,128)(2,1)S(1)}, bf16[4,2,192,128]{3,2,1,0:T(8,128)(2,1)S(1)}, u32[]{:S(2)}, u32[]{:S(2)}) collective-permute-start(bf16[4,2,192,128]{3,2,1,0:T(8,128)(2,1)S(1)} %shard_map.67), channel_id=1, source_target_pairs={{0,16},{1,17},{2,18},{3,19},{4,20},{5,21},{6,22},{7,23},{8,24},{9,... | collective-permute-start | bytes 1179656 | tf_op jit(solution)/shard_map/ppermute | solution.py:271
  33.2 2.3 %collective-permute-start.17 = (bf16[4,768,128]{2,1,0:T(8,128)(2,1)S(1)}, bf16[4,768,128]{2,1,0:T(8,128)(2,1)S(1)}, u32[]{:S(2)}, u32[]{:S(2)}) collective-permute-start(bf16[4,768,128]{2,1,0:T(8,128)(2,1)S(1)} %shard_map.66.rest_7_), channel_id=1, source_target_pairs={{0,24},{1,9},{2,26},{3,11},{4,28},{5,13},{6,30},{7,15},{8,0},{9,17... | collective-permute-start | bytes 2359304 | tf_op jit(solution)/shard_map/ppermute | solution.py:271
  36.4 3.5 %collective-permute-done.18.x1.rest_6_ = bf16[4,2,192,128]{3,2,1,0:T(8,128)(2,1)S(1)} collective-permute-done((bf16[4,2,192,128]{3,2,1,0:T(8,128)(2,1)S(1)}, bf16[4,2,192,128]{3,2,1,0:T(8,128)(2,1)S(1)}, u32[]{:S(2)}, u32[]{:S(2)}) %collective-permute-start.18) | collective-permute-done | bytes 393248 | tf_op jit(solution)/shard_map/ppermute | solution.py:271
  41.7 3.1 %collective-permute-start.13 = (bf16[4,384,128]{2,1,0:T(8,128)(2,1)S(1)}, bf16[4,384,128]{2,1,0:T(8,128)(2,1)S(1)}, u32[]{:S(2)}, u32[]{:S(2)}) collective-permute-start(bf16[4,384,128]{2,1,0:T(8,128)(2,1)S(1)} %collective-permute-done.5.rest_0_.rest_1_.rest_4_), channel_id=1, source_target_pairs={{0,6},{1,3},{2,0},{3,5},{4,2},{5,7},{6,4},{7,1},{8,14},{9,11},{10,... | collective-permute-start | bytes 1179656 | tf_op jit(solution)/shard_map/ppermute | solution.py:267
  48.9 2.2 %collective-permute-done.13.rest_2_ = bf16[4,384,128]{2,1,0:T(8,128)(2,1)S(1)} collective-permute-done((bf16[4,384,128]{2,1,0:T(8,128)(2,1)S(1)}, bf16[4,384,128]{2,1,0:T(8,128)(2,1)S(1)}, u32[]{:S(2)}, u32[]{:S(2)}) %collective-permute-start.13) | collective-permute-done | bytes 393248 | tf_op jit(solution)/shard_map/ppermute | solution.py:267
  52.5 3.1 %collective-permute-start.19 = (bf16[4,768,128]{2,1,0:T(8,128)(2,1)S(1)}, bf16[4,768,128]{2,1,0:T(8,128)(2,1)S(1)}, u32[]{:S(2)}, u32[]{:S(2)}) collective-permute-start(bf16[4,768,128]{2,1,0:T(8,128)(2,1)S(1)} %shard_map.69), channel_id=1, source_target_pairs={{0,24},{1,9},{2,26},{3,11},{4,28},{5,13},{6,30},{7,15},{8,0},{9,17... | collective-permute-start | bytes 2359304 | tf_op jit(solution)/shard_map/ppermute | solution.py:271
  56.9 2.8 %collective-permute-start.24 = (bf16[4,768,128]{2,1,0:T(8,128)(2,1)S(1)}, bf16[4,768,128]{2,1,0:T(8,128)(2,1)S(1)}, u32[]{:S(2)}, u32[]{:S(2)}) collective-permute-start(bf16[4,768,128]{2,1,0:T(8,128)(2,1)S(1)} %shard_map.73), channel_id=1, source_target_pairs={{0,24},{1,9},{2,26},{3,11},{4,28},{5,13},{6,30},{7,15},{8,0},{9,17... | collective-permute-start | bytes 2359304 | tf_op jit(solution)/shard_map/ppermute | solution.py:271
  59.7 2.5 %collective-permute-start.12 = (bf16[4,384,128]{2,1,0:T(8,128)(2,1)S(1)}, bf16[4,384,128]{2,1,0:T(8,128)(2,1)S(1)}, u32[]{:S(2)}, u32[]{:S(2)}) collective-permute-start(bf16[4,384,128]{2,1,0:T(8,128)(2,1)S(1)} %collective-permute-done.7.rest_0_.rest_1_.rest_5_), channel_id=1, source_target_pairs={{0,6},{1,3},{2,0},{3,5},{4,2},{5,7},{6,4},{7,1},{8,14},{9,11},{10,... | collective-permute-start | bytes 1179656 | tf_op jit(solution)/shard_map/ppermute | solution.py:267
  62.5 2.4 %collective-permute-start.9 = (bf16[4,384,128]{2,1,0:T(8,128)(2,1)S(1)}, bf16[4,384,128]{2,1,0:T(8,128)(2,1)S(1)}, u32[]{:S(2)}, u32[]{:S(2)}) collective-permute-start(bf16[4,384,128]{2,1,0:T(8,128)(2,1)S(1)} %shard_map.65), channel_id=1, source_target_pairs={{0,6},{1,3},{2,0},{3,5},{4,2},{5,7},{6,4},{7,1},{8,14},{9,11},{10,... | collective-permute-start | bytes 1179656 | tf_op jit(solution)/shard_map/ppermute | solution.py:267
  64.9 4.0 %collective-permute-done.12.rest_2_ = bf16[4,384,128]{2,1,0:T(8,128)(2,1)S(1)} collective-permute-done((bf16[4,384,128]{2,1,0:T(8,128)(2,1)S(1)}, bf16[4,384,128]{2,1,0:T(8,128)(2,1)S(1)}, u32[]{:S(2)}, u32[]{:S(2)}) %collective-permute-start.12) | collective-permute-done | bytes 393248 | tf_op jit(solution)/shard_map/ppermute | solution.py:267
  70.3 2.9 %collective-permute-start.20 = (bf16[4,768,128]{2,1,0:T(8,128)(2,1)S(1)}, bf16[4,768,128]{2,1,0:T(8,128)(2,1)S(1)}, u32[]{:S(2)}, u32[]{:S(2)}) collective-permute-start(bf16[4,768,128]{2,1,0:T(8,128)(2,1)S(1)} %shard_map.70), channel_id=1, source_target_pairs={{0,24},{1,9},{2,26},{3,11},{4,28},{5,13},{6,30},{7,15},{8,0},{9,17... | collective-permute-start | bytes 2359304 | tf_op jit(solution)/shard_map/ppermute | solution.py:271
  74.9 3.8 %collective-permute-start.25 = (bf16[4,768,128]{2,1,0:T(8,128)(2,1)S(1)}, bf16[4,768,128]{2,1,0:T(8,128)(2,1)S(1)}, u32[]{:S(2)}, u32[]{:S(2)}) collective-permute-start(bf16[4,768,128]{2,1,0:T(8,128)(2,1)S(1)} %shard_map.74), channel_id=1, source_target_pairs={{0,24},{1,9},{2,26},{3,11},{4,28},{5,13},{6,30},{7,15},{8,0},{9,17... | collective-permute-start | bytes 2359304 | tf_op jit(solution)/shard_map/ppermute | solution.py:271
  78.6 2.5 %collective-permute-start.10 = (bf16[4,384,128]{2,1,0:T(8,128)(2,1)S(1)}, bf16[4,384,128]{2,1,0:T(8,128)(2,1)S(1)}, u32[]{:S(2)}, u32[]{:S(2)}) collective-permute-start(bf16[4,384,128]{2,1,0:T(8,128)(2,1)S(1)} %collective-permute-done.9.rest_1_.rest_5_), channel_id=1, source_target_pairs={{0,6},{1,3},{2,0},{3,5},{4,2},{5,7},{6,4},{7,1},{8,14},{9,11},{10,... | collective-permute-start | bytes 1179656 | tf_op jit(solution)/shard_map/ppermute | solution.py:267
  81.1 5.3 %collective-permute-done.10.rest_2_ = bf16[4,384,128]{2,1,0:T(8,128)(2,1)S(1)} collective-permute-done((bf16[4,384,128]{2,1,0:T(8,128)(2,1)S(1)}, bf16[4,384,128]{2,1,0:T(8,128)(2,1)S(1)}, u32[]{:S(2)}, u32[]{:S(2)}) %collective-permute-start.10) | collective-permute-done | bytes 393248 | tf_op jit(solution)/shard_map/ppermute | solution.py:267
  86.4 2.2 %shard_map.71 = (bf16[768,128]{1,0:T(8,128)(2,1)S(1)}, bf16[768,128]{1,0:T(8,128)(2,1)S(1)}, bf16[768,128]{1,0:T(8,128)(2,1)S(1)}, bf16[768,128]{1,0:T(8,128)(2,1)S(1)}) custom-call(s32[4]{0:T(128)S(1)} %pad_add_fusion.place, s32[32,48]{1,0:T(8,128)S(1)} %bitcast.29, bf16[768,1536]{1,0:T(8,128)(2,1)S(1)} %get-tuple-element.21.green.rest_2_, ...), custom_call_target="tpu_custom_call" | custom-call | bytes 1024 | tf_op jit(solution)/shard_map/pallas_call | solution.py:38
  92.2 2.6 %collective-permute-done.21.rest_8_.rest_1_ = bf16[768,128]{1,0:T(8,128)(2,1)S(1)} collective-permute-done((bf16[768,128]{1,0:T(8,128)(2,1)S(1)}, bf16[768,128]{1,0:T(8,128)(2,1)S(1)}, u32[]{:S(2)}, u32[]{:S(2)}) %collective-permute-start.21) | collective-permute-done | bytes 196640 | tf_op jit(solution)/shard_map/ppermute | solution.py:263
  96.7 2.7 %shard_map.76 = (bf16[896,128]{1,0:T(8,128)(2,1)S(1)}, bf16[896,128]{1,0:T(8,128)(2,1)S(1)}, bf16[1664,128]{1,0:T(8,128)(2,1)S(1)}, bf16[896,128]{1,0:T(8,128)(2,1)S(1)}) custom-call(s32[4]{0:T(128)S(1)} %pad_add_fusion.place, s32[32,48]{1,0:T(8,128)S(1)} %bitcast.30, bf16[768,1536]{1,0:T(8,128)(2,1)S(1)} %get-tuple-element.29.rest_3_.green, ...), custom_call_target="tpu_custom_call" | custom-call | bytes 1024 | tf_op jit(solution)/shard_map/pallas_call | solution.py:38
  99.4 3.5 %collective-permute-start.27 = (bf16[1664,128]{1,0:T(8,128)(2,1)S(1)}, bf16[1664,128]{1,0:T(8,128)(2,1)S(1)}, u32[]{:S(2)}, u32[]{:S(2)}) collective-permute-start(bf16[1664,128]{1,0:T(8,128)(2,1)S(1)} %get-tuple-element.36), channel_id=1, source_target_pairs={{0,4},{1,5},{2,6},{3,7},{4,0},{5,1},{6,2},{7,3},{8,12},{9,13},{10,... | collective-permute-start | bytes 1277960 | tf_op jit(solution)/shard_map/ppermute | solution.py:263
  105.0 7.3 %collective-permute-done.26.rest_4_ = bf16[896,128]{1,0:T(8,128)(2,1)S(1)} collective-permute-done((bf16[896,128]{1,0:T(8,128)(2,1)S(1)}, bf16[896,128]{1,0:T(8,128)(2,1)S(1)}, u32[]{:S(2)}, u32[]{:S(2)}) %collective-permute-start.26) | collective-permute-done | bytes 229408 | tf_op jit(solution)/shard_map/ppermute | solution.py:263
  (64 shorter events, 35.7 us)
Async XLA Ops:
  8.8 11.4 %collective-permute-start.3 = (bf16[4,384,128]{2,1,0:T(8,128)(2,1)S(1)}, bf16[4,384,128]{2,1,0:T(8,128)(2,1)S(1)}, u32[]{:S(2)}, u32[]{:S(2)}) collective-permute-start(bf16[4,384,128]{2,1,0:T(8,128)(2,1)S(1)} %bitcast.19), channel_id=1, source_target_pairs={{0,6},{1,3},{2,0},{3,5},{4,2},{5,7},{6,4},{7,1},{8,14},{9,11},{10,... | collective-permute-start | bytes 1179656 | tf_op jit(solution)/shard_map/ppermute | solution.py:267
  11.0 12.6 %collective-permute-start.4 = (bf16[4,384,128]{2,1,0:T(8,128)(2,1)S(1)}, bf16[4,384,128]{2,1,0:T(8,128)(2,1)S(1)}, u32[]{:S(2)}, u32[]{:S(2)}) collective-permute-start(bf16[4,384,128]{2,1,0:T(8,128)(2,1)S(1)} %bitcast.20), channel_id=1, source_target_pairs={{0,2},{1,7},{2,4},{3,1},{4,6},{5,3},{6,0},{7,5},{8,10},{9,15},{10,... | collective-permute-start | bytes 1179656 | tf_op jit(solution)/shard_map/ppermute | solution.py:267
  12.0 13.9 %collective-permute-start.16 = (bf16[4,2,192,128]{3,2,1,0:T(8,128)(2,1)S(1)}, bf16[4,2,192,128]{3,2,1,0:T(8,128)(2,1)S(1)}, u32[]{:S(2)}, u32[]{:S(2)}) collective-permute-start(bf16[4,2,192,128]{3,2,1,0:T(8,128)(2,1)S(1)} %get-tuple-element.27), channel_id=1, source_target_pairs={{0,24},{1,9},{2,26},{3,11},{4,28},{5,13},{6,30},{7,15},{8,0},{9,17... | collective-permute-start | bytes 1179656 | tf_op jit(solution)/shard_map/ppermute | solution.py:271
  14.7 11.3 %collective-permute-start.15 = (bf16[4,2,192,128]{3,2,1,0:T(8,128)(2,1)S(1)}, bf16[4,2,192,128]{3,2,1,0:T(8,128)(2,1)S(1)}, u32[]{:S(2)}, u32[]{:S(2)}) collective-permute-start(bf16[4,2,192,128]{3,2,1,0:T(8,128)(2,1)S(1)} %shard_map.61.after), channel_id=1, source_target_pairs={{0,8},{1,25},{2,10},{3,27},{4,12},{5,29},{6,14},{7,31},{8,16},{9,1... | collective-permute-start | bytes 1179656 | tf_op jit(solution)/shard_map/ppermute | solution.py:271
  20.2 11.6 %collective-permute-start.14 = (bf16[4,384,128]{2,1,0:T(8,128)(2,1)S(1)}, bf16[4,384,128]{2,1,0:T(8,128)(2,1)S(1)}, u32[]{:S(2)}, u32[]{:S(2)}) collective-permute-start(bf16[4,384,128]{2,1,0:T(8,128)(2,1)S(1)} %collective-permute-done.3.rest_0_.rest_1_), channel_id=1, source_target_pairs={{0,6},{1,3},{2,0},{3,5},{4,2},{5,7},{6,4},{7,1},{8,14},{9,11},{10,... | collective-permute-start | bytes 1179656 | tf_op jit(solution)/shard_map/ppermute | solution.py:267
  23.9 11.6 %collective-permute-start.6 = (bf16[4,384,128]{2,1,0:T(8,128)(2,1)S(1)}, bf16[4,384,128]{2,1,0:T(8,128)(2,1)S(1)}, u32[]{:S(2)}, u32[]{:S(2)}) collective-permute-start(bf16[4,384,128]{2,1,0:T(8,128)(2,1)S(1)} %shard_map.63), channel_id=1, source_target_pairs={{0,2},{1,7},{2,4},{3,1},{4,6},{5,3},{6,0},{7,5},{8,10},{9,15},{10,... | collective-permute-start | bytes 1179656 | tf_op jit(solution)/shard_map/ppermute | solution.py:267
  24.0 12.4 %collective-permute-start.5 = (bf16[4,384,128]{2,1,0:T(8,128)(2,1)S(1)}, bf16[4,384,128]{2,1,0:T(8,128)(2,1)S(1)}, u32[]{:S(2)}, u32[]{:S(2)}) collective-permute-start(bf16[4,384,128]{2,1,0:T(8,128)(2,1)S(1)} %shard_map.63), channel_id=1, source_target_pairs={{0,6},{1,3},{2,0},{3,5},{4,2},{5,7},{6,4},{7,1},{8,14},{9,11},{10,... | collective-permute-start | bytes 1179656 | tf_op jit(solution)/shard_map/ppermute | solution.py:267
  26.2 13.7 %collective-permute-start.18 = (bf16[4,2,192,128]{3,2,1,0:T(8,128)(2,1)S(1)}, bf16[4,2,192,128]{3,2,1,0:T(8,128)(2,1)S(1)}, u32[]{:S(2)}, u32[]{:S(2)}) collective-permute-start(bf16[4,2,192,128]{3,2,1,0:T(8,128)(2,1)S(1)} %shard_map.67), channel_id=1, source_target_pairs={{0,16},{1,17},{2,18},{3,19},{4,20},{5,21},{6,22},{7,23},{8,24},{9,... | collective-permute-start | bytes 1179656 | tf_op jit(solution)/shard_map/ppermute | solution.py:271
  33.2 17.9 %collective-permute-start.17 = (bf16[4,768,128]{2,1,0:T(8,128)(2,1)S(1)}, bf16[4,768,128]{2,1,0:T(8,128)(2,1)S(1)}, u32[]{:S(2)}, u32[]{:S(2)}) collective-permute-start(bf16[4,768,128]{2,1,0:T(8,128)(2,1)S(1)} %shard_map.66.rest_7_), channel_id=1, source_target_pairs={{0,24},{1,9},{2,26},{3,11},{4,28},{5,13},{6,30},{7,15},{8,0},{9,17... | collective-permute-start | bytes 2359304 | tf_op jit(solution)/shard_map/ppermute | solution.py:271
  41.3 14.3 %collective-permute-start.23 = (bf16[4,768,128]{2,1,0:T(8,128)(2,1)S(1)}, bf16[4,768,128]{2,1,0:T(8,128)(2,1)S(1)}, u32[]{:S(2)}, u32[]{:S(2)}) collective-permute-start(bf16[4,768,128]{2,1,0:T(8,128)(2,1)S(1)} %shard_map.72), channel_id=1, source_target_pairs={{0,24},{1,9},{2,26},{3,11},{4,28},{5,13},{6,30},{7,15},{8,0},{9,17... | collective-permute-start | bytes 2359304 | tf_op jit(solution)/shard_map/ppermute | solution.py:271
  41.7 9.4 %collective-permute-start.13 = (bf16[4,384,128]{2,1,0:T(8,128)(2,1)S(1)}, bf16[4,384,128]{2,1,0:T(8,128)(2,1)S(1)}, u32[]{:S(2)}, u32[]{:S(2)}) collective-permute-start(bf16[4,384,128]{2,1,0:T(8,128)(2,1)S(1)} %collective-permute-done.5.rest_0_.rest_1_.rest_4_), channel_id=1, source_target_pairs={{0,6},{1,3},{2,0},{3,5},{4,2},{5,7},{6,4},{7,1},{8,14},{9,11},{10,... | collective-permute-start | bytes 1179656 | tf_op jit(solution)/shard_map/ppermute | solution.py:267
  45.0 10.6 %collective-permute-start.8 = (bf16[4,384,128]{2,1,0:T(8,128)(2,1)S(1)}, bf16[4,384,128]{2,1,0:T(8,128)(2,1)S(1)}, u32[]{:S(2)}, u32[]{:S(2)}) collective-permute-start(bf16[4,384,128]{2,1,0:T(8,128)(2,1)S(1)} %shard_map.64), channel_id=1, source_target_pairs={{0,2},{1,7},{2,4},{3,1},{4,6},{5,3},{6,0},{7,5},{8,10},{9,15},{10,... | collective-permute-start | bytes 1179656 | tf_op jit(solution)/shard_map/ppermute | solution.py:267
  45.0 10.5 %collective-permute-start.7 = (bf16[4,384,128]{2,1,0:T(8,128)(2,1)S(1)}, bf16[4,384,128]{2,1,0:T(8,128)(2,1)S(1)}, u32[]{:S(2)}, u32[]{:S(2)}) collective-permute-start(bf16[4,384,128]{2,1,0:T(8,128)(2,1)S(1)} %shard_map.64), channel_id=1, source_target_pairs={{0,6},{1,3},{2,0},{3,5},{4,2},{5,7},{6,4},{7,1},{8,14},{9,11},{10,... | collective-permute-start | bytes 1179656 | tf_op jit(solution)/shard_map/ppermute | solution.py:267
  52.5 16.4 %collective-permute-start.19 = (bf16[4,768,128]{2,1,0:T(8,128)(2,1)S(1)}, bf16[4,768,128]{2,1,0:T(8,128)(2,1)S(1)}, u32[]{:S(2)}, u32[]{:S(2)}) collective-permute-start(bf16[4,768,128]{2,1,0:T(8,128)(2,1)S(1)} %shard_map.69), channel_id=1, source_target_pairs={{0,24},{1,9},{2,26},{3,11},{4,28},{5,13},{6,30},{7,15},{8,0},{9,17... | collective-permute-start | bytes 2359304 | tf_op jit(solution)/shard_map/ppermute | solution.py:271
  56.9 16.5 %collective-permute-start.24 = (bf16[4,768,128]{2,1,0:T(8,128)(2,1)S(1)}, bf16[4,768,128]{2,1,0:T(8,128)(2,1)S(1)}, u32[]{:S(2)}, u32[]{:S(2)}) collective-permute-start(bf16[4,768,128]{2,1,0:T(8,128)(2,1)S(1)} %shard_map.73), channel_id=1, source_target_pairs={{0,24},{1,9},{2,26},{3,11},{4,28},{5,13},{6,30},{7,15},{8,0},{9,17... | collective-permute-start | bytes 2359304 | tf_op jit(solution)/shard_map/ppermute | solution.py:271
  59.7 9.2 %collective-permute-start.12 = (bf16[4,384,128]{2,1,0:T(8,128)(2,1)S(1)}, bf16[4,384,128]{2,1,0:T(8,128)(2,1)S(1)}, u32[]{:S(2)}, u32[]{:S(2)}) collective-permute-start(bf16[4,384,128]{2,1,0:T(8,128)(2,1)S(1)} %collective-permute-done.7.rest_0_.rest_1_.rest_5_), channel_id=1, source_target_pairs={{0,6},{1,3},{2,0},{3,5},{4,2},{5,7},{6,4},{7,1},{8,14},{9,11},{10,... | collective-permute-start | bytes 1179656 | tf_op jit(solution)/shard_map/ppermute | solution.py:267
  62.4 10.8 %collective-permute-start.11 = (bf16[4,384,128]{2,1,0:T(8,128)(2,1)S(1)}, bf16[4,384,128]{2,1,0:T(8,128)(2,1)S(1)}, u32[]{:S(2)}, u32[]{:S(2)}) collective-permute-start(bf16[4,384,128]{2,1,0:T(8,128)(2,1)S(1)} %shard_map.65), channel_id=1, source_target_pairs={{0,2},{1,7},{2,4},{3,1},{4,6},{5,3},{6,0},{7,5},{8,10},{9,15},{10,... | collective-permute-start | bytes 1179656 | tf_op jit(solution)/shard_map/ppermute | solution.py:267
  62.5 10.7 %collective-permute-start.9 = (bf16[4,384,128]{2,1,0:T(8,128)(2,1)S(1)}, bf16[4,384,128]{2,1,0:T(8,128)(2,1)S(1)}, u32[]{:S(2)}, u32[]{:S(2)}) collective-permute-start(bf16[4,384,128]{2,1,0:T(8,128)(2,1)S(1)} %shard_map.65), channel_id=1, source_target_pairs={{0,6},{1,3},{2,0},{3,5},{4,2},{5,7},{6,4},{7,1},{8,14},{9,11},{10,... | collective-permute-start | bytes 1179656 | tf_op jit(solution)/shard_map/ppermute | solution.py:267
  70.3 16.1 %collective-permute-start.20 = (bf16[4,768,128]{2,1,0:T(8,128)(2,1)S(1)}, bf16[4,768,128]{2,1,0:T(8,128)(2,1)S(1)}, u32[]{:S(2)}, u32[]{:S(2)}) collective-permute-start(bf16[4,768,128]{2,1,0:T(8,128)(2,1)S(1)} %shard_map.70), channel_id=1, source_target_pairs={{0,24},{1,9},{2,26},{3,11},{4,28},{5,13},{6,30},{7,15},{8,0},{9,17... | collective-permute-start | bytes 2359304 | tf_op jit(solution)/shard_map/ppermute | solution.py:271
  74.9 17.3 %collective-permute-start.25 = (bf16[4,768,128]{2,1,0:T(8,128)(2,1)S(1)}, bf16[4,768,128]{2,1,0:T(8,128)(2,1)S(1)}, u32[]{:S(2)}, u32[]{:S(2)}) collective-permute-start(bf16[4,768,128]{2,1,0:T(8,128)(2,1)S(1)} %shard_map.74), channel_id=1, source_target_pairs={{0,24},{1,9},{2,26},{3,11},{4,28},{5,13},{6,30},{7,15},{8,0},{9,17... | collective-permute-start | bytes 2359304 | tf_op jit(solution)/shard_map/ppermute | solution.py:271
  78.6 7.8 %collective-permute-start.10 = (bf16[4,384,128]{2,1,0:T(8,128)(2,1)S(1)}, bf16[4,384,128]{2,1,0:T(8,128)(2,1)S(1)}, u32[]{:S(2)}, u32[]{:S(2)}) collective-permute-start(bf16[4,384,128]{2,1,0:T(8,128)(2,1)S(1)} %collective-permute-done.9.rest_1_.rest_5_), channel_id=1, source_target_pairs={{0,6},{1,3},{2,0},{3,5},{4,2},{5,7},{6,4},{7,1},{8,14},{9,11},{10,... | collective-permute-start | bytes 1179656 | tf_op jit(solution)/shard_map/ppermute | solution.py:267
  99.4 12.8 %collective-permute-start.27 = (bf16[1664,128]{1,0:T(8,128)(2,1)S(1)}, bf16[1664,128]{1,0:T(8,128)(2,1)S(1)}, u32[]{:S(2)}, u32[]{:S(2)}) collective-permute-start(bf16[1664,128]{1,0:T(8,128)(2,1)S(1)} %get-tuple-element.36), channel_id=1, source_target_pairs={{0,4},{1,5},{2,6},{3,7},{4,0},{5,1},{6,2},{7,3},{8,12},{9,13},{10,... | collective-permute-start | bytes 1277960 | tf_op jit(solution)/shard_map/ppermute | solution.py:263
  103.0 9.3 %collective-permute-start.26 = (bf16[896,128]{1,0:T(8,128)(2,1)S(1)}, bf16[896,128]{1,0:T(8,128)(2,1)S(1)}, u32[]{:S(2)}, u32[]{:S(2)}) collective-permute-start(bf16[896,128]{1,0:T(8,128)(2,1)S(1)} %get-tuple-element.35), channel_id=1, source_target_pairs={{0,2},{1,3},{2,4},{3,5},{4,6},{5,7},{6,0},{7,1},{8,10},{9,11},{10,... | collective-permute-start | bytes 688136 | tf_op jit(solution)/shard_map/ppermute | solution.py:263
  103.0 9.3 %collective-permute-start.28 = (bf16[896,128]{1,0:T(8,128)(2,1)S(1)}, bf16[896,128]{1,0:T(8,128)(2,1)S(1)}, u32[]{:S(2)}, u32[]{:S(2)}) collective-permute-start(bf16[896,128]{1,0:T(8,128)(2,1)S(1)} %get-tuple-element.37), channel_id=1, source_target_pairs={{0,6},{1,7},{2,0},{3,1},{4,2},{5,3},{6,4},{7,5},{8,14},{9,15},{10,... | collective-permute-start | bytes 688136 | tf_op jit(solution)/shard_map/ppermute | solution.py:263
  (10 other events, 80.3 us)
